TPU v7x, 256 devices: a whole 4x4x8 slice. The times are simulated.
256 devices in a mesh: freq: 16 (over x, y_hi, core), src: 16 (over y_lo, z).
Axes of the slice: x: 4, y: 4 (y_hi: 2, y_lo: 2; y = y_hi * 2 + y_lo), z: 8, core: 2. Of those that a mesh axis runs over, the one named last changes fastest.
Arguments:
- spectra: bfloat16 [192, 2, 256, 8192], P('freq', None, None, 'src'), may hold values from -6 to 6
- primaries: bfloat16 [192, 2, 8192, 256], P('freq', None, 'src'), may hold values from -0.0625 to 0.0625
- wavelet_ratio: float32 [2, 192], P(None, 'freq'), may hold values from -4 to 4
- window_lengths: int32 [16], replicated, may hold values from 1 to 32, 384 in all
- event_mask: int32 [512], P('freq'), may hold values 0 or 1
- pairing: int32 [16], replicated, may hold values from 0 to 15, each once
- old_traces: bfloat16 [512, 256, 256], P('freq', 'src'), may hold values from -6 to 6
- data_traces: bfloat16 [512, 256, 256], P('freq', 'src'), may hold values from -6 to 6
Outputs:
- new_traces: bfloat16 [512, 256, 256], P('freq', 'src')
Inputs may be any that keep to these rules, and one draw needn't show every extreme that they name: `window_lengths`: each window holds 1 to 32 samples, the windows together hold 384, and one holds exactly 32. `pairing`: a permutation of the 16 blocks.
All inputs are finite; a program needn't handle non-finite values. No bound on the sum of `event_mask` on one device may be relied on, other than what follows from the above.
Results may differ from a plain program's by a relative error of at most 0.001.
Values sent between devices are 32-bit elements; how exact they have to be, the bound alone decides.
No kernel may reach another device: no remote copies, remote signals or barrier semaphores. Data moves between devices by JAX's collectives and lax.ppermute only.
A program may use at most 192 MiB of HBM per device.

v0:
```python
import math

import jax
import jax.numpy as jnp
from jax import lax
from jax.sharding import PartitionSpec as P

F = 192
NT = 384


shrink_level = 0.25
step_weight = 0.5


def time_basis(slots, freqs, window_lengths, capacity):
    starts = jnp.cumsum(window_lengths) - window_lengths
    window = slots // capacity
    offset = slots % capacity
    select = window[:, None] == jnp.arange(window_lengths.shape[0], dtype=jnp.int32)[None, :]
    begin = jnp.sum(jnp.where(select, starts[None, :], 0), axis=1)
    length = jnp.sum(jnp.where(select, window_lengths[None, :], 0), axis=1)
    inside = offset < length
    phase = (begin + offset)[:, None] * freqs[None, :] % NT
    angle = phase.astype(jnp.float32) * (2.0 * math.pi / NT)
    scale = jnp.where(inside, 1.0 / math.sqrt(F), 0.0).astype(jnp.float32)[:, None]
    basis = jnp.stack([jnp.cos(angle) * scale, -jnp.sin(angle) * scale], axis=2)
    return (basis, inside)


def complex_product(first, second, form):
    product = jnp.einsum(form, first, second, preferred_element_type=jnp.float32)
    real_part = product[:, :, 0, 0] - product[:, :, 1, 1]
    imag_part = product[:, :, 0, 1] + product[:, :, 1, 0]
    return jnp.stack([real_part, imag_part], axis=2)


def on_device(
    spectra, primaries, wavelet_ratio, window_lengths, event_mask, pairing, old_traces, data_traces
):
    src_count = lax.axis_size("src")
    freq_count = lax.axis_size("freq")
    freq_dev = spectra.shape[0]
    width = spectra.shape[2]
    block_rows = width // src_count
    capacity = old_traces.shape[0]
    inverse = (
        jnp.zeros((src_count,), jnp.int32).at[pairing].set(jnp.arange(src_count, dtype=jnp.int32))
    )
    direct = complex_product(spectra, primaries, "faik,fbkj->ifabj")
    summed = lax.psum_scatter(direct, "src", scatter_dimension=0, tiled=True)
    blocks = summed.reshape(block_rows, freq_dev, 2, src_count, block_rows)
    outgoing = (
        jnp.take(blocks, pairing, axis=3)
        .transpose(4, 1, 2, 3, 0)
        .reshape(block_rows, freq_dev, 2, width)
    )
    incoming = lax.all_to_all(outgoing, "src", split_axis=3, concat_axis=3, tiled=True)
    placed = jnp.take(
        incoming.reshape(block_rows, freq_dev, 2, src_count, block_rows), inverse, axis=3
    )
    symmetric = 0.5 * (summed + placed.reshape(block_rows, freq_dev, 2, width))
    ratio_real = wavelet_ratio[0][None, :, None]
    ratio_imag = wavelet_ratio[1][None, :, None]
    sym_real = symmetric[:, :, 0]
    sym_imag = symmetric[:, :, 1]
    weighted = jnp.stack(
        [
            ratio_real * sym_real - ratio_imag * sym_imag,
            ratio_real * sym_imag + ratio_imag * sym_real,
        ],
        axis=2,
    )
    spread = lax.all_to_all(weighted, "freq", split_axis=3, concat_axis=1, tiled=True)
    all_slots = jnp.arange(capacity * freq_count, dtype=jnp.int32)
    basis, inside = time_basis(
        all_slots, jnp.arange(freq_dev * freq_count, dtype=jnp.int32), window_lengths, capacity
    )
    local_traces = jnp.einsum("tfc,bfcw->tbw", basis, spread, precision=lax.Precision.HIGHEST)
    traces = lax.all_to_all(local_traces, "freq", split_axis=0, concat_axis=2, tiled=True)
    own_slots = lax.axis_index("freq") * capacity + jnp.arange(capacity, dtype=jnp.int32)
    window = own_slots // capacity
    offset = own_slots % capacity
    select = window[:, None] == jnp.arange(window_lengths.shape[0], dtype=jnp.int32)[None, :]
    length = jnp.sum(jnp.where(select, window_lengths[None, :], 0), axis=1)
    inside_own = offset < length
    older = old_traces.astype(jnp.float32)
    events = event_mask.astype(jnp.float32)[:, None, None]
    moved = older + step_weight * events * (data_traces.astype(jnp.float32) - older - traces)
    shrunk = jnp.sign(moved) * jnp.maximum(jnp.abs(moved) - shrink_level, 0.0)
    return jnp.where(inside_own[:, None, None], shrunk, 0.0).astype(jnp.bfloat16)


def solution(mesh):
    in_specs = (
        P("freq", None, None, "src"),
        P("freq", None, "src", None),
        P(None, "freq"),
        P(),
        P("freq"),
        P(),
        P("freq", "src", None),
        P("freq", "src", None),
    )
    out_specs = P("freq", "src", None)
    return jax.shard_map(
        on_device, mesh=mesh, in_specs=in_specs, out_specs=out_specs, check_vma=False
    )
```

profile of v0, /device:TPU:1, one launch (start us, length us, event | category | flops | bytes accessed | tf_op | source)
XLA Modules:
  0.0 343.8 jit_solution(338487404730285272)
XLA Ops:
  6.5 0.0 all-reduce.3.cloned.1.call-start
  6.5 12.8 %fusion.3 = f32[256,12,2,2,256]{0,4,2,3,1:T(8,128)} fusion(bf16[12,2,256,512]{3,2,1,0:T(8,128)(2,1)} %param.10, bf16[12,2,512,256]{3,2,1,0:T(8,128)(2,1)} %param.11), kind=kOutput, calls=%fused_computation.7 | convolution fusion | flops 3221225472 | bytes 25165824 | tf_op jit(solution)/shard_map/faik,fbkj->ifabj/dot_general | solution.py:32
  19.3 3.3 fusion.10
  22.6 3.3 fusion.8
  26.0 3.3 pad_maximum_fusion
  29.3 10.4 %copy.120 = f32[256,12,2,256]{3,2,1,0:T(2,128)} copy(f32[256,12,2,256]{0,3,1,2:T(8,128)} %pad_maximum_fusion) | data formatting | bytes 12582912 | tf_op jit(solution)/shard_map/stack | solution.py:35
  39.7 0.0 all-reduce.3.cloned.1.call-update
  39.7 0.6 copy-done.6
  40.4 0.1 copy.116
  40.5 0.1 reduce
  40.6 0.0 copy-done.12
  40.6 0.6 dynamic-slice
  41.9 0.0 copy-done.10
  41.9 0.8 scatter_custom_fusion
  42.7 0.0 copy-start.13
  42.7 0.1 select_reduce_fusion.1
  42.8 0.5 compare_select_fusion
  43.3 163.4 %all-reduce.3.cloned.1.call-done = f32[256,12,2,256]{3,2,1,0:T(2,128)} async-done(((f32[256,12,2,256]{3,2,1,0:T(2,128)}), f32[256,12,2,256]{3,2,1,0:T(2,128)}) %all-reduce.3.cloned.1.call-update) | async-done | bytes 6291472
  206.8 0.0 copy-done.13
  206.8 1.1 constant_dynamic-slice_fusion
  207.9 1.1 reshape.329
  209.0 3.8 %copy.122 = f32[16,12,2,16,16]{4,0,3,2,1:T(8,128)} copy(f32[16,12,2,16,16]{4,3,2,1,0:T(8,128)S(1)} %reshape.329) | data formatting | bytes 786432 | tf_op jit(solution)/shard_map/reshape | solution.py:52
  212.9 2.7 gather_fusion
  215.5 0.5 select_bitcast_fusion.1
  216.0 1.7 copy.141
  217.7 0.0 copy-start.8
  217.7 4.9 %reshape.334 = f32[16,1,6144]{2,1,0:T(1,128)} reshape(f32[256,12,2,16]{3,2,1,0:T(2,128)S(1)} %bitcast.73) | data formatting | bytes 786432
  222.6 5.4 %all-to-all-start = ((f32[16,1,6144]{2,1,0:T(1,128)}), f32[16,1,6144]{2,1,0:T(1,128)S(1)}, u32[]{:S(2)}, u32[]{:S(2)}) async-start(f32[16,1,6144]{2,1,0:T(1,128)} %reshape.334), calls=%async_computation | async-start | bytes 786432 | tf_op jit(solution)/shard_map/all_to_all | solution.py:58
  228.0 0.7 pad_clamp_fusion
  228.6 1.2 compare_and_fusion
  229.9 0.5 slice_bitcast_fusion.3
  230.4 6.7 %all-to-all-done = f32[16,1,6144]{2,1,0:T(1,128)S(1)} async-done(((f32[16,1,6144]{2,1,0:T(1,128)}), f32[16,1,6144]{2,1,0:T(1,128)S(1)}, u32[]{:S(2)}, u32[]{:S(2)}) %all-to-all-start) | async-done | bytes 393248 | tf_op jit(solution)/shard_map/all_to_all | solution.py:58
  237.1 0.5 broadcast.376
  237.6 2.4 reduce.1
  240.0 5.3 %reshape.335 = f32[256,12,2,16]{3,2,1,0:T(2,128)S(1)} reshape(f32[16,6144]{1,0:T(8,128)} %reduce.1) | data formatting | bytes 786432
  245.2 3.6 %copy.126 = f32[16,12,2,16,16]{4,0,3,2,1:T(8,128)} copy(f32[16,12,2,16,16]{0,2,1,4,3:T(2,128)S(1)} %bitcast.74) | data formatting | bytes 786432 | tf_op jit(solution)/shard_map/reshape | solution.py:60
  248.9 2.7 gather_fusion.1
  251.6 0.4 select_bitcast_fusion
  252.0 2.2 copy.127
  254.2 0.0 copy-start.4
  254.2 0.0 copy-start.5
  254.2 2.1 reshape.293
  256.3 1.1 fusion.17
  257.5 0.1 multiply_subtract_fusion
  257.6 2.4 copy.129
  260.0 4.9 %reshape.336 = f32[16,1,6144]{2,1,0:T(1,128)} reshape(f32[256,12,2,16]{3,2,1,0:T(2,128)S(1)} %bitcast.75) | data formatting | bytes 786432
  264.9 11.1 %all-to-all-start.1 = ((f32[16,1,6144]{2,1,0:T(1,128)}), f32[16,1,6144]{2,1,0:T(1,128)S(1)}, u32[]{:S(2)}, u32[]{:S(2)}) async-start(f32[16,1,6144]{2,1,0:T(1,128)} %reshape.336), calls=%async_computation.1 | async-start | bytes 786432 | tf_op jit(solution)/shard_map/all_to_all | solution.py:74
  276.1 2.6 cosine_multiply_fusion
  278.6 7.5 %all-to-all-done.1 = f32[16,1,6144]{2,1,0:T(1,128)S(1)} async-done(((f32[16,1,6144]{2,1,0:T(1,128)}), f32[16,1,6144]{2,1,0:T(1,128)S(1)}, u32[]{:S(2)}, u32[]{:S(2)}) %all-to-all-start.1) | async-done | bytes 393248 | tf_op jit(solution)/shard_map/all_to_all | solution.py:74
  286.1 1.6 reduce.2
  287.7 4.2 %reshape.337 = f32[256,12,2,16]{3,2,1,0:T(2,128)S(1)} reshape(f32[16,6144]{1,0:T(8,128)S(1)} %reduce.2) | data formatting | bytes 786432
  291.9 7.0 %copy.130 = f32[16,12,2,16,16]{1,3,4,2,0:T(8,128)} copy(f32[16,12,2,16,16]{0,2,1,4,3:T(2,128)S(1)} %bitcast.72) | data formatting | bytes 786432 | tf_op jit(solution)/shard_map/all_to_all | solution.py:74
  298.9 3.7 %all_to_all.33 = f32[16,192,2,16]{1,3,2,0:T(8,128)S(1)} reshape(f32[16,16,12,2,16]{2,1,4,3,0:T(8,128)} %bitcast.70) | data formatting | bytes 786432 | tf_op jit(solution)/shard_map/all_to_all | solution.py:74
  302.6 1.1 convolution_bitcast_fusion
  303.7 3.6 %copy.131 = f32[512,16,16]{2,1,0:T(8,128)} copy(f32[512,16,16]{0,2,1:T(8,128)S(1)} %convolution_bitcast_fusion) | data formatting | bytes 1048576 | tf_op jit(solution)/shard_map/tfc,bfcw->tbw/dot_general | solution.py:79
  307.3 4.2 %reshape.338 = f32[16,1,8192]{2,1,0:T(1,128)} reshape(f32[512,16,16]{2,1,0:T(8,128)} %copy.131) | data formatting | bytes 1048576
  311.6 4.5 %all-to-all-start.2 = ((f32[16,1,8192]{2,1,0:T(1,128)}), f32[16,1,8192]{2,1,0:T(1,128)S(1)}, u32[]{:S(2)}, u32[]{:S(2)}) async-start(f32[16,1,8192]{2,1,0:T(1,128)} %reshape.338), calls=%async_computation.2 | async-start | bytes 1048576 | tf_op jit(solution)/shard_map/all_to_all | solution.py:80
  316.0 0.1 select_reduce_fusion.2
  316.2 10.9 %all-to-all-done.2 = f32[16,1,8192]{2,1,0:T(1,128)S(1)} async-done(((f32[16,1,8192]{2,1,0:T(1,128)}), f32[16,1,8192]{2,1,0:T(1,128)S(1)}, u32[]{:S(2)}, u32[]{:S(2)}) %all-to-all-start.2) | async-done | bytes 524320 | tf_op jit(solution)/shard_map/all_to_all | solution.py:80
  327.1 1.9 reduce.3
  329.0 2.8 reshape.339
  331.8 2.9 copy.132
  334.7 0.7 copy.133
  335.4 1.1 select_convert_fusion
  (33 shorter events, 0.2 us)
Async XLA Ops:
  6.5 200.3 %all-reduce.3.cloned.1.call-start = ((), (), s32[]{:S(2)}) async-start(), calls=%async_computation.3 | async-start | bytes 12582912
  39.7 0.7 copy-start.6
  39.7 0.9 copy-start.12
  39.7 2.2 copy-start.10
  42.7 164.1 %copy-start.13 = (s32[16]{0:T(128)}, s32[16]{0:T(128)S(1)}, u32[]{:S(2)}) copy-start(s32[16]{0:T(128)S(1)} %scatter_custom_fusion) | copy-start | bytes 196
  217.7 12.2 %copy-start.8 = (f32[2,12]{1,0:T(2,128)S(1)}, f32[2,12]{1,0:T(2,128)}, u32[]{:S(2)}) copy-start(f32[2,12]{1,0:T(2,128)} %param.12) | copy-start | bytes 292
  222.6 14.5 %all-to-all-start = ((f32[16,1,6144]{2,1,0:T(1,128)}), f32[16,1,6144]{2,1,0:T(1,128)S(1)}, u32[]{:S(2)}, u32[]{:S(2)}) async-start(f32[16,1,6144]{2,1,0:T(1,128)} %reshape.334), calls=%async_computation | async-start | bytes 786432 | tf_op jit(solution)/shard_map/all_to_all | solution.py:58
  248.9 2.7 copy-start.9
  254.2 3.2 copy-start.4
  254.2 3.2 copy-start.5
  264.9 21.2 %all-to-all-start.1 = ((f32[16,1,6144]{2,1,0:T(1,128)}), f32[16,1,6144]{2,1,0:T(1,128)S(1)}, u32[]{:S(2)}, u32[]{:S(2)}) async-start(f32[16,1,6144]{2,1,0:T(1,128)} %reshape.336), calls=%async_computation.1 | async-start | bytes 786432 | tf_op jit(solution)/shard_map/all_to_all | solution.py:74
  298.9 3.7 %copy-start = (f32[512,192,1]{0,1,2:T(8,128)S(1)}, f32[512,192,1]{0,1,2:T(8,128)}, u32[]{:S(2)}) copy-start(f32[512,192,1]{0,1,2:T(8,128)} %get-tuple-element.10) | copy-start | bytes 1179652
  298.9 3.7 %copy-start.1 = (f32[512,192,1]{0,1,2:T(8,128)S(1)}, f32[512,192,1]{0,1,2:T(8,128)}, u32[]{:S(2)}) copy-start(f32[512,192,1]{0,1,2:T(8,128)} %get-tuple-element.11) | copy-start | bytes 1179652
  307.3 8.7 %copy-start.7 = (s32[16]{0:T(128)S(1)}, s32[16]{0:T(128)}, u32[]{:S(2)}) copy-start(s32[16]{0:T(128)} %param.13) | copy-start | bytes 196
  307.3 8.8 %copy-start.11 = (s32[32]{0:T(128)S(1)}, s32[32]{0:T(128)}, u32[]{:S(2)}) copy-start(s32[32]{0:T(128)} %param.14) | copy-start | bytes 388
  311.6 15.6 %all-to-all-start.2 = ((f32[16,1,8192]{2,1,0:T(1,128)}), f32[16,1,8192]{2,1,0:T(1,128)S(1)}, u32[]{:S(2)}, u32[]{:S(2)}) async-start(f32[16,1,8192]{2,1,0:T(1,128)} %reshape.338), calls=%async_computation.2 | async-start | bytes 1048576 | tf_op jit(solution)/shard_map/all_to_all | solution.py:80
  331.8 3.6 %copy-start.2 = (bf16[32,16,256]{2,1,0:T(8,128)(2,1)S(1)}, bf16[32,16,256]{2,1,0:T(8,128)(2,1)}, u32[]{:S(2)}) copy-start(bf16[32,16,256]{2,1,0:T(8,128)(2,1)} %param.16) | copy-start | bytes 786436
  331.8 3.6 %copy-start.3 = (bf16[32,16,256]{2,1,0:T(8,128)(2,1)S(1)}, bf16[32,16,256]{2,1,0:T(8,128)(2,1)}, u32[]{:S(2)}) copy-start(bf16[32,16,256]{2,1,0:T(8,128)(2,1)} %param.17) | copy-start | bytes 786436
Sparse Core Ops, SparseCore 0:
  39.9 166.8 all-reduce.2
where the time goes:
time: 349 us; the launch traced here: 344 us
  waiting for transfers between devices  189 us (54%)
  local copies, waits for them, and re-layouts  81.1 us (23%)
  other arithmetic  24.4 us (7%)
  starting transfers between devices  21 us (6%)
  between operations  14.9 us (4%)
  matrix products  13.8 us (4%)
    unnamed x2, waiting for transfers between devices  163 us
    unnamed x36, local copies, waits for them, and re-layouts  28.6 us
    dot_general x1, matrix products, complex_product(): jnp.einsum(form, first, second, preferred_element_type=jnp.float32)  12.8 us
    all_to_all x1, starting transfers between devices, on_device(): lax.all_to_all(weighted, 'freq', split_axis=3, concat_axis=1, tiled=True)  11.1 us
    all_to_all x1, waiting for transfers between devices, on_device(): lax.all_to_all(local_traces, 'freq', split_axis=0, concat_axis=2, tiled=T...  10.9 us
    all_to_all x2, local copies, waits for them, and re-layouts, on_device(): lax.all_to_all(weighted, 'freq', split_axis=3, concat_axis=1, tiled=True)  10.7 us
    another operation x1, local copies, waits for them, and re-layouts, complex_product(): return jnp.stack([real_part, imag_part], axis=2)  10.4 us
    all_to_all x1, waiting for transfers between devices, on_device(): lax.all_to_all(weighted, 'freq', split_axis=3, concat_axis=1, tiled=True)  7.5 us
  transfers between devices with their start and end apart: 4, of which 4 were waited for; matrix products, arithmetic and copies ran while one was open for 2% of the time, Pallas kernels for 0%

commit v1 on v0

v1 whole, which is shorter than its diff:
```python
import functools
import math

import jax
import jax.numpy as jnp
from jax import lax
from jax.experimental import pallas as pl
from jax.experimental.pallas import tpu as pltpu
from jax.sharding import Mesh, PartitionSpec as P

F = 192
NT = 384
LANES = 128
BLOCK = 16
CHUNKS = (12,)

shrink_level = 0.25
step_weight = 0.5


def product_kernel(first, zi, ratio, spectra, primaries, relabel, out):
    step = pl.program_id(0)
    width = spectra.shape[2]
    depth = spectra.shape[3]
    rings = out.shape[0]
    half = width // 2
    parts = out.shape[1]
    groups = parts // 17
    rows = 8 * groups
    left = spectra[0].reshape(2 * width, depth)
    right = [
        jnp.dot(primaries[0, b], relabel[...], preferred_element_type=jnp.float32).astype(
            jnp.bfloat16
        )
        for b in range(2)
    ]
    by_real = jnp.dot(left, right[0], preferred_element_type=jnp.float32)
    by_imag = jnp.dot(left, right[1], preferred_element_type=jnp.float32)
    real = by_real[:width] - by_imag[width:]
    imag = by_imag[:width] + by_real[width:]
    real = 0.5 * (real + real.T)
    imag = 0.5 * (imag + imag.T)
    wr = ratio[0, first + step]
    wi = ratio[1, first + step]
    lane = lax.broadcasted_iota(jnp.int32, (BLOCK, LANES), 1)
    for c, z in enumerate((wr * real - wi * imag, wr * imag + wi * real)):
        row = 2 * step + c
        slot = row % 8
        for t in range(rings):
            k = lax.rem(t - zi[0] + rings, rings)
            low = z[BLOCK * t : BLOCK * (t + 1)]
            high = z[half + BLOCK * t : half + BLOCK * (t + 1)]
            if t:
                high = jnp.concatenate(
                    [high[:, half + BLOCK * t :], high[:, : BLOCK * t]], axis=1
                )
            else:
                high = high[:, half:]
            out[k, row] = low[:, BLOCK * t : BLOCK * t + LANES]
            out[k, rows + row] = high
            opposite = pltpu.roll(low[:, half:], lax.rem(BLOCK * (slot - t) + LANES, LANES), 1)
            place = 2 * rows + row // 8
            mine = (lane >= BLOCK * slot) & (lane < BLOCK * slot + BLOCK)
            out[k, place] = jnp.where(mine, opposite, out[k, place])


def product(spectra, primaries, ratio, relabel, zi, first, count):
    width, depth = spectra.shape[2:]
    parts = 17 * (2 * count // 8)
    return pl.pallas_call(
        functools.partial(product_kernel, first),
        grid=(count,),
        in_specs=[
            pl.BlockSpec(memory_space=pltpu.SMEM),
            pl.BlockSpec(memory_space=pltpu.SMEM),
            pl.BlockSpec((1, 2, width, depth), lambda i: (first + i, 0, 0, 0)),
            pl.BlockSpec((1, 2, depth, width), lambda i: (first + i, 0, 0, 0)),
            pl.BlockSpec((width, width), lambda i: (0, 0)),
        ],
        out_specs=pl.BlockSpec((8, parts, BLOCK, LANES), lambda i: (0, 0, 0, 0)),
        out_shape=jax.ShapeDtypeStruct((8, parts, BLOCK, LANES), jnp.float32),
        compiler_params=pltpu.CompilerParams(vmem_limit_bytes=40 * 1024 * 1024),
        cost_estimate=pl.CostEstimate(
            flops=count * 2 * 2 * width * 2 * width * depth,
            bytes_accessed=count * 8 * width * depth + 8 * parts * BLOCK * LANES * 4,
            transcendentals=0,
        ),
        name="product",
    )(zi, ratio, spectra, primaries, relabel)


def exchange_lanes(tiles):
    lane = lax.broadcasted_iota(jnp.int32, tiles[0].shape, 1) // BLOCK
    for bit in (1, 2, 4):
        upper = (lane // bit) % 2 == 1
        out = list(tiles)
        for a in range(8):
            if a & bit:
                continue
            x, y = tiles[a], tiles[a | bit]
            out[a] = jnp.where(upper, pltpu.roll(y, BLOCK * bit, 1), x)
            out[a | bit] = jnp.where(upper, y, pltpu.roll(x, LANES - BLOCK * bit, 1))
        tiles = out
    return tiles


def pack_kernel(place, own, up, down, keep, give, mail):
    yl, zi = place[0], place[1]
    groups = own.shape[0] // 17
    rows = 8 * groups
    lane = lax.broadcasted_iota(jnp.int32, (BLOCK, LANES), 1)

    def total(i):
        return own[i] + up[i] + down[i]

    for g in range(groups):
        for h in range(2):
            tiles = [total(rows * h + 8 * g + a) for a in range(8)]
            for a in range(8):

                @pl.when(yl == h)
                def _():
                    keep[8 * g + a] = tiles[a]

                @pl.when(yl != h)
                def _():
                    give[8 * g + a] = tiles[a]

            swapped = exchange_lanes(tiles)
            for m in range(1, 8):
                mail[lax.rem(zi + 8 * h + m, 16), g] = swapped[m]
        opposite = total(2 * rows + g)
        mail[zi + 8, g] = opposite
        flipped = jnp.zeros((BLOCK, LANES), jnp.float32)
        turned = opposite.T
        for a in range(8):
            block = jnp.concatenate(
                [turned[BLOCK * a : BLOCK * (a + 1)], jnp.zeros((BLOCK, LANES - BLOCK), jnp.float32)],
                axis=1,
            )
            flipped = flipped + (pltpu.roll(block, BLOCK * a, 1) if a else block)
        mail[zi, g] = flipped


def pack(place, own, up, down):
    groups = own.shape[0] // 17
    whole = pl.BlockSpec(memory_space=pltpu.VMEM)
    return pl.pallas_call(
        pack_kernel,
        in_specs=[pl.BlockSpec(memory_space=pltpu.SMEM), whole, whole, whole],
        out_specs=[whole, whole, whole],
        out_shape=[
            jax.ShapeDtypeStruct((8 * groups, BLOCK, LANES), jnp.float32),
            jax.ShapeDtypeStruct((8 * groups, BLOCK, LANES), jnp.float32),
            jax.ShapeDtypeStruct((16, groups, BLOCK, LANES), jnp.float32),
        ],
        name="pack",
    )(place, own, up, down)


def join_kernel(place, keep, got, mail, out):
    zi = place[1]
    groups = mail.shape[1]
    for g in range(groups):
        stack = []
        for k in range(8):
            z = lax.rem(zi + k, 8)
            stack.append(mail[z, g] + mail[z + 8, g])
        turned = jnp.concatenate(stack, axis=0).T.reshape(8, BLOCK, LANES)
        direct = keep[8 * g : 8 * g + 8] + got[8 * g : 8 * g + 8]
        out[:, 8 * g : 8 * g + 8, :LANES] = jnp.swapaxes(direct, 0, 1)
        out[:, 8 * g : 8 * g + 8, LANES:] = jnp.swapaxes(turned, 0, 1)


def join(place, keep, got, mail):
    groups = mail.shape[1]
    whole = pl.BlockSpec(memory_space=pltpu.VMEM)
    return pl.pallas_call(
        join_kernel,
        in_specs=[pl.BlockSpec(memory_space=pltpu.SMEM), whole, whole, whole],
        out_specs=whole,
        out_shape=jax.ShapeDtypeStruct((BLOCK, 8 * groups, 2 * LANES), jnp.float32),
        name="join",
    )(place, keep, got, mail)


def transform_kernel(basis, data, relabel, out):
    placed = jnp.dot(
        data[...],
        relabel[...],
        precision=lax.Precision.HIGHEST,
        preferred_element_type=jnp.float32,
    )
    out[...] = jnp.dot(
        basis[...], placed, precision=lax.Precision.HIGHEST, preferred_element_type=jnp.float32
    )


def transform(basis, data, relabel):
    whole = pl.BlockSpec(memory_space=pltpu.VMEM)
    return pl.pallas_call(
        transform_kernel,
        in_specs=[whole] * 3,
        out_specs=whole,
        out_shape=jax.ShapeDtypeStruct((basis.shape[0], data.shape[1]), jnp.float32),
        compiler_params=pltpu.CompilerParams(vmem_limit_bytes=40 * 1024 * 1024),
        name="transform",
    )(basis, data, relabel)


def update_kernel(events, inside, traces, older, data, out):
    count = older.shape[0]
    for t in range(count):
        old = older[t].astype(jnp.float32)
        moved = old + step_weight * events[t] * (
            data[t].astype(jnp.float32) - old - traces[:, t, :]
        )
        size = jnp.maximum(jnp.abs(moved) - shrink_level, 0.0)
        shrunk = jnp.where(moved < 0.0, -size, size)
        out[t] = jnp.where(inside[t] > 0, shrunk, 0.0).astype(jnp.bfloat16)


def update(events, inside, traces, older, data):
    whole = pl.BlockSpec(memory_space=pltpu.VMEM)
    scalars = pl.BlockSpec(memory_space=pltpu.SMEM)
    return pl.pallas_call(
        update_kernel,
        in_specs=[scalars, scalars, whole, whole, whole],
        out_specs=whole,
        out_shape=jax.ShapeDtypeStruct(older.shape, jnp.bfloat16),
        name="update",
    )(events, inside, traces, older, data)


def slot_windows(slots, window_lengths, capacity):
    starts = jnp.cumsum(window_lengths) - window_lengths
    window = slots // capacity
    offset = slots % capacity
    select = window[:, None] == jnp.arange(window_lengths.shape[0], dtype=jnp.int32)[None, :]
    begin = jnp.sum(jnp.where(select, starts[None, :], 0), axis=1)
    length = jnp.sum(jnp.where(select, window_lengths[None, :], 0), axis=1)
    return begin + offset, offset < length


def time_basis(times, inside, freqs):
    phase = times[:, None] * freqs[None, :] % NT
    angle = phase.astype(jnp.float32) * (2.0 * math.pi / NT)
    scale = jnp.where(inside, 1.0 / math.sqrt(F), 0.0).astype(jnp.float32)[:, None]
    odd = (jnp.arange(freqs.shape[0]) % 2 == 1)[None, :]
    return jnp.where(odd, -jnp.sin(angle), jnp.cos(angle)) * scale


def ring(n, d):
    return [(i, (i + d) % n) for i in range(n)]


def add_head(base, head):
    n = head.shape[0]
    return jnp.concatenate([base[:n] + head, base[n:]])


def add_tail(base, tail):
    n = base.shape[0] - tail.shape[0]
    return jnp.concatenate([base[:n], base[n:] + tail])


def ring_sum(parts):
    up = functools.partial(lax.ppermute, axis_name="z", perm=ring(8, 1))
    down = functools.partial(lax.ppermute, axis_name="z", perm=ring(8, -1))
    cut = parts.shape[1] // 2
    a, b = up(parts[4, :cut]), down(parts[4, cut:])
    a, b = up(add_head(parts[3], a)), down(add_tail(parts[5], b))
    a, b = up(parts[2] + a), down(parts[6] + b)
    return parts[0], up(parts[1] + a), down(parts[7] + b)


def on_device(
    spectra, primaries, wavelet_ratio, window_lengths, event_mask, pairing, old_traces, data_traces
):
    src = ("yl", "z")
    freq = ("x", "yh", "core")
    freq_count = lax.axis_size(freq)
    freq_dev = spectra.shape[0]
    width = spectra.shape[2]
    capacity = old_traces.shape[0]
    yl, zi = lax.axis_index("yl"), lax.axis_index("z")
    own = yl * 8 + zi
    place = jnp.stack([yl, zi])
    lanes = jnp.arange(width, dtype=jnp.int32)
    blocks = lanes // BLOCK
    ids = jnp.arange(pairing.shape[0], dtype=jnp.int32)

    def paired(block):
        return jnp.sum(jnp.where(block[:, None] == ids[None, :], pairing[None, :], 0), axis=1)

    source = paired(blocks) * BLOCK + lanes % BLOCK
    relabel = (lanes[:, None] == source[None, :]).astype(jnp.bfloat16)
    target = paired((blocks + own) % pairing.shape[0]) * BLOCK + lanes % BLOCK
    restore = (target[:, None] == lanes[None, :]).astype(jnp.float32)
    slots = jnp.arange(capacity * freq_count, dtype=jnp.int32)
    times, inside = slot_windows(slots, window_lengths, capacity)
    basis = time_basis(
        times, inside, jnp.arange(2 * freq_dev * freq_count, dtype=jnp.int32) // 2
    )
    own_slots = lax.axis_index(freq) * capacity + jnp.arange(capacity, dtype=jnp.int32)
    _, inside_own = slot_windows(own_slots, window_lengths, capacity)

    first = 0
    joined = []
    for count in CHUNKS:
        parts = product(
            spectra, primaries, wavelet_ratio, relabel, zi.reshape(1), first, count
        )
        first += count
        keep, give, mail = pack(place, *ring_sum(parts))
        got = lax.ppermute(give, "yl", ring(2, 1))
        mail = lax.all_to_all(mail, src, split_axis=0, concat_axis=0, tiled=True)
        joined.append(join(place, keep, got, mail))
    whole = joined[0] if len(joined) == 1 else jnp.concatenate(joined, axis=1)
    spread = lax.all_to_all(whole, freq, split_axis=0, concat_axis=0, tiled=True)
    slotted = transform(basis, spread.reshape(-1, width), restore)
    slotted = slotted.reshape(freq_count, capacity, width)
    traces = lax.all_to_all(slotted, freq, split_axis=0, concat_axis=0, tiled=True)
    return update(
        event_mask.astype(jnp.float32),
        inside_own.astype(jnp.int32),
        traces,
        old_traces,
        data_traces,
    )


def solution(mesh):
    shape = tuple(mesh.shape.values())
    cores = 2 if shape[0] % 2 == 0 else 1
    yh = 2 if shape[0] % 4 == 0 else 1
    devices = mesh.devices.reshape(shape[0] // (cores * yh), yh, cores, shape[1] // 8, 8)
    split = Mesh(devices, ("x", "yh", "core", "yl", "z"))
    freq = ("x", "yh", "core")
    src = ("yl", "z")
    in_specs = (
        P(freq, None, None, src),
        P(freq, None, src, None),
        P(None, freq),
        P(),
        P(freq),
        P(),
        P(freq, src, None),
        P(freq, src, None),
    )
    return jax.shard_map(
        on_device, mesh=split, in_specs=in_specs, out_specs=P(freq, src, None), check_vma=False
    )
```

time: 349 us -> 136 us (0.39); the launches traced: 344 us -> 135 us
  waiting for transfers between devices: 189 us -> 55.2 us
  local copies, waits for them, and re-layouts: 81.1 us -> 5.94 us
  Pallas kernels: 0 us -> 25 us
  starting transfers between devices: 21 us -> 40.6 us
  other arithmetic: 24.4 us -> 8.54 us
  between operations: 14.9 us -> 0.16 us
  matrix products: 13.8 us -> 0 us
    unnamed x2 -> x0, waiting for transfers between devices: 163 us -> none
    ppermute x0 -> x9, waiting for transfers between devices: none -> 35.1 us  [the longest x2 12.5 us: ring_sum(): a, b = (up(parts[2] + a), down(parts[6] + b))]
    pallas_call x0 -> x5, Pallas kernels: none -> 25 us  [the longest x1 14 us: product(): pl.pallas_call(functools.partial(product_kernel, first), grid=(count,), i...]
    unnamed x36 -> x14, local copies, waits for them, and re-layouts: 28.6 us -> 5.01 us
    ppermute x0 -> x9, starting transfers between devices: none -> 18.6 us  [the longest x2 6.57 us: ring_sum(): a, b = (up(parts[4, :cut]), down(parts[4, cut:]))]
    all_to_all x5 -> x0, local copies, waits for them, and re-layouts: 14.8 us -> none  [the longest x2 10.7 us: on_device(): lax.all_to_all(weighted, 'freq', split_axis=3, concat_axis=1, tiled=True)]
    dot_general x2 -> x0, matrix products: 13.8 us -> none  [the longest x1 12.8 us: complex_product(): jnp.einsum(form, first, second, preferred_element_type=jnp.float32)]
    another operation x3 -> x1, local copies, waits for them, and re-layouts: 12.9 us -> 0.08 us  [the longest x1 10.4 us: complex_product(): return jnp.stack([real_part, imag_part], axis=2)]
  transfers between devices with their start and end apart: 4 -> 12, of which waited for: 4 -> 9; matrix products, arithmetic and copies ran while one was open for 2% -> 6% of each run, Pallas kernels for 0% -> 0%
where the time goes in v1:
time: 136 us; the launch traced here: 135 us
  waiting for transfers between devices  55.2 us (41%)
  starting transfers between devices  40.6 us (30%)
  Pallas kernels  25 us (18%)
  other arithmetic  8.54 us (6%)
  local copies, waits for them, and re-layouts  5.94 us (4%)
    pallas_call x1, Pallas kernels, product(): pl.pallas_call(functools.partial(product_kernel, first), grid=(count,), i...  14 us
    all_to_all x1, starting transfers between devices, on_device(): lax.all_to_all(whole, freq, split_axis=0, concat_axis=0, tiled=True)  12.9 us
    ppermute x2, waiting for transfers between devices, ring_sum(): a, b = (up(parts[2] + a), down(parts[6] + b))  12.5 us
    all_to_all x1, waiting for transfers between devices, on_device(): lax.all_to_all(slotted, freq, split_axis=0, concat_axis=0, tiled=True)  9.97 us
    ppermute x2, waiting for transfers between devices, ring_sum(): return (parts[0], up(parts[1] + a), down(parts[7] + b))  7.39 us
    ppermute x2, waiting for transfers between devices, ring_sum(): a, b = (up(add_head(parts[3], a)), down(add_tail(parts[5], b)))  7.22 us
    all_to_all x1, waiting for transfers between devices, on_device(): lax.all_to_all(whole, freq, split_axis=0, concat_axis=0, tiled=True)  6.73 us
    ppermute x2, starting transfers between devices, ring_sum(): a, b = (up(parts[4, :cut]), down(parts[4, cut:]))  6.57 us
  transfers between devices with their start and end apart: 12, of which 9 were waited for; matrix products, arithmetic and copies ran while one was open for 6% of the time, Pallas kernels for 0%

profile of v1, /device:TPU:1, one launch (start us, length us, event | category | flops | bytes accessed | tf_op | source)
XLA Modules:
  0.0 135.5 jit_solution(12684221563770114580)
XLA Ops:
  0.0 0.7 select_reduce_fusion.2
  0.8 0.0 copy-start
  0.8 2.8 %copy-done = bf16[12,2,256,512]{3,2,1,0:T(8,128)(2,1)S(1)} copy-done((bf16[12,2,256,512]{3,2,1,0:T(8,128)(2,1)S(1)}, bf16[12,2,256,512]{3,2,1,0:T(8,128)(2,1)}, u32[]{:S(2)}) %copy-start) | copy-done | bytes 6291480
  3.6 0.0 copy-start.1
  3.6 0.7 copy-done.1
  4.3 14.0 %product.1 = f32[8,51,16,128]{3,2,1,0:T(8,128)S(1)} custom-call(s32[1]{0:T(128)} %bitcast.2.zi, f32[2,12]{1,0:T(2,128)S(1)} %copy-done.1, bf16[12,2,256,512]{3,2,1,0:T(8,128)(2,1)S(1)} %copy-done, bf16[12,2,512,256]{3,2,1,0:T(8,128)(2,1)} %primaries.1, bf16[256,256]{1,0:T(8,128)(2,1)S(1)} %fusion.9.relabel), custom_call_target="tpu_custom_call" | custom-call | flops 3221225472 | bytes 15925248 | tf_op jit(solution)/shard_map/product/pallas_call | solution.py:70
  18.3 6.5 %collective-permute-start.4 = (f32[26,16,128]{2,1,0:T(8,128)S(1)}, f32[26,16,128]{2,1,0:T(8,128)S(1)}, u32[]{:S(2)}, u32[]{:S(2)}) collective-permute-start(f32[26,16,128]{2,1,0:T(8,128)S(1)} %get-tuple-element.19), channel_id=1, source_target_pairs={{0,7},{1,0},{2,1},{3,2},{4,3},{5,4},{6,5},{7,6},{8,15},{9,8},{10,9... | collective-permute-start | bytes 638984 | tf_op jit(solution)/shard_map/ppermute | solution.py:271
  24.8 0.0 copy-start.5
  24.8 0.1 collective-permute-start
  24.9 3.8 %collective-permute-done.4 = f32[26,16,128]{2,1,0:T(8,128)S(1)} collective-permute-done((f32[26,16,128]{2,1,0:T(8,128)S(1)}, f32[26,16,128]{2,1,0:T(8,128)S(1)}, u32[]{:S(2)}, u32[]{:S(2)}) %collective-permute-start.4) | collective-permute-done | bytes 213024 | tf_op jit(solution)/shard_map/ppermute | solution.py:271
  28.7 3.5 %collective-permute-start.5 = (f32[51,16,128]{2,1,0:T(8,128)S(1)}, f32[51,16,128]{2,1,0:T(8,128)S(1)}, u32[]{:S(2)}, u32[]{:S(2)}) collective-permute-start(f32[51,16,128]{2,1,0:T(8,128)S(1)} %pad_maximum_fusion.1), channel_id=1, source_target_pairs={{0,7},{1,0},{2,1},{3,2},{4,3},{5,4},{6,5},{7,6},{8,15},{9,8},{10,9... | collective-permute-start | bytes 1253384 | tf_op jit(solution)/shard_map/ppermute | solution.py:272
  32.2 0.0 collective-permute-done
  32.3 0.1 collective-permute-start.1
  32.4 7.2 %collective-permute-done.5 = f32[51,16,128]{2,1,0:T(8,128)S(1)} collective-permute-done((f32[51,16,128]{2,1,0:T(8,128)S(1)}, f32[51,16,128]{2,1,0:T(8,128)S(1)}, u32[]{:S(2)}, u32[]{:S(2)}) %collective-permute-start.5) | collective-permute-done | bytes 417824 | tf_op jit(solution)/shard_map/ppermute | solution.py:272
  39.6 0.1 fusion.5
  39.7 3.5 %collective-permute-start.6 = (f32[51,16,128]{2,1,0:T(8,128)S(1)}, f32[51,16,128]{2,1,0:T(8,128)S(1)}, u32[]{:S(2)}, u32[]{:S(2)}) collective-permute-start(f32[51,16,128]{2,1,0:T(8,128)S(1)} %fusion.5), channel_id=1, source_target_pairs={{0,7},{1,0},{2,1},{3,2},{4,3},{5,4},{6,5},{7,6},{8,15},{9,8},{10,9... | collective-permute-start | bytes 1253384 | tf_op jit(solution)/shard_map/ppermute | solution.py:273
  43.2 0.0 collective-permute-done.1
  43.2 6.5 %collective-permute-done.6 = f32[51,16,128]{2,1,0:T(8,128)S(1)} collective-permute-done((f32[51,16,128]{2,1,0:T(8,128)S(1)}, f32[51,16,128]{2,1,0:T(8,128)S(1)}, u32[]{:S(2)}, u32[]{:S(2)}) %collective-permute-start.6) | collective-permute-done | bytes 417824 | tf_op jit(solution)/shard_map/ppermute | solution.py:273
  49.6 1.0 fusion.6
  50.7 0.0 collective-permute-start.2
  50.7 0.0 copy-done.5
  50.7 0.1 copy.11
  50.8 0.1 reduce
  50.9 0.6 pad_add_fusion.place
  51.5 3.4 %collective-permute-start.7 = (f32[51,16,128]{2,1,0:T(8,128)}, f32[51,16,128]{2,1,0:T(8,128)}, u32[]{:S(2)}, u32[]{:S(2)}) collective-permute-start(f32[51,16,128]{2,1,0:T(8,128)} %get-tuple-element.15), channel_id=1, source_target_pairs={{0,7},{1,0},{2,1},{3,2},{4,3},{5,4},{6,5},{7,6},{8,15},{9,8},{10,9... | collective-permute-start | bytes 1253384 | tf_op jit(solution)/shard_map/ppermute | solution.py:274
  54.9 6.1 %collective-permute-done.2 = f32[51,16,128]{2,1,0:T(8,128)} collective-permute-done((f32[51,16,128]{2,1,0:T(8,128)}, f32[51,16,128]{2,1,0:T(8,128)}, u32[]{:S(2)}, u32[]{:S(2)}) %collective-permute-start.2) | collective-permute-done | bytes 417824 | tf_op jit(solution)/shard_map/ppermute | solution.py:273
  60.9 1.1 fusion.8
  62.0 0.1 collective-permute-start.3
  62.1 0.8 slice_bitcast_fusion.4.own
  62.9 0.0 collective-permute-done.7.down
  62.9 7.4 %collective-permute-done.3.up = f32[51,16,128]{2,1,0:T(8,128)} collective-permute-done((f32[51,16,128]{2,1,0:T(8,128)S(1)}, f32[51,16,128]{2,1,0:T(8,128)}, u32[]{:S(2)}, u32[]{:S(2)}) %collective-permute-start.3) | collective-permute-done | bytes 417824 | tf_op jit(solution)/shard_map/ppermute | solution.py:274
  70.3 3.8 %pack.1 = (f32[24,16,128]{2,1,0:T(8,128)}, f32[24,16,128]{2,1,0:T(8,128)}, f32[16,3,16,128]{3,2,1,0:T(8,128)}) custom-call(s32[2]{0:T(128)} %pad_add_fusion.place, f32[51,16,128]{2,1,0:T(8,128)} %slice_bitcast_fusion.4.own, f32[51,16,128]{2,1,0:T(8,128)} %collective-permute-done.3.up, f32[51,16,128]{2,1,0:T(8,128)} %collective-permute-done.7.down), custom_call_target="tpu_custom_call" | custom-call | tf_op jit(solution)/shard_map/pack/pallas_call | solution.py:148
  74.1 0.0 copy-start.6
  74.1 5.1 %all-to-all-start = ((f32[16,3,16,128]{3,2,1,0:T(8,128)}), f32[16,3,16,128]{3,2,1,0:T(8,128)S(1)}, u32[]{:S(2)}, u32[]{:S(2)}) async-start(f32[16,3,16,128]{3,2,1,0:T(8,128)} %get-tuple-element.10), calls=%async_computation | async-start | bytes 786432 | tf_op jit(solution)/shard_map/all_to_all | solution.py:317
  79.2 0.1 select_reduce_fusion.1
  79.3 0.1 fusion.10.relabel
  79.4 1.5 %collective-permute-start.8 = (f32[24,16,128]{2,1,0:T(8,128)}, f32[24,16,128]{2,1,0:T(8,128)S(1)}, u32[]{:S(2)}, u32[]{:S(2)}) collective-permute-start(f32[24,16,128]{2,1,0:T(8,128)} %get-tuple-element.9), channel_id=1, source_target_pairs={{0,8},{8,0},{1,9},{9,1},{2,10},{10,2},{3,11},{11,3},{4,12},{12,4},... | collective-permute-start | bytes 589832 | tf_op jit(solution)/shard_map/ppermute | solution.py:316
  80.9 4.2 %collective-permute-done.8.got = f32[24,16,128]{2,1,0:T(8,128)S(1)} collective-permute-done((f32[24,16,128]{2,1,0:T(8,128)}, f32[24,16,128]{2,1,0:T(8,128)S(1)}, u32[]{:S(2)}, u32[]{:S(2)}) %collective-permute-start.8) | collective-permute-done | bytes 196640 | tf_op jit(solution)/shard_map/ppermute | solution.py:316
  85.1 0.0 copy-start.4
  85.1 3.4 %all-to-all-done.mail = f32[16,3,16,128]{3,2,1,0:T(8,128)S(1)} async-done(((f32[16,3,16,128]{3,2,1,0:T(8,128)}), f32[16,3,16,128]{3,2,1,0:T(8,128)S(1)}, u32[]{:S(2)}, u32[]{:S(2)}) %all-to-all-start) | async-done | bytes 393248 | tf_op jit(solution)/shard_map/all_to_all | solution.py:317
  88.5 0.0 copy-start.3
  88.5 0.0 copy-done.4
  88.5 0.7 copy-done.3
  89.2 2.1 %join.1 = f32[16,24,256]{2,1,0:T(8,128)} custom-call(s32[2]{0:T(128)} %pad_add_fusion.place, f32[24,16,128]{2,1,0:T(8,128)} %get-tuple-element.8.keep, f32[24,16,128]{2,1,0:T(8,128)} %copy-done.4, f32[16,3,16,128]{3,2,1,0:T(8,128)} %copy-done.3), custom_call_target="tpu_custom_call" | custom-call | tf_op jit(solution)/shard_map/join/pallas_call | solution.py:178
  91.3 12.9 %all-to-all-start.1 = ((f32[16,24,256]{2,1,0:T(8,128)}), f32[16,24,256]{2,1,0:T(8,128)S(1)}, u32[]{:S(2)}, u32[]{:S(2)}) async-start(f32[16,24,256]{2,1,0:T(8,128)} %join.1), calls=%async_computation.1 | async-start | bytes 786432 | tf_op jit(solution)/shard_map/all_to_all | solution.py:320
  104.2 3.3 %select_multiply_fusion.basis = f32[512,384]{1,0:T(8,128)S(1)} fusion(f32[512]{0:T(512)S(1)} %compare_select_fusion.2, s32[384]{0:T(512)S(1)} %add_select_fusion.1, s32[512]{0:T(512)S(1)} %fusion.29, pred[384]{0:T(512)(128)(4,1)S(1)} %fusion.17), kind=kLoop, calls=%fused_computation.3 | loop fusion | flops 2359296 | bytes 792448 | tf_op jit(solution)/shard_map/mul | solution.py:250
  107.6 6.7 %all-to-all-done.1 = f32[16,24,256]{2,1,0:T(8,128)S(1)} async-done(((f32[16,24,256]{2,1,0:T(8,128)}), f32[16,24,256]{2,1,0:T(8,128)S(1)}, u32[]{:S(2)}, u32[]{:S(2)}) %all-to-all-start.1) | async-done | bytes 393248 | tf_op jit(solution)/shard_map/all_to_all | solution.py:320
  114.3 2.8 %transform.1 = f32[512,256]{1,0:T(8,128)} custom-call(f32[512,384]{1,0:T(8,128)S(1)} %select_multiply_fusion.basis, f32[384,256]{1,0:T(8,128)S(1)} %bitcast.39, f32[256,256]{1,0:T(8,128)S(1)} %fusion.10.relabel), custom_call_target="tpu_custom_call" | custom-call | tf_op jit(solution)/shard_map/transform/pallas_call | solution.py:201
  117.1 4.1 %all-to-all-start.2 = ((f32[16,32,256]{2,1,0:T(8,128)}), f32[16,32,256]{2,1,0:T(8,128)S(1)}, u32[]{:S(2)}, u32[]{:S(2)}) async-start(f32[16,32,256]{2,1,0:T(8,128)} %bitcast.15), calls=%async_computation.2 | async-start | bytes 1048576 | tf_op jit(solution)/shard_map/all_to_all | solution.py:323
  121.2 0.0 copy-done.6
  121.2 0.6 convert_element_type.15.events
  121.8 0.1 select_reduce_fusion.4
  121.9 0.6 compare_convert_fusion.inside
  122.4 10.0 %all-to-all-done.2.traces = f32[16,32,256]{2,1,0:T(8,128)S(1)} async-done(((f32[16,32,256]{2,1,0:T(8,128)}), f32[16,32,256]{2,1,0:T(8,128)S(1)}, u32[]{:S(2)}, u32[]{:S(2)}) %all-to-all-start.2) | async-done | bytes 524320 | tf_op jit(solution)/shard_map/all_to_all | solution.py:323
  132.4 0.0 copy-start.2
  132.4 0.8 copy-done.2
  133.2 2.3 %update.1 = bf16[32,16,256]{2,1,0:T(8,128)(2,1)} custom-call(f32[32]{0:T(128)} %convert_element_type.15.events, s32[32]{0:T(128)} %compare_convert_fusion.inside, f32[16,32,256]{2,1,0:T(8,128)} %copy-done.2, bf16[32,16,256]{2,1,0:T(8,128)(2,1)} %older.1, bf16[32,16,256]{2,1,0:T(8,128)(2,1)} %data.1), custom_call_target="tpu_custom_call" | custom-call | tf_op jit(solution)/shard_map/update/pallas_call | solution.py:226
  (18 shorter events, 0.3 us)
Async XLA Ops:
  0.8 2.8 %copy-start = (bf16[12,2,256,512]{3,2,1,0:T(8,128)(2,1)S(1)}, bf16[12,2,256,512]{3,2,1,0:T(8,128)(2,1)}, u32[]{:S(2)}) copy-start(bf16[12,2,256,512]{3,2,1,0:T(8,128)(2,1)} %spectra.1) | copy-start | bytes 18874372
  3.6 0.7 copy-start.1
  18.3 10.4 %collective-permute-start.4 = (f32[26,16,128]{2,1,0:T(8,128)S(1)}, f32[26,16,128]{2,1,0:T(8,128)S(1)}, u32[]{:S(2)}, u32[]{:S(2)}) collective-permute-start(f32[26,16,128]{2,1,0:T(8,128)S(1)} %get-tuple-element.19), channel_id=1, source_target_pairs={{0,7},{1,0},{2,1},{3,2},{4,3},{5,4},{6,5},{7,6},{8,15},{9,8},{10,9... | collective-permute-start | bytes 638984 | tf_op jit(solution)/shard_map/ppermute | solution.py:271
  24.8 25.9 %copy-start.5 = (s32[16]{0:T(128)S(1)}, s32[16]{0:T(128)}, u32[]{:S(2)}) copy-start(s32[16]{0:T(128)} %param.11) | copy-start | bytes 196
  24.8 7.4 %collective-permute-start = (f32[25,16,128]{2,1,0:T(8,128)S(1)}, f32[25,16,128]{2,1,0:T(8,128)S(1)}, u32[]{:S(2)}, u32[]{:S(2)}) collective-permute-start(f32[25,16,128]{2,1,0:T(8,128)S(1)} %get-tuple-element.18), channel_id=1, source_target_pairs={{0,1},{1,2},{2,3},{3,4},{4,5},{5,6},{6,7},{7,0},{8,9},{9,10},{10,1... | collective-permute-start | bytes 614408 | tf_op jit(solution)/shard_map/ppermute | solution.py:271
  28.7 10.9 %collective-permute-start.5 = (f32[51,16,128]{2,1,0:T(8,128)S(1)}, f32[51,16,128]{2,1,0:T(8,128)S(1)}, u32[]{:S(2)}, u32[]{:S(2)}) collective-permute-start(f32[51,16,128]{2,1,0:T(8,128)S(1)} %pad_maximum_fusion.1), channel_id=1, source_target_pairs={{0,7},{1,0},{2,1},{3,2},{4,3},{5,4},{6,5},{7,6},{8,15},{9,8},{10,9... | collective-permute-start | bytes 1253384 | tf_op jit(solution)/shard_map/ppermute | solution.py:272
  32.3 10.9 %collective-permute-start.1 = (f32[51,16,128]{2,1,0:T(8,128)S(1)}, f32[51,16,128]{2,1,0:T(8,128)S(1)}, u32[]{:S(2)}, u32[]{:S(2)}) collective-permute-start(f32[51,16,128]{2,1,0:T(8,128)S(1)} %pad_maximum_fusion), channel_id=1, source_target_pairs={{0,1},{1,2},{2,3},{3,4},{4,5},{5,6},{6,7},{7,0},{8,9},{9,10},{10,1... | collective-permute-start | bytes 1253384 | tf_op jit(solution)/shard_map/ppermute | solution.py:272
  39.7 9.9 %collective-permute-start.6 = (f32[51,16,128]{2,1,0:T(8,128)S(1)}, f32[51,16,128]{2,1,0:T(8,128)S(1)}, u32[]{:S(2)}, u32[]{:S(2)}) collective-permute-start(f32[51,16,128]{2,1,0:T(8,128)S(1)} %fusion.5), channel_id=1, source_target_pairs={{0,7},{1,0},{2,1},{3,2},{4,3},{5,4},{6,5},{7,6},{8,15},{9,8},{10,9... | collective-permute-start | bytes 1253384 | tf_op jit(solution)/shard_map/ppermute | solution.py:273
  50.7 10.3 %collective-permute-start.2 = (f32[51,16,128]{2,1,0:T(8,128)}, f32[51,16,128]{2,1,0:T(8,128)}, u32[]{:S(2)}, u32[]{:S(2)}) collective-permute-start(f32[51,16,128]{2,1,0:T(8,128)} %get-tuple-element.16), channel_id=1, source_target_pairs={{0,1},{1,2},{2,3},{3,4},{4,5},{5,6},{6,7},{7,0},{8,9},{9,10},{10,1... | collective-permute-start | bytes 1253384 | tf_op jit(solution)/shard_map/ppermute | solution.py:273
  51.5 11.4 %collective-permute-start.7 = (f32[51,16,128]{2,1,0:T(8,128)}, f32[51,16,128]{2,1,0:T(8,128)}, u32[]{:S(2)}, u32[]{:S(2)}) collective-permute-start(f32[51,16,128]{2,1,0:T(8,128)} %get-tuple-element.15), channel_id=1, source_target_pairs={{0,7},{1,0},{2,1},{3,2},{4,3},{5,4},{6,5},{7,6},{8,15},{9,8},{10,9... | collective-permute-start | bytes 1253384 | tf_op jit(solution)/shard_map/ppermute | solution.py:274
  62.0 8.3 %collective-permute-start.3 = (f32[51,16,128]{2,1,0:T(8,128)S(1)}, f32[51,16,128]{2,1,0:T(8,128)}, u32[]{:S(2)}, u32[]{:S(2)}) collective-permute-start(f32[51,16,128]{2,1,0:T(8,128)S(1)} %fusion.8), channel_id=1, source_target_pairs={{0,1},{1,2},{2,3},{3,4},{4,5},{5,6},{6,7},{7,0},{8,9},{9,10},{10,1... | collective-permute-start | bytes 1253384 | tf_op jit(solution)/shard_map/ppermute | solution.py:274
  74.1 47.1 %copy-start.6 = (s32[32]{0:T(128)S(1)}, s32[32]{0:T(128)}, u32[]{:S(2)}) copy-start(s32[32]{0:T(128)} %param.12) | copy-start | bytes 388
  74.1 14.4 %all-to-all-start = ((f32[16,3,16,128]{3,2,1,0:T(8,128)}), f32[16,3,16,128]{3,2,1,0:T(8,128)S(1)}, u32[]{:S(2)}, u32[]{:S(2)}) async-start(f32[16,3,16,128]{3,2,1,0:T(8,128)} %get-tuple-element.10), calls=%async_computation | async-start | bytes 786432 | tf_op jit(solution)/shard_map/all_to_all | solution.py:317
  79.4 5.7 %collective-permute-start.8 = (f32[24,16,128]{2,1,0:T(8,128)}, f32[24,16,128]{2,1,0:T(8,128)S(1)}, u32[]{:S(2)}, u32[]{:S(2)}) collective-permute-start(f32[24,16,128]{2,1,0:T(8,128)} %get-tuple-element.9), channel_id=1, source_target_pairs={{0,8},{8,0},{1,9},{9,1},{2,10},{10,2},{3,11},{11,3},{4,12},{12,4},... | collective-permute-start | bytes 589832 | tf_op jit(solution)/shard_map/ppermute | solution.py:316
  85.1 3.4 %copy-start.4 = (f32[24,16,128]{2,1,0:T(8,128)}, f32[24,16,128]{2,1,0:T(8,128)S(1)}, u32[]{:S(2)}) copy-start(f32[24,16,128]{2,1,0:T(8,128)S(1)} %collective-permute-done.8.got) | copy-start | bytes 589828
  88.5 0.7 copy-start.3
  91.3 23.0 %all-to-all-start.1 = ((f32[16,24,256]{2,1,0:T(8,128)}), f32[16,24,256]{2,1,0:T(8,128)S(1)}, u32[]{:S(2)}, u32[]{:S(2)}) async-start(f32[16,24,256]{2,1,0:T(8,128)} %join.1), calls=%async_computation.1 | async-start | bytes 786432 | tf_op jit(solution)/shard_map/all_to_all | solution.py:320
  117.1 15.3 %all-to-all-start.2 = ((f32[16,32,256]{2,1,0:T(8,128)}), f32[16,32,256]{2,1,0:T(8,128)S(1)}, u32[]{:S(2)}, u32[]{:S(2)}) async-start(f32[16,32,256]{2,1,0:T(8,128)} %bitcast.15), calls=%async_computation.2 | async-start | bytes 1048576 | tf_op jit(solution)/shard_map/all_to_all | solution.py:323
  132.4 0.8 copy-start.2

commit v2 on v1

v2 whole, which is shorter than its diff:
```python
import functools
import math

import jax
import jax.numpy as jnp
from jax import lax
from jax.experimental import pallas as pl
from jax.experimental.pallas import tpu as pltpu
from jax.sharding import Mesh, PartitionSpec as P

F = 192
NT = 384
LANES = 128
BLOCK = 16
RING = 8
PRODUCT_VMEM = 59 * 1024 * 1024
SMALL_VMEM = 24 * 1024 * 1024

shrink_level = 0.25
step_weight = 0.5


def window(near, far, shift):
    lane = lax.broadcasted_iota(jnp.int32, near.shape, 1)
    row = lax.broadcasted_iota(jnp.int32, near.shape, 0)
    if shift:
        near = pltpu.roll(near, LANES - shift, 1)
        far = pltpu.roll(far, LANES - shift, 1)
    return jnp.where((lane < LANES - shift) & (lane >= row), near, far)


def product_kernel(
    pairing, ratio, spectra, primaries, keep_first, keep, give_first, give, own,
    left, right, relabel, relabel_low, chosen, held, out, slots, left_sems, right_sems, out_sems,
):
    freqs, _, width, depth = left.shape
    count = freqs // 2
    half = width // 2
    rows = 2 * count
    tail = 2 * rows * BLOCK
    core, zi = lax.axis_index("core"), lax.axis_index("z")
    lane = lax.broadcasted_iota(jnp.int32, (BLOCK, LANES), 1)
    level = lax.broadcasted_iota(jnp.int32, (BLOCK, LANES), 0)

    def fetch_left(i):
        return pltpu.make_async_copy(spectra.at[i], left.at[i], left_sems.at[i])

    def fetch_right(i):
        return pltpu.make_async_copy(primaries.at[i], right.at[i], right_sems.at[i])

    for i in range(freqs):
        fetch_right(i).start()
        fetch_left(i).start()
    block = lax.broadcasted_iota(jnp.int32, (8, width), 1) // BLOCK
    source = jnp.zeros((8, width), jnp.int32)
    for b in range(width // BLOCK):
        source = jnp.where(block == b, pairing[b], source)
    source = source * BLOCK + lax.broadcasted_iota(jnp.int32, (8, width), 1) % BLOCK
    for r in range(0, width, 8):
        row = lax.broadcasted_iota(jnp.int32, (8, width), 0) + r
        relabel[r : r + 8] = jnp.where(row == source, 1.0, 0.0)
    relabel_low[...] = relabel[...].astype(jnp.bfloat16)
    out[:, tail:] = jnp.zeros((out.shape[0], out.shape[1] - tail, LANES), out.dtype)
    for second in range(2):
        long_up = second == core
        for t in range(RING):
            k = lax.rem(t - zi + RING, RING)
            away = jnp.where(k <= 4, 4 - k, k - 4)
            goes_up = (k < 4) | ((k == 4) & long_up)
            send = 2 * away - jnp.where(long_up == goes_up, 0, 1)
            mine = goes_up == (core == 0)
            slots[second, t] = jnp.where(k == 0, 14 + second, send + jnp.where(mine, 0, 7))

    def cut(i):
        second = lax.div(i, count)
        real, imag = held[i & 1, 0], held[i & 1, 1]
        real = 0.5 * (real + real.T)
        imag = 0.5 * (imag + imag.T)
        wr = ratio[0, i]
        wi = ratio[1, i]
        for c, z in enumerate((wr * real - wi * imag, wr * imag + wi * real)):
            row = 2 * i + c
            shift = row & 7
            place = tail + (row >> 3) - second * (2 * count // 8)
            row = row - second * rows
            for t in range(RING):
                k = slots[second, t]
                low = z[BLOCK * t : BLOCK * (t + 1)]
                high = z[half + BLOCK * t : half + BLOCK * (t + 1)]
                out[k, pl.ds(pl.multiple_of(row * BLOCK, BLOCK), BLOCK)] = window(
                    low[:, :half], low[:, half:], BLOCK * t
                )
                out[k, pl.ds(pl.multiple_of((rows + row) * BLOCK, BLOCK), BLOCK)] = window(
                    high[:, half:], high[:, :half], BLOCK * t
                )
                middle = jnp.where(lane == level + BLOCK * t, low[:, half:], 0.0)
                middle = jnp.sum(middle, axis=0, keepdims=True)
                middle = pltpu.roll(middle, (BLOCK * (shift - t)) & (LANES - 1), 1)
                out[k, pl.ds(place, 1)] += middle

    def multiply(i):
        a = left[i].reshape(2 * width, depth)
        by_real = jnp.dot(a, chosen[i & 1, 0], preferred_element_type=jnp.float32)
        by_imag = jnp.dot(a, chosen[i & 1, 1], preferred_element_type=jnp.float32)
        held[i & 1, 0] = by_real[:width] - by_imag[width:]
        held[i & 1, 1] = by_imag[:width] + by_real[width:]

    def choose(i):
        for b in range(2):
            chosen[i & 1, b] = jnp.dot(
                right[i, b], relabel_low[...], preferred_element_type=jnp.float32
            ).astype(jnp.bfloat16)

    def stages(i, carry):
        fetch_right(i).wait()
        fetch_left(i - 1).wait()
        cut(i - 2)
        multiply(i - 1)
        choose(i)
        return carry

    def copies(moves):
        return [
            pltpu.make_async_copy(out.at[slot], dst.at[i], out_sems.at[slot])
            for slot, dst, i in moves
        ]

    early = copies(
        [(0, keep_first, 0)]
        + [(n, keep, n - 1) for n in (2, 4, 6)]
        + [(7 + n, give, n - 1) for n in (1, 3, 5)]
        + [(14, own, 0)]
    )
    late = copies(
        [(7, give_first, 0)]
        + [(n, keep, n - 1) for n in (1, 3, 5)]
        + [(7 + n, give, n - 1) for n in (2, 4, 6)]
        + [(15, own, 1)]
    )
    fetch_right(0).wait()
    choose(0)
    fetch_right(1).wait()
    fetch_left(0).wait()
    multiply(0)
    choose(1)
    lax.fori_loop(2, count + 2, stages, 0)
    for copy in early:
        copy.start()
    lax.fori_loop(count + 2, freqs, stages, 0)
    fetch_left(freqs - 1).wait()
    cut(freqs - 2)
    multiply(freqs - 1)
    cut(freqs - 1)
    for copy in late:
        copy.start()
    for copy in early + late:
        copy.wait()


def product(spectra, primaries, ratio, pairing):
    freqs = spectra.shape[0]
    width, depth = spectra.shape[2:]
    height = 2 * freqs * BLOCK + 8
    smem = pl.BlockSpec(memory_space=pltpu.SMEM)
    anywhere = pl.BlockSpec(memory_space=pl.ANY)
    shapes = [(n, height, LANES) for n in (1, 6, 1, 6, 2)]
    return pl.pallas_call(
        product_kernel,
        in_specs=[smem, smem, anywhere, anywhere],
        out_specs=[anywhere] * 5,
        out_shape=[jax.ShapeDtypeStruct(s, jnp.float32) for s in shapes],
        scratch_shapes=[
            pltpu.VMEM(spectra.shape, spectra.dtype),
            pltpu.VMEM(primaries.shape, primaries.dtype),
            pltpu.VMEM((width, width), jnp.float32),
            pltpu.VMEM((width, width), jnp.bfloat16),
            pltpu.VMEM((2, 2, depth, width), jnp.bfloat16),
            pltpu.VMEM((2, 2, width, width), jnp.float32),
            pltpu.VMEM((16, height, LANES), jnp.float32),
            pltpu.SMEM((2, RING), jnp.int32),
            pltpu.SemaphoreType.DMA((freqs,)),
            pltpu.SemaphoreType.DMA((freqs,)),
            pltpu.SemaphoreType.DMA((16,)),
        ],
        compiler_params=pltpu.CompilerParams(vmem_limit_bytes=PRODUCT_VMEM),
        cost_estimate=pl.CostEstimate(
            flops=freqs * 2 * 2 * width * 2 * width * depth,
            bytes_accessed=freqs * 8 * width * depth + 16 * height * LANES * 4,
            transcendentals=0,
        ),
        name="product",
    )(pairing, ratio, spectra, primaries)


def collect_kernel(keep, got, *refs):
    arrived, out = refs[:-2], refs[-1]
    for i, part in enumerate((keep, got)):
        out[i] = arrived[0][i] + part[0] if arrived else part[0]


def collect(index, keep, got, before, *arrived):
    shape = (2,) + keep.shape[1:]
    one = pl.BlockSpec((1,) + shape[1:], lambda i: (index, 0, 0))
    whole = pl.BlockSpec(shape, lambda i: (0, 0, 0))
    return pl.pallas_call(
        collect_kernel,
        grid=(1,),
        in_specs=[one, one] + [whole] * len(arrived) + [pl.BlockSpec(memory_space=pl.ANY)],
        out_specs=whole,
        out_shape=jax.ShapeDtypeStruct(shape, jnp.float32),
        compiler_params=pltpu.CompilerParams(vmem_limit_bytes=SMALL_VMEM),
        name="collect",
    )(keep, got, *arrived, before)


def exchange_lanes(tiles):
    lane = lax.broadcasted_iota(jnp.int32, tiles[0].shape, 1) // BLOCK
    for bit in (1, 2, 4):
        upper = (lane // bit) % 2 == 1
        out = list(tiles)
        for a in range(8):
            if a & bit:
                continue
            x, y = tiles[a], tiles[a | bit]
            out[a] = jnp.where(upper, pltpu.roll(y, BLOCK * bit, 1), x)
            out[a | bit] = jnp.where(upper, y, pltpu.roll(x, LANES - BLOCK * bit, 1))
        tiles = out
    return tiles


def ring_total(refs, half, start, size=BLOCK):
    own, late, early, got_late, got_early = refs
    at = pl.ds(start, size)
    if half:
        return own[1, at] + early[0, at] + got_late[at]
    return own[0, at] + late[0, at] + got_early[at]


def direct_kernel(*refs):
    keep, give = refs[5:]
    yl = lax.axis_index("yl")
    rows = keep.shape[0] // 2
    for half in range(2):
        for a in range(rows):
            for h, dst in ((yl, keep), (1 - yl, give)):
                start = pl.multiple_of(BLOCK * (rows * h + a), BLOCK)
                dst[rows * half + a] = ring_total(refs[:5], half, start)


def turn_blocks(x):
    turned = x.T
    out = jnp.zeros(x.shape, x.dtype)
    for a in range(8):
        block = jnp.concatenate(
            [turned[BLOCK * a : BLOCK * (a + 1)], jnp.zeros((BLOCK, LANES - BLOCK), x.dtype)],
            axis=1,
        )
        out = out + (pltpu.roll(block, BLOCK * a, 1) if a else block)
    return out


def mail_kernel(*refs):
    mail = refs[5]
    zi = lax.axis_index("z")
    groups = mail.shape[1]
    rows = 4 * groups
    across = lax.broadcasted_iota(jnp.int32, (BLOCK, LANES), 1) % BLOCK
    down = lax.broadcasted_iota(jnp.int32, (BLOCK, LANES), 0)

    for g in range(groups):
        firsts = []
        for h in range(2):
            tiles = [
                ring_total(refs[:5], row // rows, BLOCK * (rows * h + row % rows))
                for row in range(8 * g, 8 * g + 8)
            ]
            swapped = exchange_lanes(tiles)
            firsts.append(swapped[0])
            for m in range(1, 8):
                mail[lax.rem(zi + 8 * h + m, 16), g] = swapped[m]
        middle = 0.0
        for half in range(2):
            if rows * half < 8 * g + 8 and rows * (half + 1) > 8 * g:
                place = 2 * rows * BLOCK + g - rows * half // 8
                middle = middle + ring_total(refs[:5], half, place, 1)
        for at, below, above in ((8, firsts[0], firsts[1]), (0, firsts[1], firsts[0])):
            mail[zi + at, g] = jnp.where(
                across < down, below, jnp.where(across == down, middle, turn_blocks(above))
            )


def pack(rows, *sums):
    whole = pl.BlockSpec(memory_space=pltpu.VMEM)

    def call(kernel, shapes, name):
        return pl.pallas_call(
            kernel,
            in_specs=[whole] * 5,
            out_specs=[whole] * len(shapes),
            out_shape=[jax.ShapeDtypeStruct(s, jnp.float32) for s in shapes],
            compiler_params=pltpu.CompilerParams(vmem_limit_bytes=SMALL_VMEM),
            name=name,
        )(*sums)

    keep, give = call(direct_kernel, [(rows, BLOCK, LANES)] * 2, "direct")
    (mail,) = call(mail_kernel, [(16, rows // 8, BLOCK, LANES)], "mail")
    return keep, give, mail


def join_kernel(keep, got, mail, out):
    zi = lax.axis_index("z")
    groups = mail.shape[1]
    lane = lax.broadcasted_iota(jnp.int32, (BLOCK, LANES), 1)
    level = lax.broadcasted_iota(jnp.int32, (BLOCK, LANES), 0)
    rest = jnp.zeros((BLOCK, LANES - BLOCK), jnp.float32)
    for g in range(groups):
        stack = []
        for k in range(8):
            z = lax.rem(zi + k, 8)
            stack.append(mail[z, g] + mail[z + 8, g])
        turned = jnp.concatenate(stack, axis=0).T.reshape(8, BLOCK, LANES)
        tiles = [keep[8 * g + a] + got[8 * g + a] for a in range(8)]
        packed = jnp.where(lane < BLOCK, tiles[0], 0.0)
        for a in range(1, 8):
            packed = packed + pltpu.roll(jnp.where(lane < BLOCK, tiles[a], 0.0), BLOCK * a, 1)
        upper = packed.T
        direct = jnp.stack(
            [
                jnp.where(
                    lane < level,
                    jnp.concatenate([upper[BLOCK * a : BLOCK * (a + 1)], rest], axis=1),
                    tiles[a],
                )
                for a in range(8)
            ]
        )
        out[:, 8 * g : 8 * g + 8, :LANES] = jnp.swapaxes(direct, 0, 1)
        out[:, 8 * g : 8 * g + 8, LANES:] = jnp.swapaxes(turned, 0, 1)


def join(keep, got, mail):
    groups = mail.shape[1]
    whole = pl.BlockSpec(memory_space=pltpu.VMEM)
    return pl.pallas_call(
        join_kernel,
        in_specs=[whole] * 3,
        out_specs=whole,
        out_shape=jax.ShapeDtypeStruct((BLOCK, 8 * groups, 2 * LANES), jnp.float32),
        compiler_params=pltpu.CompilerParams(vmem_limit_bytes=SMALL_VMEM),
        name="join",
    )(keep, got, mail)


def transform_kernel(basis, data, relabel, out):
    dot = functools.partial(jnp.dot, preferred_element_type=jnp.float32)
    x = data[...]
    high = x.astype(jnp.bfloat16)
    low = (x - high.astype(jnp.float32)).astype(jnp.bfloat16)
    high = dot(high, relabel[...]).astype(jnp.bfloat16)
    low = dot(low, relabel[...]).astype(jnp.bfloat16)
    out[...] = dot(basis[0], high) + (dot(basis[0], low) + dot(basis[1], high))


def transform(basis, data, relabel):
    whole = pl.BlockSpec(memory_space=pltpu.VMEM)
    return pl.pallas_call(
        transform_kernel,
        in_specs=[whole] * 3,
        out_specs=whole,
        out_shape=jax.ShapeDtypeStruct((basis.shape[1], data.shape[1]), jnp.float32),
        compiler_params=pltpu.CompilerParams(vmem_limit_bytes=SMALL_VMEM),
        name="transform",
    )(basis, data, relabel)


def update_kernel(events, inside, traces, older, data, out):
    count = older.shape[0]
    for t in range(count):
        old = older[t].astype(jnp.float32)
        moved = old + step_weight * events[t] * (
            data[t].astype(jnp.float32) - old - traces[:, t, :]
        )
        size = jnp.maximum(jnp.abs(moved) - shrink_level, 0.0)
        shrunk = jnp.where(moved < 0.0, -size, size)
        out[t] = jnp.where(inside[t] > 0, shrunk, 0.0).astype(jnp.bfloat16)


def update(events, inside, traces, older, data):
    whole = pl.BlockSpec(memory_space=pltpu.VMEM)
    scalars = pl.BlockSpec(memory_space=pltpu.SMEM)
    return pl.pallas_call(
        update_kernel,
        in_specs=[scalars, scalars, whole, whole, whole],
        out_specs=whole,
        out_shape=jax.ShapeDtypeStruct(older.shape, jnp.bfloat16),
        compiler_params=pltpu.CompilerParams(vmem_limit_bytes=SMALL_VMEM),
        name="update",
    )(events, inside, traces, older, data)


def slot_windows(slots, window_lengths, capacity):
    starts = jnp.cumsum(window_lengths) - window_lengths
    window = slots // capacity
    offset = slots % capacity
    select = window[:, None] == jnp.arange(window_lengths.shape[0], dtype=jnp.int32)[None, :]
    begin = jnp.sum(jnp.where(select, starts[None, :], 0), axis=1)
    length = jnp.sum(jnp.where(select, window_lengths[None, :], 0), axis=1)
    return begin + offset, offset < length


def time_basis(times, inside, freqs):
    phase = times[:, None] * freqs[None, :] % NT
    angle = phase.astype(jnp.float32) * (2.0 * math.pi / NT)
    scale = jnp.where(inside, 1.0 / math.sqrt(F), 0.0).astype(jnp.float32)[:, None]
    odd = (jnp.arange(freqs.shape[0]) % 2 == 1)[None, :]
    return jnp.where(odd, -jnp.sin(angle), jnp.cos(angle)) * scale


def ring(n, d):
    return [(i, (i + d) % n) for i in range(n)]


def other_half_kernel(arrived, before, out):
    out[...] = arrived[1]


def other_half(arrived, before):
    whole = pl.BlockSpec(memory_space=pltpu.VMEM)
    return pl.pallas_call(
        other_half_kernel,
        in_specs=[whole, pl.BlockSpec(memory_space=pl.ANY)],
        out_specs=whole,
        out_shape=jax.ShapeDtypeStruct(arrived.shape[1:], arrived.dtype),
        compiler_params=pltpu.CompilerParams(vmem_limit_bytes=SMALL_VMEM),
        name="other_half",
    )(arrived, before)


def ring_sums(keep_first, keep, give_first, give):
    swap = functools.partial(lax.ppermute, axis_name="core", perm=ring(2, 1))
    step = functools.partial(
        lax.ppermute,
        axis_name=("core", "z"),
        perm=[
            (c * RING + z, c * RING + (z + (1 if c == 0 else -1)) % RING)
            for c in range(2)
            for z in range(RING)
        ],
    )
    payload = collect(0, keep_first, swap(give_first), keep_first)
    payload, give = lax.optimization_barrier((payload, give))
    got = swap(give)
    flying = [step(payload)]
    for n in range(6):
        payload = collect(n, keep, got, payload, *flying[:-1])
        flying = flying[-1:] + [step(payload)]
    early, late = flying
    return late, early, swap(late[1]), swap(other_half(early, payload))


def on_device(
    spectra, primaries, wavelet_ratio, window_lengths, event_mask, pairing, old_traces, data_traces
):
    src = ("yl", "z")
    freq = ("x", "yh", "core")
    freq_count = lax.axis_size(freq)
    freq_dev = spectra.shape[0]
    width = spectra.shape[2]
    capacity = old_traces.shape[0]
    yl, zi = lax.axis_index("yl"), lax.axis_index("z")
    own = yl * 8 + zi
    lanes = jnp.arange(width, dtype=jnp.int32)
    blocks = lanes // BLOCK
    ids = jnp.arange(pairing.shape[0], dtype=jnp.int32)

    def paired(block):
        return jnp.sum(jnp.where(block[:, None] == ids[None, :], pairing[None, :], 0), axis=1)

    target = paired((blocks + own) % pairing.shape[0]) * BLOCK + lanes % BLOCK
    restore = (target[:, None] == lanes[None, :]).astype(jnp.bfloat16)
    slots = jnp.arange(capacity * freq_count, dtype=jnp.int32)
    times, inside = slot_windows(slots, window_lengths, capacity)
    basis = time_basis(
        times, inside, jnp.arange(2 * freq_dev * freq_count, dtype=jnp.int32) // 2
    )
    coarse = lax.reduce_precision(basis, 8, 7)
    basis = jnp.stack([coarse, basis - coarse]).astype(jnp.bfloat16)
    own_slots = lax.axis_index(freq) * capacity + jnp.arange(capacity, dtype=jnp.int32)
    _, inside_own = slot_windows(own_slots, window_lengths, capacity)

    *sends, ends = product(spectra, primaries, wavelet_ratio, pairing)
    keep, give, mail = pack(2 * freq_dev, ends, *ring_sums(*sends))
    got = lax.ppermute(give, "yl", ring(2, 1))
    mail = lax.all_to_all(mail, src, split_axis=0, concat_axis=0, tiled=True)
    whole = join(keep, got, mail)
    spread = lax.all_to_all(whole, freq, split_axis=0, concat_axis=0, tiled=True)
    slotted = transform(basis, spread.reshape(-1, width), restore)
    slotted = slotted.reshape(freq_count, capacity, width)
    traces = lax.all_to_all(slotted, freq, split_axis=0, concat_axis=0, tiled=True)
    return update(
        event_mask.astype(jnp.float32),
        inside_own.astype(jnp.int32),
        traces,
        old_traces,
        data_traces,
    )


def solution(mesh):
    shape = tuple(mesh.shape.values())
    cores = 2 if shape[0] % 2 == 0 else 1
    yh = 2 if shape[0] % 4 == 0 else 1
    devices = mesh.devices.reshape(shape[0] // (cores * yh), yh, cores, shape[1] // 8, 8)
    split = Mesh(devices, ("x", "yh", "core", "yl", "z"))
    freq = ("x", "yh", "core")
    src = ("yl", "z")
    in_specs = (
        P(freq, None, None, src),
        P(freq, None, src, None),
        P(None, freq),
        P(),
        P(freq),
        P(),
        P(freq, src, None),
        P(freq, src, None),
    )
    return jax.shard_map(
        on_device, mesh=split, in_specs=in_specs, out_specs=P(freq, src, None), check_vma=False
    )
```

time: 136 us -> 115 us (0.85)
  waiting for transfers between devices: 55.2 us -> 35.7 us
  starting transfers between devices: 40.6 us -> 54.2 us
  Pallas kernels: 25 us -> 17.7 us
  other arithmetic: 8.54 us -> 4.53 us
  local copies, waits for them, and re-layouts: 5.94 us -> 2.33 us
    ppermute x8 -> x11, waiting for transfers between devices: 30.9 us -> 9.29 us  [the longest x6 6.33 us: ring_sums(): flying = flying[-1:] + [step(payload)]]
    ppermute x8 -> x11, starting transfers between devices: 17.1 us -> 32.6 us  [the longest x6 18.8 us: ring_sums(): flying = flying[-1:] + [step(payload)]]
    pallas_call x3 -> x12, Pallas kernels: 19.9 us -> 14.5 us  [the longest x1 11.2 us: product(): pl.pallas_call(product_kernel, in_specs=[smem, smem, anywhere, anywhere],...]
    all_to_all x1, starting transfers between devices: 12.9 us -> 9.25 us  [on_device(): lax.all_to_all(whole, freq, split_axis=0, concat_axis=0, tiled=True)]
    another operation x3 -> x4, other arithmetic: 0.71 us -> 4.09 us  [the longest x1 0.56 us: on_device(): place = jnp.stack([yl, zi])]
    mul x1 -> x0, other arithmetic: 3.33 us -> none  [time_basis(): return jnp.where(odd, -jnp.sin(angle), jnp.cos(angle)) * scale]
    all_to_all x1, waiting for transfers between devices: 6.73 us -> 9.87 us  [on_device(): lax.all_to_all(whole, freq, split_axis=0, concat_axis=0, tiled=True)]
    unnamed x14 -> x16, local copies, waits for them, and re-layouts: 5.01 us -> 2.24 us
  transfers between devices with their start and end apart: 12 -> 15, of which waited for: 9 -> 13; matrix products, arithmetic and copies ran while one was open for 6% -> 4% of each run, Pallas kernels for 0% -> 0%
where the time goes in v2:
time: 115 us
  starting transfers between devices  54.2 us (47%)
  waiting for transfers between devices  35.7 us (31%)
  Pallas kernels  17.7 us (15%)
  other arithmetic  4.53 us (4%)
  local copies, waits for them, and re-layouts  2.33 us (2%)
    ppermute x6, starting transfers between devices, ring_sums(): flying = flying[-1:] + [step(payload)]  18.8 us
    pallas_call x1, Pallas kernels, product(): pl.pallas_call(product_kernel, in_specs=[smem, smem, anywhere, anywhere],...  11.2 us
    all_to_all x1, waiting for transfers between devices, on_device(): lax.all_to_all(slotted, freq, split_axis=0, concat_axis=0, tiled=True)  11 us
    all_to_all x1, waiting for transfers between devices, on_device(): lax.all_to_all(whole, freq, split_axis=0, concat_axis=0, tiled=True)  9.87 us
    all_to_all x1, starting transfers between devices, on_device(): lax.all_to_all(whole, freq, split_axis=0, concat_axis=0, tiled=True)  9.25 us
    all_to_all x1, starting transfers between devices, on_device(): mail = lax.all_to_all(mail, src, split_axis=0, concat_axis=0, tiled=True)  6.68 us
    ppermute x6, waiting for transfers between devices, ring_sums(): flying = flying[-1:] + [step(payload)]  6.33 us
    ppermute x2, starting transfers between devices, ring_sums(): return (late, early, swap(late[1]), swap(other_half(early, payload)))  6.17 us
  transfers between devices with their start and end apart: 15, of which 13 were waited for; matrix products, arithmetic and copies ran while one was open for 4% of the time, Pallas kernels for 0%

profile of v2, /device:TPU:1, one launch (start us, length us, event | category | flops | bytes accessed | tf_op | source)
XLA Modules:
  0.0 114.7 jit_solution(8130912202929575443)
XLA Ops:
  0.0 11.2 %product.1 = (f32[1,392,128]{2,1,0:T(8,128)}, f32[6,392,128]{2,1,0:T(8,128)}, f32[1,392,128]{2,1,0:T(8,128)}, f32[6,392,128]{2,1,0:T(8,128)}, f32[2,392,128]{2,1,0:T(8,128)}) custom-call(s32[16]{0:T(128)} %pairing.1, f32[2,12]{1,0:T(2,128)} %ratio.1, bf16[12,2,256,512]{3,2,1,0:T(8,128)(2,1)} %spectra.1, bf16[12,2,512,256]{3,2,1,0:T(8,128)(2,1)} %primaries.1), custom_call_target="tpu_custom_call" | custom-call | flops 3221225472 | bytes 15794176 | tf_op jit(solution)/shard_map/product/pallas_call | solution.py:167
  11.2 3.3 %collective-permute-start = (f32[1,392,128]{2,1,0:T(8,128)}, f32[1,392,128]{2,1,0:T(8,128)S(1)}, u32[]{:S(2)}, u32[]{:S(2)}) collective-permute-start(f32[1,392,128]{2,1,0:T(8,128)} %get-tuple-element.17), channel_id=1, source_target_pairs={{0,16},{16,0},{1,17},{17,1},{2,18},{18,2},{3,19},{19,3},{4,20},{20... | collective-permute-start | bytes 602120 | tf_op jit(solution)/shard_map/ppermute | solution.py:450
  14.5 1.3 %collective-permute-done.got = f32[1,392,128]{2,1,0:T(8,128)S(1)} collective-permute-done((f32[1,392,128]{2,1,0:T(8,128)}, f32[1,392,128]{2,1,0:T(8,128)S(1)}, u32[]{:S(2)}, u32[]{:S(2)}) %collective-permute-start) | collective-permute-done | bytes 200736 | tf_op jit(solution)/shard_map/ppermute | solution.py:450
  15.8 0.0 copy-start.2
  15.8 0.9 copy-done.2
  16.7 0.5 collective-permute-start.1
  17.2 3.9 %collective-permute-start.2 = (f32[2,392,128]{2,1,0:T(8,128)S(1)}, f32[2,392,128]{2,1,0:T(8,128)S(1)}, u32[]{:S(2)}, u32[]{:S(2)}) collective-permute-start(f32[2,392,128]{2,1,0:T(8,128)S(1)} %collect.7.refs_0_), channel_id=1, source_target_pairs={{0,1},{1,2},{2,3},{3,4},{4,5},{5,6},{6,7},{7,0},{16,23},{17,16},{1... | collective-permute-start | bytes 1204232 | tf_op jit(solution)/shard_map/ppermute | solution.py:453
  21.0 0.0 collective-permute-done.1.got
  21.1 0.0 copy-start
  21.1 1.3 %copy-done = f32[6,392,128]{2,1,0:T(8,128)S(1)} copy-done((f32[6,392,128]{2,1,0:T(8,128)S(1)}, f32[6,392,128]{2,1,0:T(8,128)}, u32[]{:S(2)}) %copy-start) | copy-done | bytes 1204248
  22.4 2.8 %collective-permute-start.4 = (f32[2,392,128]{2,1,0:T(8,128)S(1)}, f32[2,392,128]{2,1,0:T(8,128)S(1)}, u32[]{:S(2)}, u32[]{:S(2)}) collective-permute-start(f32[2,392,128]{2,1,0:T(8,128)S(1)} %collect.8.refs_1_), channel_id=1, source_target_pairs={{0,1},{1,2},{2,3},{3,4},{4,5},{5,6},{6,7},{7,0},{16,23},{17,16},{1... | collective-permute-start | bytes 1204232 | tf_op jit(solution)/shard_map/ppermute | solution.py:456
  25.2 0.7 collective-permute-done.2.refs_0_
  25.9 3.2 %collective-permute-start.3 = (f32[2,392,128]{2,1,0:T(8,128)S(1)}, f32[2,392,128]{2,1,0:T(8,128)S(1)}, u32[]{:S(2)}, u32[]{:S(2)}) collective-permute-start(f32[2,392,128]{2,1,0:T(8,128)S(1)} %collect.9.refs_1_), channel_id=1, source_target_pairs={{0,1},{1,2},{2,3},{3,4},{4,5},{5,6},{6,7},{7,0},{16,23},{17,16},{1... | collective-permute-start | bytes 1204232 | tf_op jit(solution)/shard_map/ppermute | solution.py:456
  29.1 1.1 collective-permute-done.4.refs_0_
  30.2 0.1 collect.10.refs_1_
  30.2 3.2 %collective-permute-start.6 = (f32[2,392,128]{2,1,0:T(8,128)S(1)}, f32[2,392,128]{2,1,0:T(8,128)S(1)}, u32[]{:S(2)}, u32[]{:S(2)}) collective-permute-start(f32[2,392,128]{2,1,0:T(8,128)S(1)} %collect.10.refs_1_), channel_id=1, source_target_pairs={{0,1},{1,2},{2,3},{3,4},{4,5},{5,6},{6,7},{7,0},{16,23},{17,16},{1... | collective-permute-start | bytes 1204232 | tf_op jit(solution)/shard_map/ppermute | solution.py:456
  33.4 1.0 collective-permute-done.3.refs_0_
  34.5 0.1 collect.11.refs_1_
  34.5 3.2 %collective-permute-start.5 = (f32[2,392,128]{2,1,0:T(8,128)S(1)}, f32[2,392,128]{2,1,0:T(8,128)S(1)}, u32[]{:S(2)}, u32[]{:S(2)}) collective-permute-start(f32[2,392,128]{2,1,0:T(8,128)S(1)} %collect.11.refs_1_), channel_id=1, source_target_pairs={{0,1},{1,2},{2,3},{3,4},{4,5},{5,6},{6,7},{7,0},{16,23},{17,16},{1... | collective-permute-start | bytes 1204232 | tf_op jit(solution)/shard_map/ppermute | solution.py:456
  37.7 1.1 collective-permute-done.6.refs_0_
  38.8 0.0 copy-start.6
  38.8 0.0 copy-start.5
  38.8 3.2 %collective-permute-start.8 = (f32[2,392,128]{2,1,0:T(8,128)S(1)}, f32[2,392,128]{2,1,0:T(8,128)S(1)}, u32[]{:S(2)}, u32[]{:S(2)}) collective-permute-start(f32[2,392,128]{2,1,0:T(8,128)S(1)} %collect.12.refs_1_), channel_id=1, source_target_pairs={{0,1},{1,2},{2,3},{3,4},{4,5},{5,6},{6,7},{7,0},{16,23},{17,16},{1... | collective-permute-start | bytes 1204232 | tf_op jit(solution)/shard_map/ppermute | solution.py:456
  42.0 1.0 collective-permute-done.5.refs_0_
  43.1 0.0 copy-start.1
  43.1 3.2 %collective-permute-start.7 = (f32[2,392,128]{2,1,0:T(8,128)S(1)}, f32[2,392,128]{2,1,0:T(8,128)S(1)}, u32[]{:S(2)}, u32[]{:S(2)}) collective-permute-start(f32[2,392,128]{2,1,0:T(8,128)S(1)} %collect.13.before), channel_id=1, source_target_pairs={{0,1},{1,2},{2,3},{3,4},{4,5},{5,6},{6,7},{7,0},{16,23},{17,16},{1... | collective-permute-start | bytes 1204232 | tf_op jit(solution)/shard_map/ppermute | solution.py:456
  46.3 0.0 copy-done.6
  46.3 0.1 copy.11
  46.4 0.1 reduce
  46.6 0.0 copy-done.5
  46.6 0.1 select_reduce_fusion.2
  46.7 0.7 collective-permute-done.8.arrived.refs_2_
  47.4 2.8 %collective-permute-start.10 = (f32[392,128]{1,0:T(8,128)S(1)}, f32[392,128]{1,0:T(8,128)S(1)}, u32[]{:S(2)}, u32[]{:S(2)}) collective-permute-start(f32[392,128]{1,0:T(8,128)S(1)} %other_half.1), channel_id=1, source_target_pairs={{0,16},{16,0},{1,17},{17,1},{2,18},{18,2},{3,19},{19,3},{4,20},{20... | collective-permute-start | bytes 602120 | tf_op jit(solution)/shard_map/ppermute | solution.py:458
  50.2 1.5 %collective-permute-done.7.refs_1_ = f32[2,392,128]{2,1,0:T(8,128)S(1)} collective-permute-done((f32[2,392,128]{2,1,0:T(8,128)S(1)}, f32[2,392,128]{2,1,0:T(8,128)S(1)}, u32[]{:S(2)}, u32[]{:S(2)}) %collective-permute-start.7) | collective-permute-done | bytes 401440 | tf_op jit(solution)/shard_map/ppermute | solution.py:456
  51.7 3.4 %collective-permute-start.9 = (f32[392,128]{1,0:T(8,128)S(1)}, f32[392,128]{1,0:T(8,128)S(1)}, u32[]{:S(2)}, u32[]{:S(2)}) collective-permute-start(f32[392,128]{1,0:T(8,128)S(1)} %slice_bitcast_fusion), channel_id=1, source_target_pairs={{0,16},{16,0},{1,17},{17,1},{2,18},{18,2},{3,19},{19,3},{4,20},{20... | collective-permute-start | bytes 602120 | tf_op jit(solution)/shard_map/ppermute | solution.py:458
  55.0 0.1 select_reduce_fusion.1
  55.1 0.0 collective-permute-done.10.refs_4_
  55.1 1.0 collective-permute-done.9.refs_3_
  56.1 0.0 copy-done.1
  56.1 1.9 %mail.1 = f32[16,3,16,128]{3,2,1,0:T(8,128)} custom-call(f32[2,392,128]{2,1,0:T(8,128)S(1)} %copy-done.1, f32[2,392,128]{2,1,0:T(8,128)S(1)} %collective-permute-done.7.refs_1_, f32[2,392,128]{2,1,0:T(8,128)S(1)} %collective-permute-done.8.arrived.refs_2_, f32[392,128]{1,0:T(8,128)S(1)} %collective-permute-done.9.refs_3_, ...), custom_call_target="tpu_custom_call" | custom-call | tf_op jit(solution)/shard_map/mail/pallas_call | solution.py:296
  58.0 6.7 %all-to-all-start = ((f32[16,3,16,128]{3,2,1,0:T(8,128)}), f32[16,3,16,128]{3,2,1,0:T(8,128)S(1)}, u32[]{:S(2)}, u32[]{:S(2)}) async-start(f32[16,3,16,128]{3,2,1,0:T(8,128)} %mail.1), calls=%async_computation | async-start | bytes 786432 | tf_op jit(solution)/shard_map/all_to_all | solution.py:494
  64.8 0.1 direct.1
  64.8 1.6 %collective-permute-start.11 = (f32[24,16,128]{2,1,0:T(8,128)S(1)}, f32[24,16,128]{2,1,0:T(8,128)S(1)}, u32[]{:S(2)}, u32[]{:S(2)}) collective-permute-start(f32[24,16,128]{2,1,0:T(8,128)S(1)} %get-tuple-element.22), channel_id=1, source_target_pairs={{0,8},{8,0},{1,9},{9,1},{2,10},{10,2},{3,11},{11,3},{4,12},{12,4},... | collective-permute-start | bytes 589832 | tf_op jit(solution)/shard_map/ppermute | solution.py:493
  66.5 3.8 %reduce-precision_convert_fusion = (bf16[1,512,384]{2,1,0:T(8,128)(2,1)S(1)}, bf16[1,512,384]{2,1,0:T(8,128)(2,1)S(1)}) fusion(f32[512]{0:T(512)S(1)} %compare_select_fusion.2, s32[384]{0:T(512)S(1)} %add_select_fusion.1, s32[512]{0:T(512)S(1)} %fusion.25, pred[384]{0:T(512)(128)(4,1)S(1)} %fusion.11), kind=kLoop, calls=%fused_computation.2 | loop fusion | flops 3145728 | bytes 792448 | tf_op jit(solution)/shard_map/convert
  70.3 2.7 %collective-permute-done.11.got = f32[24,16,128]{2,1,0:T(8,128)S(1)} collective-permute-done((f32[24,16,128]{2,1,0:T(8,128)S(1)}, f32[24,16,128]{2,1,0:T(8,128)S(1)}, u32[]{:S(2)}, u32[]{:S(2)}) %collective-permute-start.11) | collective-permute-done | bytes 196640 | tf_op jit(solution)/shard_map/ppermute | solution.py:493
  73.0 2.8 %all-to-all-done.mail = f32[16,3,16,128]{3,2,1,0:T(8,128)S(1)} async-done(((f32[16,3,16,128]{3,2,1,0:T(8,128)}), f32[16,3,16,128]{3,2,1,0:T(8,128)S(1)}, u32[]{:S(2)}, u32[]{:S(2)}) %all-to-all-start) | async-done | bytes 393248 | tf_op jit(solution)/shard_map/all_to_all | solution.py:494
  75.8 1.0 join.1
  76.8 9.3 %all-to-all-start.1 = ((f32[16,24,256]{2,1,0:T(8,128)}), f32[16,24,256]{2,1,0:T(8,128)S(1)}, u32[]{:S(2)}, u32[]{:S(2)}) async-start(f32[16,24,256]{2,1,0:T(8,128)} %join.1), calls=%async_computation.1 | async-start | bytes 786432 | tf_op jit(solution)/shard_map/all_to_all | solution.py:496
  86.1 0.1 pad_maximum_fusion.basis
  86.2 0.1 fusion.6.relabel
  86.3 9.9 %all-to-all-done.1 = f32[16,24,256]{2,1,0:T(8,128)S(1)} async-done(((f32[16,24,256]{2,1,0:T(8,128)}), f32[16,24,256]{2,1,0:T(8,128)S(1)}, u32[]{:S(2)}, u32[]{:S(2)}) %all-to-all-start.1) | async-done | bytes 393248 | tf_op jit(solution)/shard_map/all_to_all | solution.py:496
  96.2 0.0 copy-start.7
  96.2 0.0 copy-start.3
  96.2 0.0 copy-start.4
  96.2 1.6 %transform.1 = f32[512,256]{1,0:T(8,128)} custom-call(bf16[2,512,384]{2,1,0:T(8,128)(2,1)S(1)} %pad_maximum_fusion.basis, f32[384,256]{1,0:T(8,128)S(1)} %bitcast.5, bf16[256,256]{1,0:T(8,128)(2,1)S(1)} %fusion.6.relabel), custom_call_target="tpu_custom_call" | custom-call | tf_op jit(solution)/shard_map/transform/pallas_call | solution.py:366
  97.8 4.1 %all-to-all-start.2 = ((f32[16,32,256]{2,1,0:T(8,128)}), f32[16,32,256]{2,1,0:T(8,128)S(1)}, u32[]{:S(2)}, u32[]{:S(2)}) async-start(f32[16,32,256]{2,1,0:T(8,128)} %bitcast.3), calls=%async_computation.2 | async-start | bytes 1048576 | tf_op jit(solution)/shard_map/all_to_all | solution.py:499
  101.9 0.0 copy-done.7
  101.9 0.1 select_reduce_fusion.3
  102.0 11.0 %all-to-all-done.2.traces = f32[16,32,256]{2,1,0:T(8,128)S(1)} async-done(((f32[16,32,256]{2,1,0:T(8,128)}), f32[16,32,256]{2,1,0:T(8,128)S(1)}, u32[]{:S(2)}, u32[]{:S(2)}) %all-to-all-start.2) | async-done | bytes 524320 | tf_op jit(solution)/shard_map/all_to_all | solution.py:499
  113.1 0.0 copy-done.3
  113.1 0.0 copy-done.4
  113.1 1.6 %update.1 = bf16[32,16,256]{2,1,0:T(8,128)(2,1)} custom-call(f32[32]{0:T(128)S(1)} %convert_element_type.24.events, s32[32]{0:T(128)S(1)} %compare_convert_fusion.inside, f32[16,32,256]{2,1,0:T(8,128)S(1)} %all-to-all-done.2.traces, bf16[32,16,256]{2,1,0:T(8,128)(2,1)S(1)} %copy-done.3, bf16[32,16,256]{2,1,0:T(8,128)(2,1)S(1)} %copy-done.4), custom_call_target="tpu_custom_call" | custom-call | tf_op jit(solution)/shard_map/update/pallas_call | solution.py:391
  (19 shorter events, 0.3 us)
Async XLA Ops:
  11.2 4.6 %collective-permute-start = (f32[1,392,128]{2,1,0:T(8,128)}, f32[1,392,128]{2,1,0:T(8,128)S(1)}, u32[]{:S(2)}, u32[]{:S(2)}) collective-permute-start(f32[1,392,128]{2,1,0:T(8,128)} %get-tuple-element.17), channel_id=1, source_target_pairs={{0,16},{16,0},{1,17},{17,1},{2,18},{18,2},{3,19},{19,3},{4,20},{20... | collective-permute-start | bytes 602120 | tf_op jit(solution)/shard_map/ppermute | solution.py:450
  15.8 0.9 copy-start.2
  16.7 4.3 %collective-permute-start.1 = (f32[6,392,128]{2,1,0:T(8,128)}, f32[6,392,128]{2,1,0:T(8,128)S(1)}, u32[]{:S(2)}, u32[]{:S(2)}) collective-permute-start(f32[6,392,128]{2,1,0:T(8,128)} %get-tuple-element.19), channel_id=1, source_target_pairs={{0,16},{16,0},{1,17},{17,1},{2,18},{18,2},{3,19},{19,3},{4,20},{20... | collective-permute-start | bytes 3612680 | tf_op jit(solution)/shard_map/ppermute | solution.py:452
  17.2 8.7 %collective-permute-start.2 = (f32[2,392,128]{2,1,0:T(8,128)S(1)}, f32[2,392,128]{2,1,0:T(8,128)S(1)}, u32[]{:S(2)}, u32[]{:S(2)}) collective-permute-start(f32[2,392,128]{2,1,0:T(8,128)S(1)} %collect.7.refs_0_), channel_id=1, source_target_pairs={{0,1},{1,2},{2,3},{3,4},{4,5},{5,6},{6,7},{7,0},{16,23},{17,16},{1... | collective-permute-start | bytes 1204232 | tf_op jit(solution)/shard_map/ppermute | solution.py:453
  21.1 1.3 %copy-start = (f32[6,392,128]{2,1,0:T(8,128)S(1)}, f32[6,392,128]{2,1,0:T(8,128)}, u32[]{:S(2)}) copy-start(f32[6,392,128]{2,1,0:T(8,128)} %get-tuple-element.15.keep) | copy-start | bytes 3612676
  22.4 7.8 %collective-permute-start.4 = (f32[2,392,128]{2,1,0:T(8,128)S(1)}, f32[2,392,128]{2,1,0:T(8,128)S(1)}, u32[]{:S(2)}, u32[]{:S(2)}) collective-permute-start(f32[2,392,128]{2,1,0:T(8,128)S(1)} %collect.8.refs_1_), channel_id=1, source_target_pairs={{0,1},{1,2},{2,3},{3,4},{4,5},{5,6},{6,7},{7,0},{16,23},{17,16},{1... | collective-permute-start | bytes 1204232 | tf_op jit(solution)/shard_map/ppermute | solution.py:456
  25.9 8.6 %collective-permute-start.3 = (f32[2,392,128]{2,1,0:T(8,128)S(1)}, f32[2,392,128]{2,1,0:T(8,128)S(1)}, u32[]{:S(2)}, u32[]{:S(2)}) collective-permute-start(f32[2,392,128]{2,1,0:T(8,128)S(1)} %collect.9.refs_1_), channel_id=1, source_target_pairs={{0,1},{1,2},{2,3},{3,4},{4,5},{5,6},{6,7},{7,0},{16,23},{17,16},{1... | collective-permute-start | bytes 1204232 | tf_op jit(solution)/shard_map/ppermute | solution.py:456
  30.2 8.5 %collective-permute-start.6 = (f32[2,392,128]{2,1,0:T(8,128)S(1)}, f32[2,392,128]{2,1,0:T(8,128)S(1)}, u32[]{:S(2)}, u32[]{:S(2)}) collective-permute-start(f32[2,392,128]{2,1,0:T(8,128)S(1)} %collect.10.refs_1_), channel_id=1, source_target_pairs={{0,1},{1,2},{2,3},{3,4},{4,5},{5,6},{6,7},{7,0},{16,23},{17,16},{1... | collective-permute-start | bytes 1204232 | tf_op jit(solution)/shard_map/ppermute | solution.py:456
  34.5 8.5 %collective-permute-start.5 = (f32[2,392,128]{2,1,0:T(8,128)S(1)}, f32[2,392,128]{2,1,0:T(8,128)S(1)}, u32[]{:S(2)}, u32[]{:S(2)}) collective-permute-start(f32[2,392,128]{2,1,0:T(8,128)S(1)} %collect.11.refs_1_), channel_id=1, source_target_pairs={{0,1},{1,2},{2,3},{3,4},{4,5},{5,6},{6,7},{7,0},{16,23},{17,16},{1... | collective-permute-start | bytes 1204232 | tf_op jit(solution)/shard_map/ppermute | solution.py:456
  38.8 7.5 %copy-start.6 = (s32[16]{0:T(128)S(1)}, s32[16]{0:T(128)}, u32[]{:S(2)}) copy-start(s32[16]{0:T(128)} %param.11) | copy-start | bytes 196
  38.8 7.8 %copy-start.5 = (s32[16]{0:T(128)S(1)}, s32[16]{0:T(128)}, u32[]{:S(2)}) copy-start(s32[16]{0:T(128)} %pairing.1) | copy-start | bytes 196
  38.8 8.5 %collective-permute-start.8 = (f32[2,392,128]{2,1,0:T(8,128)S(1)}, f32[2,392,128]{2,1,0:T(8,128)S(1)}, u32[]{:S(2)}, u32[]{:S(2)}) collective-permute-start(f32[2,392,128]{2,1,0:T(8,128)S(1)} %collect.12.refs_1_), channel_id=1, source_target_pairs={{0,1},{1,2},{2,3},{3,4},{4,5},{5,6},{6,7},{7,0},{16,23},{17,16},{1... | collective-permute-start | bytes 1204232 | tf_op jit(solution)/shard_map/ppermute | solution.py:456
  43.1 13.0 %copy-start.1 = (f32[2,392,128]{2,1,0:T(8,128)S(1)}, f32[2,392,128]{2,1,0:T(8,128)}, u32[]{:S(2)}) copy-start(f32[2,392,128]{2,1,0:T(8,128)} %get-tuple-element.14.refs_0_) | copy-start | bytes 1204228
  43.1 8.5 %collective-permute-start.7 = (f32[2,392,128]{2,1,0:T(8,128)S(1)}, f32[2,392,128]{2,1,0:T(8,128)S(1)}, u32[]{:S(2)}, u32[]{:S(2)}) collective-permute-start(f32[2,392,128]{2,1,0:T(8,128)S(1)} %collect.13.before), channel_id=1, source_target_pairs={{0,1},{1,2},{2,3},{3,4},{4,5},{5,6},{6,7},{7,0},{16,23},{17,16},{1... | collective-permute-start | bytes 1204232 | tf_op jit(solution)/shard_map/ppermute | solution.py:456
  47.4 7.7 %collective-permute-start.10 = (f32[392,128]{1,0:T(8,128)S(1)}, f32[392,128]{1,0:T(8,128)S(1)}, u32[]{:S(2)}, u32[]{:S(2)}) collective-permute-start(f32[392,128]{1,0:T(8,128)S(1)} %other_half.1), channel_id=1, source_target_pairs={{0,16},{16,0},{1,17},{17,1},{2,18},{18,2},{3,19},{19,3},{4,20},{20... | collective-permute-start | bytes 602120 | tf_op jit(solution)/shard_map/ppermute | solution.py:458
  51.7 4.4 %collective-permute-start.9 = (f32[392,128]{1,0:T(8,128)S(1)}, f32[392,128]{1,0:T(8,128)S(1)}, u32[]{:S(2)}, u32[]{:S(2)}) collective-permute-start(f32[392,128]{1,0:T(8,128)S(1)} %slice_bitcast_fusion), channel_id=1, source_target_pairs={{0,16},{16,0},{1,17},{17,1},{2,18},{18,2},{3,19},{19,3},{4,20},{20... | collective-permute-start | bytes 602120 | tf_op jit(solution)/shard_map/ppermute | solution.py:458
  58.0 17.8 %all-to-all-start = ((f32[16,3,16,128]{3,2,1,0:T(8,128)}), f32[16,3,16,128]{3,2,1,0:T(8,128)S(1)}, u32[]{:S(2)}, u32[]{:S(2)}) async-start(f32[16,3,16,128]{3,2,1,0:T(8,128)} %mail.1), calls=%async_computation | async-start | bytes 786432 | tf_op jit(solution)/shard_map/all_to_all | solution.py:494
  64.8 8.2 %collective-permute-start.11 = (f32[24,16,128]{2,1,0:T(8,128)S(1)}, f32[24,16,128]{2,1,0:T(8,128)S(1)}, u32[]{:S(2)}, u32[]{:S(2)}) collective-permute-start(f32[24,16,128]{2,1,0:T(8,128)S(1)} %get-tuple-element.22), channel_id=1, source_target_pairs={{0,8},{8,0},{1,9},{9,1},{2,10},{10,2},{3,11},{11,3},{4,12},{12,4},... | collective-permute-start | bytes 589832 | tf_op jit(solution)/shard_map/ppermute | solution.py:493
  76.8 19.3 %all-to-all-start.1 = ((f32[16,24,256]{2,1,0:T(8,128)}), f32[16,24,256]{2,1,0:T(8,128)S(1)}, u32[]{:S(2)}, u32[]{:S(2)}) async-start(f32[16,24,256]{2,1,0:T(8,128)} %join.1), calls=%async_computation.1 | async-start | bytes 786432 | tf_op jit(solution)/shard_map/all_to_all | solution.py:496
  96.2 5.7 %copy-start.7 = (s32[32]{0:T(128)S(1)}, s32[32]{0:T(128)}, u32[]{:S(2)}) copy-start(s32[32]{0:T(128)} %param.12) | copy-start | bytes 388
  96.2 16.9 %copy-start.3 = (bf16[32,16,256]{2,1,0:T(8,128)(2,1)S(1)}, bf16[32,16,256]{2,1,0:T(8,128)(2,1)}, u32[]{:S(2)}) copy-start(bf16[32,16,256]{2,1,0:T(8,128)(2,1)} %older.1) | copy-start | bytes 786436
  96.2 16.9 %copy-start.4 = (bf16[32,16,256]{2,1,0:T(8,128)(2,1)S(1)}, bf16[32,16,256]{2,1,0:T(8,128)(2,1)}, u32[]{:S(2)}) copy-start(bf16[32,16,256]{2,1,0:T(8,128)(2,1)} %data.1) | copy-start | bytes 786436
  97.8 15.3 %all-to-all-start.2 = ((f32[16,32,256]{2,1,0:T(8,128)}), f32[16,32,256]{2,1,0:T(8,128)S(1)}, u32[]{:S(2)}, u32[]{:S(2)}) async-start(f32[16,32,256]{2,1,0:T(8,128)} %bitcast.3), calls=%async_computation.2 | async-start | bytes 1048576 | tf_op jit(solution)/shard_map/all_to_all | solution.py:499

commit v3 on v2

--- a/solution.py
+++ b/solution.py
@@ -222,6 +222,10 @@
             if a & bit:
                 continue
             x, y = tiles[a], tiles[a | bit]
+            if bit == 4:
+                moved = pltpu.roll(jnp.where(upper, x, y), LANES // 2, 1)
+                out[a], out[a | bit] = jnp.where(upper, moved, x), jnp.where(upper, y, moved)
+                continue
             out[a] = jnp.where(upper, pltpu.roll(y, BLOCK * bit, 1), x)
             out[a | bit] = jnp.where(upper, y, pltpu.roll(x, LANES - BLOCK * bit, 1))
         tiles = out
@@ -237,7 +241,7 @@
 
 
 def direct_kernel(*refs):
-    keep, give = refs[5:]
+    keep, give = refs[6:]
     yl = lax.axis_index("yl")
     rows = keep.shape[0] // 2
     for half in range(2):
@@ -292,18 +296,18 @@
 def pack(rows, *sums):
     whole = pl.BlockSpec(memory_space=pltpu.VMEM)
 
-    def call(kernel, shapes, name):
+    def call(kernel, shapes, name, *before):
         return pl.pallas_call(
             kernel,
-            in_specs=[whole] * 5,
+            in_specs=[whole] * 5 + [pl.BlockSpec(memory_space=pl.ANY)] * len(before),
             out_specs=[whole] * len(shapes),
             out_shape=[jax.ShapeDtypeStruct(s, jnp.float32) for s in shapes],
             compiler_params=pltpu.CompilerParams(vmem_limit_bytes=SMALL_VMEM),
             name=name,
-        )(*sums)
-
-    keep, give = call(direct_kernel, [(rows, BLOCK, LANES)] * 2, "direct")
+        )(*sums, *before)
+
     (mail,) = call(mail_kernel, [(16, rows // 8, BLOCK, LANES)], "mail")
+    keep, give = call(direct_kernel, [(rows, BLOCK, LANES)] * 2, "direct", mail)
     return keep, give, mail
 
 
@@ -436,6 +440,27 @@
     )(arrived, before)
 
 
+def lift_kernel(source, out, sem):
+    copy = pltpu.make_async_copy(source, out, sem)
+    copy.start()
+    copy.wait()
+
+
+def lift(source):
+    return pl.pallas_call(
+        lift_kernel,
+        in_specs=[pl.BlockSpec(memory_space=pl.ANY)],
+        out_specs=pl.BlockSpec(memory_space=pltpu.VMEM),
+        out_shape=jax.ShapeDtypeStruct(source.shape, source.dtype),
+        scratch_shapes=[pltpu.SemaphoreType.DMA],
+        compiler_params=pltpu.CompilerParams(vmem_limit_bytes=SMALL_VMEM),
+        cost_estimate=pl.CostEstimate(
+            flops=0, bytes_accessed=8 * source.size, transcendentals=0
+        ),
+        name="lift",
+    )(source)
+
+
 def ring_sums(keep_first, keep, give_first, give):
     swap = functools.partial(lax.ppermute, axis_name="core", perm=ring(2, 1))
     step = functools.partial(
@@ -447,7 +472,7 @@
             for z in range(RING)
         ],
     )
-    payload = collect(0, keep_first, swap(give_first), keep_first)
+    payload = collect(0, lift(keep_first), swap(give_first), keep_first)
     payload, give = lax.optimization_barrier((payload, give))
     got = swap(give)
     flying = [step(payload)]

time: 115 us -> 114 us (level)
  local copies, waits for them, and re-layouts: 2.33 us -> 1.05 us
    unnamed x16, local copies, waits for them, and re-layouts: 2.24 us -> 0.96 us
    ppermute x1, waiting for transfers between devices: 0.7 us -> 1.98 us  [ring_sums(): flying = [step(payload)]]
    ppermute x1, waiting for transfers between devices: 1.29 us -> 0.12 us  [ring_sums(): payload = collect(0, lift(keep_first), swap(give_first), keep_first)]
  transfers between devices with their start and end apart: 15 -> 15, of which waited for: 13 -> 13; matrix products, arithmetic and copies ran while one was open for 4% -> 4% of each run, Pallas kernels for 0% -> 1%
where the time goes in v3:
time: 114 us
  starting transfers between devices  54.2 us (48%)
  waiting for transfers between devices  35.9 us (31%)
  Pallas kernels  17.9 us (16%)
  other arithmetic  4.53 us (4%)
    ppermute x6, starting transfers between devices, ring_sums(): flying = flying[-1:] + [step(payload)]  18.8 us
    pallas_call x1, Pallas kernels, product(): pl.pallas_call(product_kernel, in_specs=[smem, smem, anywhere, anywhere],...  11.2 us
    all_to_all x1, waiting for transfers between devices, on_device(): lax.all_to_all(slotted, freq, split_axis=0, concat_axis=0, tiled=True)  11 us
    all_to_all x1, waiting for transfers between devices, on_device(): lax.all_to_all(whole, freq, split_axis=0, concat_axis=0, tiled=True)  9.87 us
    all_to_all x1, starting transfers between devices, on_device(): lax.all_to_all(whole, freq, split_axis=0, concat_axis=0, tiled=True)  9.25 us
    all_to_all x1, starting transfers between devices, on_device(): mail = lax.all_to_all(mail, src, split_axis=0, concat_axis=0, tiled=True)  6.68 us
    ppermute x6, waiting for transfers between devices, ring_sums(): flying = flying[-1:] + [step(payload)]  6.37 us
    ppermute x2, starting transfers between devices, ring_sums(): return (late, early, swap(late[1]), swap(other_half(early, payload)))  6.13 us
  transfers between devices with their start and end apart: 15, of which 13 were waited for; matrix products, arithmetic and copies ran while one was open for 4% of the time, Pallas kernels for 1%

profile of v3, /device:TPU:1, one launch (start us, length us, event | category | flops | bytes accessed | tf_op | source)
XLA Modules:
  0.0 113.8 jit_solution(691657697056133494)
XLA Ops:
  0.0 11.2 %product.1 = (f32[1,392,128]{2,1,0:T(8,128)}, f32[6,392,128]{2,1,0:T(8,128)}, f32[1,392,128]{2,1,0:T(8,128)}, f32[6,392,128]{2,1,0:T(8,128)}, f32[2,392,128]{2,1,0:T(8,128)}) custom-call(s32[16]{0:T(128)} %pairing.1, f32[2,12]{1,0:T(2,128)} %ratio.1, bf16[12,2,256,512]{3,2,1,0:T(8,128)(2,1)} %spectra.1, bf16[12,2,512,256]{3,2,1,0:T(8,128)(2,1)} %primaries.1), custom_call_target="tpu_custom_call" | custom-call | flops 3221225472 | bytes 15794176 | tf_op jit(solution)/shard_map/product/pallas_call | solution.py:167
  11.2 0.0 copy-start
  11.2 3.3 %collective-permute-start = (f32[1,392,128]{2,1,0:T(8,128)}, f32[1,392,128]{2,1,0:T(8,128)S(1)}, u32[]{:S(2)}, u32[]{:S(2)}) collective-permute-start(f32[1,392,128]{2,1,0:T(8,128)} %get-tuple-element.17), channel_id=1, source_target_pairs={{0,16},{16,0},{1,17},{17,1},{2,18},{18,2},{3,19},{19,3},{4,20},{20... | collective-permute-start | bytes 602120 | tf_op jit(solution)/shard_map/ppermute | solution.py:475
  14.5 0.0 copy-start.2
  14.5 0.9 copy-done.2
  15.4 0.2 lift.1.keep
  15.7 0.1 collective-permute-done.got
  15.8 0.5 collective-permute-start.1
  16.3 3.9 %collective-permute-start.2 = (f32[2,392,128]{2,1,0:T(8,128)S(1)}, f32[2,392,128]{2,1,0:T(8,128)S(1)}, u32[]{:S(2)}, u32[]{:S(2)}) collective-permute-start(f32[2,392,128]{2,1,0:T(8,128)S(1)} %collect.7.refs_0_), channel_id=1, source_target_pairs={{0,1},{1,2},{2,3},{3,4},{4,5},{5,6},{6,7},{7,0},{16,23},{17,16},{1... | collective-permute-start | bytes 1204232 | tf_op jit(solution)/shard_map/ppermute | solution.py:478
  20.1 0.0 collective-permute-done.1.got
  20.1 0.0 copy-done
  20.2 2.8 %collective-permute-start.4 = (f32[2,392,128]{2,1,0:T(8,128)S(1)}, f32[2,392,128]{2,1,0:T(8,128)S(1)}, u32[]{:S(2)}, u32[]{:S(2)}) collective-permute-start(f32[2,392,128]{2,1,0:T(8,128)S(1)} %collect.8.refs_1_), channel_id=1, source_target_pairs={{0,1},{1,2},{2,3},{3,4},{4,5},{5,6},{6,7},{7,0},{16,23},{17,16},{1... | collective-permute-start | bytes 1204232 | tf_op jit(solution)/shard_map/ppermute | solution.py:481
  23.0 2.0 %collective-permute-done.2.refs_0_ = f32[2,392,128]{2,1,0:T(8,128)S(1)} collective-permute-done((f32[2,392,128]{2,1,0:T(8,128)S(1)}, f32[2,392,128]{2,1,0:T(8,128)S(1)}, u32[]{:S(2)}, u32[]{:S(2)}) %collective-permute-start.2) | collective-permute-done | bytes 401440 | tf_op jit(solution)/shard_map/ppermute | solution.py:478
  25.0 3.2 %collective-permute-start.3 = (f32[2,392,128]{2,1,0:T(8,128)S(1)}, f32[2,392,128]{2,1,0:T(8,128)S(1)}, u32[]{:S(2)}, u32[]{:S(2)}) collective-permute-start(f32[2,392,128]{2,1,0:T(8,128)S(1)} %collect.9.refs_1_), channel_id=1, source_target_pairs={{0,1},{1,2},{2,3},{3,4},{4,5},{5,6},{6,7},{7,0},{16,23},{17,16},{1... | collective-permute-start | bytes 1204232 | tf_op jit(solution)/shard_map/ppermute | solution.py:481
  28.2 1.1 collective-permute-done.4.refs_0_
  29.3 3.2 %collective-permute-start.6 = (f32[2,392,128]{2,1,0:T(8,128)S(1)}, f32[2,392,128]{2,1,0:T(8,128)S(1)}, u32[]{:S(2)}, u32[]{:S(2)}) collective-permute-start(f32[2,392,128]{2,1,0:T(8,128)S(1)} %collect.10.refs_1_), channel_id=1, source_target_pairs={{0,1},{1,2},{2,3},{3,4},{4,5},{5,6},{6,7},{7,0},{16,23},{17,16},{1... | collective-permute-start | bytes 1204232 | tf_op jit(solution)/shard_map/ppermute | solution.py:481
  32.5 1.1 collective-permute-done.3.refs_0_
  33.5 0.1 collect.11.refs_1_
  33.6 3.2 %collective-permute-start.5 = (f32[2,392,128]{2,1,0:T(8,128)S(1)}, f32[2,392,128]{2,1,0:T(8,128)S(1)}, u32[]{:S(2)}, u32[]{:S(2)}) collective-permute-start(f32[2,392,128]{2,1,0:T(8,128)S(1)} %collect.11.refs_1_), channel_id=1, source_target_pairs={{0,1},{1,2},{2,3},{3,4},{4,5},{5,6},{6,7},{7,0},{16,23},{17,16},{1... | collective-permute-start | bytes 1204232 | tf_op jit(solution)/shard_map/ppermute | solution.py:481
  36.8 1.0 collective-permute-done.6.refs_0_
  37.8 0.1 collect.12.refs_1_
  37.9 0.0 copy-start.6
  37.9 0.0 copy-start.5
  37.9 3.2 %collective-permute-start.8 = (f32[2,392,128]{2,1,0:T(8,128)S(1)}, f32[2,392,128]{2,1,0:T(8,128)S(1)}, u32[]{:S(2)}, u32[]{:S(2)}) collective-permute-start(f32[2,392,128]{2,1,0:T(8,128)S(1)} %collect.12.refs_1_), channel_id=1, source_target_pairs={{0,1},{1,2},{2,3},{3,4},{4,5},{5,6},{6,7},{7,0},{16,23},{17,16},{1... | collective-permute-start | bytes 1204232 | tf_op jit(solution)/shard_map/ppermute | solution.py:481
  41.1 1.0 collective-permute-done.5.refs_0_
  42.2 0.0 copy-start.1
  42.2 3.2 %collective-permute-start.7 = (f32[2,392,128]{2,1,0:T(8,128)S(1)}, f32[2,392,128]{2,1,0:T(8,128)S(1)}, u32[]{:S(2)}, u32[]{:S(2)}) collective-permute-start(f32[2,392,128]{2,1,0:T(8,128)S(1)} %collect.13.before), channel_id=1, source_target_pairs={{0,1},{1,2},{2,3},{3,4},{4,5},{5,6},{6,7},{7,0},{16,23},{17,16},{1... | collective-permute-start | bytes 1204232 | tf_op jit(solution)/shard_map/ppermute | solution.py:481
  45.4 0.0 copy-done.6
  45.4 0.1 copy.11
  45.5 0.1 reduce
  45.7 0.0 copy-done.5
  45.7 0.1 select_reduce_fusion.2
  45.8 0.7 collective-permute-done.8.arrived.refs_2_
  46.5 2.8 %collective-permute-start.10 = (f32[392,128]{1,0:T(8,128)S(1)}, f32[392,128]{1,0:T(8,128)S(1)}, u32[]{:S(2)}, u32[]{:S(2)}) collective-permute-start(f32[392,128]{1,0:T(8,128)S(1)} %other_half.1), channel_id=1, source_target_pairs={{0,16},{16,0},{1,17},{17,1},{2,18},{18,2},{3,19},{19,3},{4,20},{20... | collective-permute-start | bytes 602120 | tf_op jit(solution)/shard_map/ppermute | solution.py:483
  49.2 1.5 %collective-permute-done.7.refs_1_ = f32[2,392,128]{2,1,0:T(8,128)S(1)} collective-permute-done((f32[2,392,128]{2,1,0:T(8,128)S(1)}, f32[2,392,128]{2,1,0:T(8,128)S(1)}, u32[]{:S(2)}, u32[]{:S(2)}) %collective-permute-start.7) | collective-permute-done | bytes 401440 | tf_op jit(solution)/shard_map/ppermute | solution.py:481
  50.8 3.4 %collective-permute-start.9 = (f32[392,128]{1,0:T(8,128)S(1)}, f32[392,128]{1,0:T(8,128)S(1)}, u32[]{:S(2)}, u32[]{:S(2)}) collective-permute-start(f32[392,128]{1,0:T(8,128)S(1)} %slice_bitcast_fusion), channel_id=1, source_target_pairs={{0,16},{16,0},{1,17},{17,1},{2,18},{18,2},{3,19},{19,3},{4,20},{20... | collective-permute-start | bytes 602120 | tf_op jit(solution)/shard_map/ppermute | solution.py:483
  54.1 0.1 select_reduce_fusion.1
  54.2 0.0 collective-permute-done.10.refs_4_
  54.2 1.0 collective-permute-done.9.refs_3_
  55.2 0.0 copy-done.1
  55.2 1.9 %mail.1.refs_5_ = f32[16,3,16,128]{3,2,1,0:T(8,128)} custom-call(f32[2,392,128]{2,1,0:T(8,128)S(1)} %copy-done.1, f32[2,392,128]{2,1,0:T(8,128)S(1)} %collective-permute-done.7.refs_1_, f32[2,392,128]{2,1,0:T(8,128)S(1)} %collective-permute-done.8.arrived.refs_2_, f32[392,128]{1,0:T(8,128)S(1)} %collective-permute-done.9.refs_3_, ...), custom_call_target="tpu_custom_call" | custom-call | tf_op jit(solution)/shard_map/mail/pallas_call | solution.py:300
  57.1 6.7 %all-to-all-start = ((f32[16,3,16,128]{3,2,1,0:T(8,128)}), f32[16,3,16,128]{3,2,1,0:T(8,128)S(1)}, u32[]{:S(2)}, u32[]{:S(2)}) async-start(f32[16,3,16,128]{3,2,1,0:T(8,128)} %mail.1.refs_5_), calls=%async_computation | async-start | bytes 786432 | tf_op jit(solution)/shard_map/all_to_all | solution.py:519
  63.8 0.1 direct.1
  63.9 1.6 %collective-permute-start.11 = (f32[24,16,128]{2,1,0:T(8,128)S(1)}, f32[24,16,128]{2,1,0:T(8,128)S(1)}, u32[]{:S(2)}, u32[]{:S(2)}) collective-permute-start(f32[24,16,128]{2,1,0:T(8,128)S(1)} %get-tuple-element.22), channel_id=1, source_target_pairs={{0,8},{8,0},{1,9},{9,1},{2,10},{10,2},{3,11},{11,3},{4,12},{12,4},... | collective-permute-start | bytes 589832 | tf_op jit(solution)/shard_map/ppermute | solution.py:518
  65.5 3.8 %reduce-precision_convert_fusion = (bf16[1,512,384]{2,1,0:T(8,128)(2,1)S(1)}, bf16[1,512,384]{2,1,0:T(8,128)(2,1)S(1)}) fusion(f32[512]{0:T(512)S(1)} %compare_select_fusion.2, s32[384]{0:T(512)S(1)} %add_select_fusion.1, s32[512]{0:T(512)S(1)} %fusion.25, pred[384]{0:T(512)(128)(4,1)S(1)} %fusion.11), kind=kLoop, calls=%fused_computation.2 | loop fusion | flops 3145728 | bytes 792448 | tf_op jit(solution)/shard_map/convert
  69.4 2.7 %collective-permute-done.11.got = f32[24,16,128]{2,1,0:T(8,128)S(1)} collective-permute-done((f32[24,16,128]{2,1,0:T(8,128)S(1)}, f32[24,16,128]{2,1,0:T(8,128)S(1)}, u32[]{:S(2)}, u32[]{:S(2)}) %collective-permute-start.11) | collective-permute-done | bytes 196640 | tf_op jit(solution)/shard_map/ppermute | solution.py:518
  72.1 2.8 %all-to-all-done.mail = f32[16,3,16,128]{3,2,1,0:T(8,128)S(1)} async-done(((f32[16,3,16,128]{3,2,1,0:T(8,128)}), f32[16,3,16,128]{3,2,1,0:T(8,128)S(1)}, u32[]{:S(2)}, u32[]{:S(2)}) %all-to-all-start) | async-done | bytes 393248 | tf_op jit(solution)/shard_map/all_to_all | solution.py:519
  74.9 1.0 join.1
  75.9 9.3 %all-to-all-start.1 = ((f32[16,24,256]{2,1,0:T(8,128)}), f32[16,24,256]{2,1,0:T(8,128)S(1)}, u32[]{:S(2)}, u32[]{:S(2)}) async-start(f32[16,24,256]{2,1,0:T(8,128)} %join.1), calls=%async_computation.1 | async-start | bytes 786432 | tf_op jit(solution)/shard_map/all_to_all | solution.py:521
  85.1 0.1 pad_maximum_fusion.basis
  85.2 0.1 fusion.6.relabel
  85.4 9.9 %all-to-all-done.1 = f32[16,24,256]{2,1,0:T(8,128)S(1)} async-done(((f32[16,24,256]{2,1,0:T(8,128)}), f32[16,24,256]{2,1,0:T(8,128)S(1)}, u32[]{:S(2)}, u32[]{:S(2)}) %all-to-all-start.1) | async-done | bytes 393248 | tf_op jit(solution)/shard_map/all_to_all | solution.py:521
  95.2 0.0 copy-start.7
  95.2 0.0 copy-start.3
  95.2 0.0 copy-start.4
  95.2 1.6 %transform.1 = f32[512,256]{1,0:T(8,128)} custom-call(bf16[2,512,384]{2,1,0:T(8,128)(2,1)S(1)} %pad_maximum_fusion.basis, f32[384,256]{1,0:T(8,128)S(1)} %bitcast.5, bf16[256,256]{1,0:T(8,128)(2,1)S(1)} %fusion.6.relabel), custom_call_target="tpu_custom_call" | custom-call | tf_op jit(solution)/shard_map/transform/pallas_call | solution.py:370
  96.9 4.1 %all-to-all-start.2 = ((f32[16,32,256]{2,1,0:T(8,128)}), f32[16,32,256]{2,1,0:T(8,128)S(1)}, u32[]{:S(2)}, u32[]{:S(2)}) async-start(f32[16,32,256]{2,1,0:T(8,128)} %bitcast.3), calls=%async_computation.2 | async-start | bytes 1048576 | tf_op jit(solution)/shard_map/all_to_all | solution.py:524
  100.9 0.0 copy-done.7
  101.0 0.1 select_reduce_fusion.3
  101.1 11.0 %all-to-all-done.2.traces = f32[16,32,256]{2,1,0:T(8,128)S(1)} async-done(((f32[16,32,256]{2,1,0:T(8,128)}), f32[16,32,256]{2,1,0:T(8,128)S(1)}, u32[]{:S(2)}, u32[]{:S(2)}) %all-to-all-start.2) | async-done | bytes 524320 | tf_op jit(solution)/shard_map/all_to_all | solution.py:524
  112.1 0.0 copy-done.3
  112.1 0.0 copy-done.4
  112.1 1.6 %update.1 = bf16[32,16,256]{2,1,0:T(8,128)(2,1)} custom-call(f32[32]{0:T(128)S(1)} %convert_element_type.24.events, s32[32]{0:T(128)S(1)} %compare_convert_fusion.inside, f32[16,32,256]{2,1,0:T(8,128)S(1)} %all-to-all-done.2.traces, bf16[32,16,256]{2,1,0:T(8,128)(2,1)S(1)} %copy-done.3, bf16[32,16,256]{2,1,0:T(8,128)(2,1)S(1)} %copy-done.4), custom_call_target="tpu_custom_call" | custom-call | tf_op jit(solution)/shard_map/update/pallas_call | solution.py:395
  (19 shorter events, 0.3 us)
Async XLA Ops:
  11.2 9.0 %copy-start = (f32[6,392,128]{2,1,0:T(8,128)S(1)}, f32[6,392,128]{2,1,0:T(8,128)}, u32[]{:S(2)}) copy-start(f32[6,392,128]{2,1,0:T(8,128)} %get-tuple-element.15.keep) | copy-start | bytes 3612676
  11.2 4.6 %collective-permute-start = (f32[1,392,128]{2,1,0:T(8,128)}, f32[1,392,128]{2,1,0:T(8,128)S(1)}, u32[]{:S(2)}, u32[]{:S(2)}) collective-permute-start(f32[1,392,128]{2,1,0:T(8,128)} %get-tuple-element.17), channel_id=1, source_target_pairs={{0,16},{16,0},{1,17},{17,1},{2,18},{18,2},{3,19},{19,3},{4,20},{20... | collective-permute-start | bytes 602120 | tf_op jit(solution)/shard_map/ppermute | solution.py:475
  14.5 0.9 copy-start.2
  15.8 4.3 %collective-permute-start.1 = (f32[6,392,128]{2,1,0:T(8,128)}, f32[6,392,128]{2,1,0:T(8,128)S(1)}, u32[]{:S(2)}, u32[]{:S(2)}) collective-permute-start(f32[6,392,128]{2,1,0:T(8,128)} %get-tuple-element.19), channel_id=1, source_target_pairs={{0,16},{16,0},{1,17},{17,1},{2,18},{18,2},{3,19},{19,3},{4,20},{20... | collective-permute-start | bytes 3612680 | tf_op jit(solution)/shard_map/ppermute | solution.py:477
  16.3 8.7 %collective-permute-start.2 = (f32[2,392,128]{2,1,0:T(8,128)S(1)}, f32[2,392,128]{2,1,0:T(8,128)S(1)}, u32[]{:S(2)}, u32[]{:S(2)}) collective-permute-start(f32[2,392,128]{2,1,0:T(8,128)S(1)} %collect.7.refs_0_), channel_id=1, source_target_pairs={{0,1},{1,2},{2,3},{3,4},{4,5},{5,6},{6,7},{7,0},{16,23},{17,16},{1... | collective-permute-start | bytes 1204232 | tf_op jit(solution)/shard_map/ppermute | solution.py:478
  20.2 9.1 %collective-permute-start.4 = (f32[2,392,128]{2,1,0:T(8,128)S(1)}, f32[2,392,128]{2,1,0:T(8,128)S(1)}, u32[]{:S(2)}, u32[]{:S(2)}) collective-permute-start(f32[2,392,128]{2,1,0:T(8,128)S(1)} %collect.8.refs_1_), channel_id=1, source_target_pairs={{0,1},{1,2},{2,3},{3,4},{4,5},{5,6},{6,7},{7,0},{16,23},{17,16},{1... | collective-permute-start | bytes 1204232 | tf_op jit(solution)/shard_map/ppermute | solution.py:481
  25.0 8.6 %collective-permute-start.3 = (f32[2,392,128]{2,1,0:T(8,128)S(1)}, f32[2,392,128]{2,1,0:T(8,128)S(1)}, u32[]{:S(2)}, u32[]{:S(2)}) collective-permute-start(f32[2,392,128]{2,1,0:T(8,128)S(1)} %collect.9.refs_1_), channel_id=1, source_target_pairs={{0,1},{1,2},{2,3},{3,4},{4,5},{5,6},{6,7},{7,0},{16,23},{17,16},{1... | collective-permute-start | bytes 1204232 | tf_op jit(solution)/shard_map/ppermute | solution.py:481
  29.3 8.6 %collective-permute-start.6 = (f32[2,392,128]{2,1,0:T(8,128)S(1)}, f32[2,392,128]{2,1,0:T(8,128)S(1)}, u32[]{:S(2)}, u32[]{:S(2)}) collective-permute-start(f32[2,392,128]{2,1,0:T(8,128)S(1)} %collect.10.refs_1_), channel_id=1, source_target_pairs={{0,1},{1,2},{2,3},{3,4},{4,5},{5,6},{6,7},{7,0},{16,23},{17,16},{1... | collective-permute-start | bytes 1204232 | tf_op jit(solution)/shard_map/ppermute | solution.py:481
  33.6 8.5 %collective-permute-start.5 = (f32[2,392,128]{2,1,0:T(8,128)S(1)}, f32[2,392,128]{2,1,0:T(8,128)S(1)}, u32[]{:S(2)}, u32[]{:S(2)}) collective-permute-start(f32[2,392,128]{2,1,0:T(8,128)S(1)} %collect.11.refs_1_), channel_id=1, source_target_pairs={{0,1},{1,2},{2,3},{3,4},{4,5},{5,6},{6,7},{7,0},{16,23},{17,16},{1... | collective-permute-start | bytes 1204232 | tf_op jit(solution)/shard_map/ppermute | solution.py:481
  37.9 7.5 %copy-start.6 = (s32[16]{0:T(128)S(1)}, s32[16]{0:T(128)}, u32[]{:S(2)}) copy-start(s32[16]{0:T(128)} %param.11) | copy-start | bytes 196
  37.9 7.8 %copy-start.5 = (s32[16]{0:T(128)S(1)}, s32[16]{0:T(128)}, u32[]{:S(2)}) copy-start(s32[16]{0:T(128)} %pairing.1) | copy-start | bytes 196
  37.9 8.5 %collective-permute-start.8 = (f32[2,392,128]{2,1,0:T(8,128)S(1)}, f32[2,392,128]{2,1,0:T(8,128)S(1)}, u32[]{:S(2)}, u32[]{:S(2)}) collective-permute-start(f32[2,392,128]{2,1,0:T(8,128)S(1)} %collect.12.refs_1_), channel_id=1, source_target_pairs={{0,1},{1,2},{2,3},{3,4},{4,5},{5,6},{6,7},{7,0},{16,23},{17,16},{1... | collective-permute-start | bytes 1204232 | tf_op jit(solution)/shard_map/ppermute | solution.py:481
  42.2 13.0 %copy-start.1 = (f32[2,392,128]{2,1,0:T(8,128)S(1)}, f32[2,392,128]{2,1,0:T(8,128)}, u32[]{:S(2)}) copy-start(f32[2,392,128]{2,1,0:T(8,128)} %get-tuple-element.14.refs_0_) | copy-start | bytes 1204228
  42.2 8.5 %collective-permute-start.7 = (f32[2,392,128]{2,1,0:T(8,128)S(1)}, f32[2,392,128]{2,1,0:T(8,128)S(1)}, u32[]{:S(2)}, u32[]{:S(2)}) collective-permute-start(f32[2,392,128]{2,1,0:T(8,128)S(1)} %collect.13.before), channel_id=1, source_target_pairs={{0,1},{1,2},{2,3},{3,4},{4,5},{5,6},{6,7},{7,0},{16,23},{17,16},{1... | collective-permute-start | bytes 1204232 | tf_op jit(solution)/shard_map/ppermute | solution.py:481
  46.5 7.8 %collective-permute-start.10 = (f32[392,128]{1,0:T(8,128)S(1)}, f32[392,128]{1,0:T(8,128)S(1)}, u32[]{:S(2)}, u32[]{:S(2)}) collective-permute-start(f32[392,128]{1,0:T(8,128)S(1)} %other_half.1), channel_id=1, source_target_pairs={{0,16},{16,0},{1,17},{17,1},{2,18},{18,2},{3,19},{19,3},{4,20},{20... | collective-permute-start | bytes 602120 | tf_op jit(solution)/shard_map/ppermute | solution.py:483
  50.8 4.4 %collective-permute-start.9 = (f32[392,128]{1,0:T(8,128)S(1)}, f32[392,128]{1,0:T(8,128)S(1)}, u32[]{:S(2)}, u32[]{:S(2)}) collective-permute-start(f32[392,128]{1,0:T(8,128)S(1)} %slice_bitcast_fusion), channel_id=1, source_target_pairs={{0,16},{16,0},{1,17},{17,1},{2,18},{18,2},{3,19},{19,3},{4,20},{20... | collective-permute-start | bytes 602120 | tf_op jit(solution)/shard_map/ppermute | solution.py:483
  57.1 17.8 %all-to-all-start = ((f32[16,3,16,128]{3,2,1,0:T(8,128)}), f32[16,3,16,128]{3,2,1,0:T(8,128)S(1)}, u32[]{:S(2)}, u32[]{:S(2)}) async-start(f32[16,3,16,128]{3,2,1,0:T(8,128)} %mail.1.refs_5_), calls=%async_computation | async-start | bytes 786432 | tf_op jit(solution)/shard_map/all_to_all | solution.py:519
  63.9 8.2 %collective-permute-start.11 = (f32[24,16,128]{2,1,0:T(8,128)S(1)}, f32[24,16,128]{2,1,0:T(8,128)S(1)}, u32[]{:S(2)}, u32[]{:S(2)}) collective-permute-start(f32[24,16,128]{2,1,0:T(8,128)S(1)} %get-tuple-element.22), channel_id=1, source_target_pairs={{0,8},{8,0},{1,9},{9,1},{2,10},{10,2},{3,11},{11,3},{4,12},{12,4},... | collective-permute-start | bytes 589832 | tf_op jit(solution)/shard_map/ppermute | solution.py:518
  75.9 19.3 %all-to-all-start.1 = ((f32[16,24,256]{2,1,0:T(8,128)}), f32[16,24,256]{2,1,0:T(8,128)S(1)}, u32[]{:S(2)}, u32[]{:S(2)}) async-start(f32[16,24,256]{2,1,0:T(8,128)} %join.1), calls=%async_computation.1 | async-start | bytes 786432 | tf_op jit(solution)/shard_map/all_to_all | solution.py:521
  95.2 5.7 %copy-start.7 = (s32[32]{0:T(128)S(1)}, s32[32]{0:T(128)}, u32[]{:S(2)}) copy-start(s32[32]{0:T(128)} %param.12) | copy-start | bytes 388
  95.2 16.9 %copy-start.3 = (bf16[32,16,256]{2,1,0:T(8,128)(2,1)S(1)}, bf16[32,16,256]{2,1,0:T(8,128)(2,1)}, u32[]{:S(2)}) copy-start(bf16[32,16,256]{2,1,0:T(8,128)(2,1)} %older.1) | copy-start | bytes 786436
  95.2 16.9 %copy-start.4 = (bf16[32,16,256]{2,1,0:T(8,128)(2,1)S(1)}, bf16[32,16,256]{2,1,0:T(8,128)(2,1)}, u32[]{:S(2)}) copy-start(bf16[32,16,256]{2,1,0:T(8,128)(2,1)} %data.1) | copy-start | bytes 786436
  96.9 15.3 %all-to-all-start.2 = ((f32[16,32,256]{2,1,0:T(8,128)}), f32[16,32,256]{2,1,0:T(8,128)S(1)}, u32[]{:S(2)}, u32[]{:S(2)}) async-start(f32[16,32,256]{2,1,0:T(8,128)} %bitcast.3), calls=%async_computation.2 | async-start | bytes 1048576 | tf_op jit(solution)/shard_map/all_to_all | solution.py:524

commit v4 on v3

--- a/solution.py
+++ b/solution.py
@@ -192,22 +192,26 @@
     )(pairing, ratio, spectra, primaries)
 
 
-def collect_kernel(keep, got, *refs):
-    arrived, out = refs[:-2], refs[-1]
+def collect_kernel(arrivals, keep, got, *refs):
+    arrived, outs = refs[:arrivals], refs[arrivals + 1 :]
+    outs = outs if len(outs) == 2 else (outs[0].at[pl.ds(0, 1)], outs[0].at[pl.ds(1, 1)])
     for i, part in enumerate((keep, got)):
-        out[i] = arrived[0][i] + part[0] if arrived else part[0]
-
-
-def collect(index, keep, got, before, *arrived):
+        outs[i][0] = arrived[0][i] + part[0] if arrived else part[0]
+
+
+def collect(index, keep, got, before, *arrived, split=False):
     shape = (2,) + keep.shape[1:]
     one = pl.BlockSpec((1,) + shape[1:], lambda i: (index, 0, 0))
     whole = pl.BlockSpec(shape, lambda i: (0, 0, 0))
-    return pl.pallas_call(
-        collect_kernel,
+    half = pl.BlockSpec((1,) + shape[1:], lambda i: (0, 0, 0))
+    return pl.pallas_call(
+        functools.partial(collect_kernel, len(arrived)),
         grid=(1,),
         in_specs=[one, one] + [whole] * len(arrived) + [pl.BlockSpec(memory_space=pl.ANY)],
-        out_specs=whole,
-        out_shape=jax.ShapeDtypeStruct(shape, jnp.float32),
+        out_specs=[half, half] if split else whole,
+        out_shape=[jax.ShapeDtypeStruct((1,) + shape[1:], jnp.float32)] * 2
+        if split
+        else jax.ShapeDtypeStruct(shape, jnp.float32),
         compiler_params=pltpu.CompilerParams(vmem_limit_bytes=SMALL_VMEM),
         name="collect",
     )(keep, got, *arrived, before)
@@ -251,18 +255,6 @@
                 dst[rows * half + a] = ring_total(refs[:5], half, start)
 
 
-def turn_blocks(x):
-    turned = x.T
-    out = jnp.zeros(x.shape, x.dtype)
-    for a in range(8):
-        block = jnp.concatenate(
-            [turned[BLOCK * a : BLOCK * (a + 1)], jnp.zeros((BLOCK, LANES - BLOCK), x.dtype)],
-            axis=1,
-        )
-        out = out + (pltpu.roll(block, BLOCK * a, 1) if a else block)
-    return out
-
-
 def mail_kernel(*refs):
     mail = refs[5]
     zi = lax.axis_index("z")
@@ -287,10 +279,8 @@
             if rows * half < 8 * g + 8 and rows * (half + 1) > 8 * g:
                 place = 2 * rows * BLOCK + g - rows * half // 8
                 middle = middle + ring_total(refs[:5], half, place, 1)
-        for at, below, above in ((8, firsts[0], firsts[1]), (0, firsts[1], firsts[0])):
-            mail[zi + at, g] = jnp.where(
-                across < down, below, jnp.where(across == down, middle, turn_blocks(above))
-            )
+        for at, below in ((8, firsts[0]), (0, firsts[1])):
+            mail[zi + at, g] = jnp.where(across == down, middle, below)
 
 
 def pack(rows, *sums):
@@ -328,18 +318,16 @@
         for a in range(1, 8):
             packed = packed + pltpu.roll(jnp.where(lane < BLOCK, tiles[a], 0.0), BLOCK * a, 1)
         upper = packed.T
-        direct = jnp.stack(
-            [
-                jnp.where(
-                    lane < level,
-                    jnp.concatenate([upper[BLOCK * a : BLOCK * (a + 1)], rest], axis=1),
-                    tiles[a],
-                )
-                for a in range(8)
-            ]
-        )
-        out[:, 8 * g : 8 * g + 8, :LANES] = jnp.swapaxes(direct, 0, 1)
-        out[:, 8 * g : 8 * g + 8, LANES:] = jnp.swapaxes(turned, 0, 1)
+        own = lane < level
+        direct = [
+            jnp.where(
+                own, jnp.concatenate([upper[BLOCK * a : BLOCK * (a + 1)], rest], axis=1), tiles[a]
+            )
+            for a in range(8)
+        ]
+        mirrored = [jnp.where(own, tiles[a], turned[a]) for a in range(8)]
+        out[:, 8 * g : 8 * g + 8, :LANES] = jnp.swapaxes(jnp.stack(direct), 0, 1)
+        out[:, 8 * g : 8 * g + 8, LANES:] = jnp.swapaxes(jnp.stack(mirrored), 0, 1)
 
 
 def join(keep, got, mail):
@@ -472,15 +460,24 @@
             for z in range(RING)
         ],
     )
+    cross = functools.partial(
+        lax.ppermute,
+        axis_name=("core", "z"),
+        perm=[
+            (c * RING + z, (1 - c) * RING + (z + (1 if c == 0 else -1)) % RING)
+            for c in range(2)
+            for z in range(RING)
+        ],
+    )
     payload = collect(0, lift(keep_first), swap(give_first), keep_first)
     payload, give = lax.optimization_barrier((payload, give))
     got = swap(give)
     flying = [step(payload)]
-    for n in range(6):
+    for n in range(5):
         payload = collect(n, keep, got, payload, *flying[:-1])
         flying = flying[-1:] + [step(payload)]
-    early, late = flying
-    return late, early, swap(late[1]), swap(other_half(early, payload))
+    mine, other = collect(5, keep, got, payload, flying[0], split=True)
+    return step(mine), flying[1], cross(other)[0], swap(other_half(flying[1], other))
 
 
 def on_device(

time: 114 us -> 112 us (0.982)
  starting transfers between devices: 54.2 us -> 50.8 us
  Pallas kernels: 17.9 us -> 19.8 us
    ppermute x6 -> x5, waiting for transfers between devices: 6.37 us -> 2.93 us  [ring_sums(): flying = flying[-1:] + [step(payload)]]
    ppermute x6 -> x5, starting transfers between devices: 18.8 us -> 15.4 us  [ring_sums(): flying = flying[-1:] + [step(payload)]]
    ppermute x2 -> x3, waiting for transfers between devices: 0.98 us -> 3.63 us  [the longest x1 2.36 us: ring_sums(): step(mine)]
    pallas_call x7, Pallas kernels: 0.31 us -> 2.8 us  [collect(): pl.pallas_call(functools.partial(collect_kernel, len(arrived)), grid=(1,)...]
    ppermute x2 -> x3, starting transfers between devices: 6.13 us -> 6.44 us  [the longest x1 3.1 us: ring_sums(): cross(other)[0]]
  transfers between devices with their start and end apart: 15 -> 15, of which waited for: 13 -> 12; matrix products, arithmetic and copies ran while one was open for 4% -> 4% of each run, Pallas kernels for 1% -> 3%
where the time goes in v4:
time: 112 us
  starting transfers between devices  50.8 us (45%)
  waiting for transfers between devices  35.1 us (31%)
  Pallas kernels  19.8 us (18%)
  other arithmetic  4.53 us (4%)
    ppermute x5, starting transfers between devices, ring_sums(): flying = flying[-1:] + [step(payload)]  15.4 us
    pallas_call x1, Pallas kernels, product(): pl.pallas_call(product_kernel, in_specs=[smem, smem, anywhere, anywhere],...  11.1 us
    all_to_all x1, waiting for transfers between devices, on_device(): lax.all_to_all(slotted, freq, split_axis=0, concat_axis=0, tiled=True)  11 us
    all_to_all x1, waiting for transfers between devices, on_device(): lax.all_to_all(whole, freq, split_axis=0, concat_axis=0, tiled=True)  9.87 us
    all_to_all x1, starting transfers between devices, on_device(): lax.all_to_all(whole, freq, split_axis=0, concat_axis=0, tiled=True)  8.95 us
    all_to_all x1, starting transfers between devices, on_device(): mail = lax.all_to_all(mail, src, split_axis=0, concat_axis=0, tiled=True)  6.68 us
    all_to_all x1, starting transfers between devices, on_device(): lax.all_to_all(slotted, freq, split_axis=0, concat_axis=0, tiled=True)  4.09 us
    another operation x3, other arithmetic  4 us
  transfers between devices with their start and end apart: 15, of which 12 were waited for; matrix products, arithmetic and copies ran while one was open for 4% of the time, Pallas kernels for 3%

profile of v4, /device:TPU:1, one launch (start us, length us, event | category | flops | bytes accessed | tf_op | source)
XLA Modules:
  0.0 111.5 jit_solution(7784359606576507996)
XLA Ops:
  0.0 11.1 %product.1 = (f32[1,392,128]{2,1,0:T(8,128)}, f32[6,392,128]{2,1,0:T(8,128)}, f32[1,392,128]{2,1,0:T(8,128)}, f32[6,392,128]{2,1,0:T(8,128)}, f32[2,392,128]{2,1,0:T(8,128)}) custom-call(s32[16]{0:T(128)} %pairing.1, f32[2,12]{1,0:T(2,128)} %ratio.1, bf16[12,2,256,512]{3,2,1,0:T(8,128)(2,1)} %spectra.1, bf16[12,2,512,256]{3,2,1,0:T(8,128)(2,1)} %primaries.1), custom_call_target="tpu_custom_call" | custom-call | flops 3221225472 | bytes 15794176 | tf_op jit(solution)/shard_map/product/pallas_call | solution.py:167
  11.1 0.0 copy-start
  11.1 3.3 %collective-permute-start = (f32[1,392,128]{2,1,0:T(8,128)}, f32[1,392,128]{2,1,0:T(8,128)S(1)}, u32[]{:S(2)}, u32[]{:S(2)}) collective-permute-start(f32[1,392,128]{2,1,0:T(8,128)} %get-tuple-element.19), channel_id=1, source_target_pairs={{0,16},{16,0},{1,17},{17,1},{2,18},{18,2},{3,19},{19,3},{4,20},{20... | collective-permute-start | bytes 602120 | tf_op jit(solution)/shard_map/ppermute | solution.py:472
  14.5 0.0 copy-start.2
  14.5 0.9 copy-done.2
  15.4 0.2 lift.1.keep
  15.6 0.1 collective-permute-done.got
  15.8 0.5 collective-permute-start.1
  16.2 3.9 %collective-permute-start.2 = (f32[2,392,128]{2,1,0:T(8,128)S(1)}, f32[2,392,128]{2,1,0:T(8,128)S(1)}, u32[]{:S(2)}, u32[]{:S(2)}) collective-permute-start(f32[2,392,128]{2,1,0:T(8,128)S(1)} %collect.7.refs_0_), channel_id=1, source_target_pairs={{0,1},{1,2},{2,3},{3,4},{4,5},{5,6},{6,7},{7,0},{16,23},{17,16},{1... | collective-permute-start | bytes 1204232 | tf_op jit(solution)/shard_map/ppermute | solution.py:475
  20.1 0.0 collective-permute-done.1.got
  20.1 0.0 copy-done
  20.1 2.8 %collective-permute-start.4 = (f32[2,392,128]{2,1,0:T(8,128)S(1)}, f32[2,392,128]{2,1,0:T(8,128)S(1)}, u32[]{:S(2)}, u32[]{:S(2)}) collective-permute-start(f32[2,392,128]{2,1,0:T(8,128)S(1)} %collect.8.refs_1_), channel_id=1, source_target_pairs={{0,1},{1,2},{2,3},{3,4},{4,5},{5,6},{6,7},{7,0},{16,23},{17,16},{1... | collective-permute-start | bytes 1204232 | tf_op jit(solution)/shard_map/ppermute | solution.py:478
  22.9 2.0 %collective-permute-done.2.refs_0_ = f32[2,392,128]{2,1,0:T(8,128)S(1)} collective-permute-done((f32[2,392,128]{2,1,0:T(8,128)S(1)}, f32[2,392,128]{2,1,0:T(8,128)S(1)}, u32[]{:S(2)}, u32[]{:S(2)}) %collective-permute-start.2) | collective-permute-done | bytes 401440 | tf_op jit(solution)/shard_map/ppermute | solution.py:475
  25.0 3.2 %collective-permute-start.3 = (f32[2,392,128]{2,1,0:T(8,128)S(1)}, f32[2,392,128]{2,1,0:T(8,128)S(1)}, u32[]{:S(2)}, u32[]{:S(2)}) collective-permute-start(f32[2,392,128]{2,1,0:T(8,128)S(1)} %collect.9.refs_1_), channel_id=1, source_target_pairs={{0,1},{1,2},{2,3},{3,4},{4,5},{5,6},{6,7},{7,0},{16,23},{17,16},{1... | collective-permute-start | bytes 1204232 | tf_op jit(solution)/shard_map/ppermute | solution.py:478
  28.1 1.1 collective-permute-done.4.refs_0_
  29.2 0.1 collect.10.refs_1_
  29.3 3.2 %collective-permute-start.6 = (f32[2,392,128]{2,1,0:T(8,128)S(1)}, f32[2,392,128]{2,1,0:T(8,128)S(1)}, u32[]{:S(2)}, u32[]{:S(2)}) collective-permute-start(f32[2,392,128]{2,1,0:T(8,128)S(1)} %collect.10.refs_1_), channel_id=1, source_target_pairs={{0,1},{1,2},{2,3},{3,4},{4,5},{5,6},{6,7},{7,0},{16,23},{17,16},{1... | collective-permute-start | bytes 1204232 | tf_op jit(solution)/shard_map/ppermute | solution.py:478
  32.5 1.0 collective-permute-done.3.refs_0_
  33.5 0.8 collect.11.refs_1_
  34.3 0.0 copy-start.6
  34.3 0.0 copy-start.5
  34.3 3.1 %collective-permute-start.5 = (f32[2,392,128]{2,1,0:T(8,128)}, f32[2,392,128]{2,1,0:T(8,128)}, u32[]{:S(2)}, u32[]{:S(2)}) collective-permute-start(f32[2,392,128]{2,1,0:T(8,128)} %collect.11.refs_1_), channel_id=1, source_target_pairs={{0,1},{1,2},{2,3},{3,4},{4,5},{5,6},{6,7},{7,0},{16,23},{17,16},{1... | collective-permute-start | bytes 1204232 | tf_op jit(solution)/shard_map/ppermute | solution.py:478
  37.4 0.4 collective-permute-done.6.refs_0_
  37.8 0.8 collect.12.refs_1_
  38.6 3.1 %collective-permute-start.8 = (f32[2,392,128]{2,1,0:T(8,128)}, f32[2,392,128]{2,1,0:T(8,128)S(1)}, u32[]{:S(2)}, u32[]{:S(2)}) collective-permute-start(f32[2,392,128]{2,1,0:T(8,128)} %collect.12.refs_1_), channel_id=1, source_target_pairs={{0,1},{1,2},{2,3},{3,4},{4,5},{5,6},{6,7},{7,0},{16,23},{17,16},{1... | collective-permute-start | bytes 1204232 | tf_op jit(solution)/shard_map/ppermute | solution.py:478
  41.7 0.0 copy-done.6
  41.7 0.1 copy.11
  41.8 0.1 reduce
  42.0 0.0 copy-done.5
  42.0 0.1 select_reduce_fusion.2
  42.1 0.0 copy-start.1
  42.1 0.4 collective-permute-done.5.refs_0_
  42.5 1.0 collect.13
  43.6 3.1 %collective-permute-start.9 = (f32[1,392,128]{2,1,0:T(8,128)S(1)}, f32[1,392,128]{2,1,0:T(8,128)S(1)}, u32[]{:S(2)}, u32[]{:S(2)}) collective-permute-start(f32[1,392,128]{2,1,0:T(8,128)S(1)} %get-tuple-element.24.before), channel_id=1, source_target_pairs={{0,17},{1,18},{2,19},{3,20},{4,21},{5,22},{6,23},{7,16},{16,7},{17... | collective-permute-start | bytes 602120 | tf_op jit(solution)/shard_map/ppermute | solution.py:480
  46.7 0.7 collective-permute-start.7
  47.4 0.0 collective-permute-done.8.arrived.refs_2_
  47.4 2.6 %collective-permute-start.10 = (f32[392,128]{1,0:T(8,128)S(1)}, f32[392,128]{1,0:T(8,128)S(1)}, u32[]{:S(2)}, u32[]{:S(2)}) collective-permute-start(f32[392,128]{1,0:T(8,128)S(1)} %other_half.1), channel_id=1, source_target_pairs={{0,16},{16,0},{1,17},{17,1},{2,18},{18,2},{3,19},{19,3},{4,20},{20... | collective-permute-start | bytes 602120 | tf_op jit(solution)/shard_map/ppermute | solution.py:480
  50.1 0.1 select_reduce_fusion.1
  50.2 1.3 %collective-permute-done.9 = f32[1,392,128]{2,1,0:T(8,128)S(1)} collective-permute-done((f32[1,392,128]{2,1,0:T(8,128)S(1)}, f32[1,392,128]{2,1,0:T(8,128)S(1)}, u32[]{:S(2)}, u32[]{:S(2)}) %collective-permute-start.9) | collective-permute-done | bytes 200736 | tf_op jit(solution)/shard_map/ppermute | solution.py:480
  51.4 2.4 %collective-permute-done.7.refs_1_ = f32[1,392,128]{2,1,0:T(8,128)S(1)} collective-permute-done((f32[1,392,128]{2,1,0:T(8,128)S(1)}, f32[1,392,128]{2,1,0:T(8,128)S(1)}, u32[]{:S(2)}, u32[]{:S(2)}) %collective-permute-start.7) | collective-permute-done | bytes 200736 | tf_op jit(solution)/shard_map/ppermute | solution.py:480
  53.8 0.0 collective-permute-done.10.refs_4_
  53.8 0.0 copy-done.1
  53.8 1.3 %mail.1.refs_5_ = f32[16,3,16,128]{3,2,1,0:T(8,128)} custom-call(f32[2,392,128]{2,1,0:T(8,128)S(1)} %copy-done.1, f32[1,392,128]{2,1,0:T(8,128)S(1)} %collective-permute-done.7.refs_1_, f32[2,392,128]{2,1,0:T(8,128)S(1)} %collective-permute-done.8.arrived.refs_2_, f32[392,128]{1,0:T(8,128)S(1)} %bitcast.5, f32[392,128]{1,0:T(8,128)S(1)} %collective-permute-done.10.refs_4_), custom_call_target="tpu_custom_call" | custom-call | tf_op jit(solution)/shard_map/mail/pallas_call | solution.py:290
  55.1 6.7 %all-to-all-start = ((f32[16,3,16,128]{3,2,1,0:T(8,128)}), f32[16,3,16,128]{3,2,1,0:T(8,128)S(1)}, u32[]{:S(2)}, u32[]{:S(2)}) async-start(f32[16,3,16,128]{3,2,1,0:T(8,128)} %mail.1.refs_5_), calls=%async_computation | async-start | bytes 786432 | tf_op jit(solution)/shard_map/all_to_all | solution.py:516
  61.8 0.1 direct.1
  61.9 1.6 %collective-permute-start.11 = (f32[24,16,128]{2,1,0:T(8,128)S(1)}, f32[24,16,128]{2,1,0:T(8,128)S(1)}, u32[]{:S(2)}, u32[]{:S(2)}) collective-permute-start(f32[24,16,128]{2,1,0:T(8,128)S(1)} %get-tuple-element.26), channel_id=1, source_target_pairs={{0,8},{8,0},{1,9},{9,1},{2,10},{10,2},{3,11},{11,3},{4,12},{12,4},... | collective-permute-start | bytes 589832 | tf_op jit(solution)/shard_map/ppermute | solution.py:515
  63.5 3.8 %reduce-precision_convert_fusion = (bf16[1,512,384]{2,1,0:T(8,128)(2,1)S(1)}, bf16[1,512,384]{2,1,0:T(8,128)(2,1)S(1)}) fusion(f32[512]{0:T(512)S(1)} %compare_select_fusion.2, s32[384]{0:T(512)S(1)} %add_select_fusion.1, s32[512]{0:T(512)S(1)} %fusion.25, pred[384]{0:T(512)(128)(4,1)S(1)} %fusion.11), kind=kLoop, calls=%fused_computation.2 | loop fusion | flops 3145728 | bytes 792448 | tf_op jit(solution)/shard_map/convert
  67.4 1.6 %collective-permute-done.11.got = f32[24,16,128]{2,1,0:T(8,128)S(1)} collective-permute-done((f32[24,16,128]{2,1,0:T(8,128)S(1)}, f32[24,16,128]{2,1,0:T(8,128)S(1)}, u32[]{:S(2)}, u32[]{:S(2)}) %collective-permute-start.11) | collective-permute-done | bytes 196640 | tf_op jit(solution)/shard_map/ppermute | solution.py:515
  69.0 3.9 %all-to-all-done.mail = f32[16,3,16,128]{3,2,1,0:T(8,128)S(1)} async-done(((f32[16,3,16,128]{3,2,1,0:T(8,128)}), f32[16,3,16,128]{3,2,1,0:T(8,128)S(1)}, u32[]{:S(2)}, u32[]{:S(2)}) %all-to-all-start) | async-done | bytes 393248 | tf_op jit(solution)/shard_map/all_to_all | solution.py:516
  72.9 1.0 join.1
  73.9 9.0 %all-to-all-start.1 = ((f32[16,24,256]{2,1,0:T(8,128)}), f32[16,24,256]{2,1,0:T(8,128)S(1)}, u32[]{:S(2)}, u32[]{:S(2)}) async-start(f32[16,24,256]{2,1,0:T(8,128)} %join.1), calls=%async_computation.1 | async-start | bytes 786432 | tf_op jit(solution)/shard_map/all_to_all | solution.py:518
  82.9 0.1 pad_maximum_fusion.basis
  83.0 0.1 fusion.6.relabel
  83.1 9.9 %all-to-all-done.1 = f32[16,24,256]{2,1,0:T(8,128)S(1)} async-done(((f32[16,24,256]{2,1,0:T(8,128)}), f32[16,24,256]{2,1,0:T(8,128)S(1)}, u32[]{:S(2)}, u32[]{:S(2)}) %all-to-all-start.1) | async-done | bytes 393248 | tf_op jit(solution)/shard_map/all_to_all | solution.py:518
  93.0 0.0 copy-start.7
  93.0 0.0 copy-start.3
  93.0 1.6 %transform.1 = f32[512,256]{1,0:T(8,128)} custom-call(bf16[2,512,384]{2,1,0:T(8,128)(2,1)S(1)} %pad_maximum_fusion.basis, f32[384,256]{1,0:T(8,128)S(1)} %bitcast.4, bf16[256,256]{1,0:T(8,128)(2,1)S(1)} %fusion.6.relabel), custom_call_target="tpu_custom_call" | custom-call | tf_op jit(solution)/shard_map/transform/pallas_call | solution.py:358
  94.6 4.1 %all-to-all-start.2 = ((f32[16,32,256]{2,1,0:T(8,128)}), f32[16,32,256]{2,1,0:T(8,128)S(1)}, u32[]{:S(2)}, u32[]{:S(2)}) async-start(f32[16,32,256]{2,1,0:T(8,128)} %bitcast.3), calls=%async_computation.2 | async-start | bytes 1048576 | tf_op jit(solution)/shard_map/all_to_all | solution.py:521
  98.7 0.0 copy-done.7
  98.7 0.1 select_reduce_fusion.3
  98.8 11.0 %all-to-all-done.2.traces = f32[16,32,256]{2,1,0:T(8,128)S(1)} async-done(((f32[16,32,256]{2,1,0:T(8,128)}), f32[16,32,256]{2,1,0:T(8,128)S(1)}, u32[]{:S(2)}, u32[]{:S(2)}) %all-to-all-start.2) | async-done | bytes 524320 | tf_op jit(solution)/shard_map/all_to_all | solution.py:521
  109.9 0.0 copy-done.3
  109.9 0.0 copy-done.4
  109.9 1.6 %update.1 = bf16[32,16,256]{2,1,0:T(8,128)(2,1)} custom-call(f32[32]{0:T(128)S(1)} %convert_element_type.24.events, s32[32]{0:T(128)S(1)} %compare_convert_fusion.inside, f32[16,32,256]{2,1,0:T(8,128)S(1)} %all-to-all-done.2.traces, bf16[32,16,256]{2,1,0:T(8,128)(2,1)S(1)} %copy-done.3, bf16[32,16,256]{2,1,0:T(8,128)(2,1)S(1)} %copy-done.4), custom_call_target="tpu_custom_call" | custom-call | tf_op jit(solution)/shard_map/update/pallas_call | solution.py:383
  (17 shorter events, 0.2 us)
Async XLA Ops:
  11.1 9.0 %copy-start = (f32[6,392,128]{2,1,0:T(8,128)S(1)}, f32[6,392,128]{2,1,0:T(8,128)}, u32[]{:S(2)}) copy-start(f32[6,392,128]{2,1,0:T(8,128)} %get-tuple-element.17.keep) | copy-start | bytes 3612676
  11.1 4.6 %collective-permute-start = (f32[1,392,128]{2,1,0:T(8,128)}, f32[1,392,128]{2,1,0:T(8,128)S(1)}, u32[]{:S(2)}, u32[]{:S(2)}) collective-permute-start(f32[1,392,128]{2,1,0:T(8,128)} %get-tuple-element.19), channel_id=1, source_target_pairs={{0,16},{16,0},{1,17},{17,1},{2,18},{18,2},{3,19},{19,3},{4,20},{20... | collective-permute-start | bytes 602120 | tf_op jit(solution)/shard_map/ppermute | solution.py:472
  14.5 0.9 copy-start.2
  15.8 4.3 %collective-permute-start.1 = (f32[6,392,128]{2,1,0:T(8,128)}, f32[6,392,128]{2,1,0:T(8,128)S(1)}, u32[]{:S(2)}, u32[]{:S(2)}) collective-permute-start(f32[6,392,128]{2,1,0:T(8,128)} %get-tuple-element.21), channel_id=1, source_target_pairs={{0,16},{16,0},{1,17},{17,1},{2,18},{18,2},{3,19},{19,3},{4,20},{20... | collective-permute-start | bytes 3612680 | tf_op jit(solution)/shard_map/ppermute | solution.py:474
  16.2 8.7 %collective-permute-start.2 = (f32[2,392,128]{2,1,0:T(8,128)S(1)}, f32[2,392,128]{2,1,0:T(8,128)S(1)}, u32[]{:S(2)}, u32[]{:S(2)}) collective-permute-start(f32[2,392,128]{2,1,0:T(8,128)S(1)} %collect.7.refs_0_), channel_id=1, source_target_pairs={{0,1},{1,2},{2,3},{3,4},{4,5},{5,6},{6,7},{7,0},{16,23},{17,16},{1... | collective-permute-start | bytes 1204232 | tf_op jit(solution)/shard_map/ppermute | solution.py:475
  20.1 9.1 %collective-permute-start.4 = (f32[2,392,128]{2,1,0:T(8,128)S(1)}, f32[2,392,128]{2,1,0:T(8,128)S(1)}, u32[]{:S(2)}, u32[]{:S(2)}) collective-permute-start(f32[2,392,128]{2,1,0:T(8,128)S(1)} %collect.8.refs_1_), channel_id=1, source_target_pairs={{0,1},{1,2},{2,3},{3,4},{4,5},{5,6},{6,7},{7,0},{16,23},{17,16},{1... | collective-permute-start | bytes 1204232 | tf_op jit(solution)/shard_map/ppermute | solution.py:478
  25.0 8.6 %collective-permute-start.3 = (f32[2,392,128]{2,1,0:T(8,128)S(1)}, f32[2,392,128]{2,1,0:T(8,128)S(1)}, u32[]{:S(2)}, u32[]{:S(2)}) collective-permute-start(f32[2,392,128]{2,1,0:T(8,128)S(1)} %collect.9.refs_1_), channel_id=1, source_target_pairs={{0,1},{1,2},{2,3},{3,4},{4,5},{5,6},{6,7},{7,0},{16,23},{17,16},{1... | collective-permute-start | bytes 1204232 | tf_op jit(solution)/shard_map/ppermute | solution.py:478
  29.3 8.5 %collective-permute-start.6 = (f32[2,392,128]{2,1,0:T(8,128)S(1)}, f32[2,392,128]{2,1,0:T(8,128)S(1)}, u32[]{:S(2)}, u32[]{:S(2)}) collective-permute-start(f32[2,392,128]{2,1,0:T(8,128)S(1)} %collect.10.refs_1_), channel_id=1, source_target_pairs={{0,1},{1,2},{2,3},{3,4},{4,5},{5,6},{6,7},{7,0},{16,23},{17,16},{1... | collective-permute-start | bytes 1204232 | tf_op jit(solution)/shard_map/ppermute | solution.py:478
  34.3 7.4 %copy-start.6 = (s32[16]{0:T(128)S(1)}, s32[16]{0:T(128)}, u32[]{:S(2)}) copy-start(s32[16]{0:T(128)} %param.11) | copy-start | bytes 196
  34.3 7.7 %copy-start.5 = (s32[16]{0:T(128)S(1)}, s32[16]{0:T(128)}, u32[]{:S(2)}) copy-start(s32[16]{0:T(128)} %pairing.1) | copy-start | bytes 196
  34.3 8.2 %collective-permute-start.5 = (f32[2,392,128]{2,1,0:T(8,128)}, f32[2,392,128]{2,1,0:T(8,128)}, u32[]{:S(2)}, u32[]{:S(2)}) collective-permute-start(f32[2,392,128]{2,1,0:T(8,128)} %collect.11.refs_1_), channel_id=1, source_target_pairs={{0,1},{1,2},{2,3},{3,4},{4,5},{5,6},{6,7},{7,0},{16,23},{17,16},{1... | collective-permute-start | bytes 1204232 | tf_op jit(solution)/shard_map/ppermute | solution.py:478
  38.6 8.8 %collective-permute-start.8 = (f32[2,392,128]{2,1,0:T(8,128)}, f32[2,392,128]{2,1,0:T(8,128)S(1)}, u32[]{:S(2)}, u32[]{:S(2)}) collective-permute-start(f32[2,392,128]{2,1,0:T(8,128)} %collect.12.refs_1_), channel_id=1, source_target_pairs={{0,1},{1,2},{2,3},{3,4},{4,5},{5,6},{6,7},{7,0},{16,23},{17,16},{1... | collective-permute-start | bytes 1204232 | tf_op jit(solution)/shard_map/ppermute | solution.py:478
  42.1 11.7 %copy-start.1 = (f32[2,392,128]{2,1,0:T(8,128)S(1)}, f32[2,392,128]{2,1,0:T(8,128)}, u32[]{:S(2)}) copy-start(f32[2,392,128]{2,1,0:T(8,128)} %get-tuple-element.16.refs_0_) | copy-start | bytes 1204228
  43.6 7.8 %collective-permute-start.9 = (f32[1,392,128]{2,1,0:T(8,128)S(1)}, f32[1,392,128]{2,1,0:T(8,128)S(1)}, u32[]{:S(2)}, u32[]{:S(2)}) collective-permute-start(f32[1,392,128]{2,1,0:T(8,128)S(1)} %get-tuple-element.24.before), channel_id=1, source_target_pairs={{0,17},{1,18},{2,19},{3,20},{4,21},{5,22},{6,23},{7,16},{16,7},{17... | collective-permute-start | bytes 602120 | tf_op jit(solution)/shard_map/ppermute | solution.py:480
  46.7 7.1 %collective-permute-start.7 = (f32[1,392,128]{2,1,0:T(8,128)S(1)}, f32[1,392,128]{2,1,0:T(8,128)S(1)}, u32[]{:S(2)}, u32[]{:S(2)}) collective-permute-start(f32[1,392,128]{2,1,0:T(8,128)S(1)} %get-tuple-element.23), channel_id=1, source_target_pairs={{0,1},{1,2},{2,3},{3,4},{4,5},{5,6},{6,7},{7,0},{16,23},{17,16},{1... | collective-permute-start | bytes 602120 | tf_op jit(solution)/shard_map/ppermute | solution.py:480
  47.4 6.3 %collective-permute-start.10 = (f32[392,128]{1,0:T(8,128)S(1)}, f32[392,128]{1,0:T(8,128)S(1)}, u32[]{:S(2)}, u32[]{:S(2)}) collective-permute-start(f32[392,128]{1,0:T(8,128)S(1)} %other_half.1), channel_id=1, source_target_pairs={{0,16},{16,0},{1,17},{17,1},{2,18},{18,2},{3,19},{19,3},{4,20},{20... | collective-permute-start | bytes 602120 | tf_op jit(solution)/shard_map/ppermute | solution.py:480
  55.1 17.9 %all-to-all-start = ((f32[16,3,16,128]{3,2,1,0:T(8,128)}), f32[16,3,16,128]{3,2,1,0:T(8,128)S(1)}, u32[]{:S(2)}, u32[]{:S(2)}) async-start(f32[16,3,16,128]{3,2,1,0:T(8,128)} %mail.1.refs_5_), calls=%async_computation | async-start | bytes 786432 | tf_op jit(solution)/shard_map/all_to_all | solution.py:516
  61.9 7.1 %collective-permute-start.11 = (f32[24,16,128]{2,1,0:T(8,128)S(1)}, f32[24,16,128]{2,1,0:T(8,128)S(1)}, u32[]{:S(2)}, u32[]{:S(2)}) collective-permute-start(f32[24,16,128]{2,1,0:T(8,128)S(1)} %get-tuple-element.26), channel_id=1, source_target_pairs={{0,8},{8,0},{1,9},{9,1},{2,10},{10,2},{3,11},{11,3},{4,12},{12,4},... | collective-permute-start | bytes 589832 | tf_op jit(solution)/shard_map/ppermute | solution.py:515
  73.9 19.0 %all-to-all-start.1 = ((f32[16,24,256]{2,1,0:T(8,128)}), f32[16,24,256]{2,1,0:T(8,128)S(1)}, u32[]{:S(2)}, u32[]{:S(2)}) async-start(f32[16,24,256]{2,1,0:T(8,128)} %join.1), calls=%async_computation.1 | async-start | bytes 786432 | tf_op jit(solution)/shard_map/all_to_all | solution.py:518
  93.0 5.7 %copy-start.7 = (s32[32]{0:T(128)S(1)}, s32[32]{0:T(128)}, u32[]{:S(2)}) copy-start(s32[32]{0:T(128)} %param.12) | copy-start | bytes 388
  93.0 16.9 %copy-start.3 = (bf16[32,16,256]{2,1,0:T(8,128)(2,1)S(1)}, bf16[32,16,256]{2,1,0:T(8,128)(2,1)}, u32[]{:S(2)}) copy-start(bf16[32,16,256]{2,1,0:T(8,128)(2,1)} %older.1) | copy-start | bytes 786436
  93.0 16.9 %copy-start.4 = (bf16[32,16,256]{2,1,0:T(8,128)(2,1)S(1)}, bf16[32,16,256]{2,1,0:T(8,128)(2,1)}, u32[]{:S(2)}) copy-start(bf16[32,16,256]{2,1,0:T(8,128)(2,1)} %data.1) | copy-start | bytes 786436
  94.6 15.3 %all-to-all-start.2 = ((f32[16,32,256]{2,1,0:T(8,128)}), f32[16,32,256]{2,1,0:T(8,128)S(1)}, u32[]{:S(2)}, u32[]{:S(2)}) async-start(f32[16,32,256]{2,1,0:T(8,128)} %bitcast.3), calls=%async_computation.2 | async-start | bytes 1048576 | tf_op jit(solution)/shard_map/all_to_all | solution.py:521

commit v5 on v4

--- a/solution.py
+++ b/solution.py
@@ -30,7 +30,7 @@
 
 
 def product_kernel(
-    pairing, ratio, spectra, primaries, keep_first, keep, give_first, give, own,
+    pairing, ratio, spectra, primaries, keep_first, keep, keep_last, give_first, give, give_last, own,
     left, right, relabel, relabel_low, chosen, held, out, slots, left_sems, right_sems, out_sems,
 ):
     freqs, _, width, depth = left.shape
@@ -125,18 +125,13 @@
             for slot, dst, i in moves
         ]
 
-    early = copies(
-        [(0, keep_first, 0)]
-        + [(n, keep, n - 1) for n in (2, 4, 6)]
-        + [(7 + n, give, n - 1) for n in (1, 3, 5)]
-        + [(14, own, 0)]
-    )
-    late = copies(
-        [(7, give_first, 0)]
-        + [(n, keep, n - 1) for n in (1, 3, 5)]
-        + [(7 + n, give, n - 1) for n in (2, 4, 6)]
-        + [(15, own, 1)]
-    )
+    def unit(first, some, last, n):
+        return (first, 0) if n == 0 else (some, n - 1) if n < 4 else (last, n - 4)
+
+    moves = [(n,) + unit(keep_first, keep, keep_last, n) for n in range(7)]
+    moves += [(7 + n,) + unit(give_first, give, give_last, n) for n in range(7)]
+    early = copies([moves[n] for n in (0, 2, 4, 6, 8, 10, 12)] + [(14, own, 0)])
+    late = copies([moves[n] for n in (7, 1, 3, 5, 9, 11, 13)] + [(15, own, 1)])
     fetch_right(0).wait()
     choose(0)
     fetch_right(1).wait()
@@ -163,11 +158,11 @@
     height = 2 * freqs * BLOCK + 8
     smem = pl.BlockSpec(memory_space=pltpu.SMEM)
     anywhere = pl.BlockSpec(memory_space=pl.ANY)
-    shapes = [(n, height, LANES) for n in (1, 6, 1, 6, 2)]
+    shapes = [(n, height, LANES) for n in (1, 3, 3, 1, 3, 3, 2)]
     return pl.pallas_call(
         product_kernel,
         in_specs=[smem, smem, anywhere, anywhere],
-        out_specs=[anywhere] * 5,
+        out_specs=[anywhere] * 7,
         out_shape=[jax.ShapeDtypeStruct(s, jnp.float32) for s in shapes],
         scratch_shapes=[
             pltpu.VMEM(spectra.shape, spectra.dtype),
@@ -449,7 +444,7 @@
     )(source)
 
 
-def ring_sums(keep_first, keep, give_first, give):
+def ring_sums(keep_first, keep, keep_last, give_first, give, give_last):
     swap = functools.partial(lax.ppermute, axis_name="core", perm=ring(2, 1))
     step = functools.partial(
         lax.ppermute,
@@ -474,9 +469,14 @@
     got = swap(give)
     flying = [step(payload)]
     for n in range(5):
-        payload = collect(n, keep, got, payload, *flying[:-1])
+        if n == 1:
+            payload, give_last = lax.optimization_barrier((payload, give_last))
+            got_last = swap(give_last)
+        if n == 3:
+            keep, got = keep_last, got_last
+        payload = collect(n % 3, keep, got, payload, *flying[:-1])
         flying = flying[-1:] + [step(payload)]
-    mine, other = collect(5, keep, got, payload, flying[0], split=True)
+    mine, other = collect(2, keep, got, payload, flying[0], split=True)
     return step(mine), flying[1], cross(other)[0], swap(other_half(flying[1], other))
 
 

time: 112 us -> 110 us (0.982)
  Pallas kernels: 19.8 us -> 17.3 us
    pallas_call x7, Pallas kernels: 2.8 us -> 0.31 us  [collect(): pl.pallas_call(functools.partial(collect_kernel, len(arrived)), grid=(1,)...]
    ppermute x5, waiting for transfers between devices: 2.93 us -> 4.19 us  [ring_sums(): flying = flying[-1:] + [step(payload)]]
  transfers between devices with their start and end apart: 15 -> 16, of which waited for: 12 -> 13; matrix products, arithmetic and copies ran while one was open for 4% -> 4% of each run, Pallas kernels for 3% -> 1%
where the time goes in v5:
time: 110 us
  starting transfers between devices  50.9 us (46%)
  waiting for transfers between devices  34.8 us (32%)
  Pallas kernels  17.3 us (16%)
  other arithmetic  4.53 us (4%)
  local copies, waits for them, and re-layouts  2.11 us (2%)
    ppermute x5, starting transfers between devices, ring_sums(): flying = flying[-1:] + [step(payload)]  14.7 us
    pallas_call x1, Pallas kernels, product(): pl.pallas_call(product_kernel, in_specs=[smem, smem, anywhere, anywhere],...  11.1 us
    all_to_all x1, waiting for transfers between devices, on_device(): lax.all_to_all(slotted, freq, split_axis=0, concat_axis=0, tiled=True)  11 us
    all_to_all x1, waiting for transfers between devices, on_device(): lax.all_to_all(whole, freq, split_axis=0, concat_axis=0, tiled=True)  9.87 us
    all_to_all x1, starting transfers between devices, on_device(): lax.all_to_all(whole, freq, split_axis=0, concat_axis=0, tiled=True)  9.52 us
    all_to_all x1, starting transfers between devices, on_device(): mail = lax.all_to_all(mail, src, split_axis=0, concat_axis=0, tiled=True)  6.86 us
    all_to_all x1, waiting for transfers between devices, on_device(): mail = lax.all_to_all(mail, src, split_axis=0, concat_axis=0, tiled=True)  4.4 us
    ppermute x5, waiting for transfers between devices, ring_sums(): flying = flying[-1:] + [step(payload)]  4.19 us
  transfers between devices with their start and end apart: 16, of which 13 were waited for; matrix products, arithmetic and copies ran while one was open for 4% of the time, Pallas kernels for 1%

profile of v5, /device:TPU:1, one launch (start us, length us, event | category | flops | bytes accessed | tf_op | source)
XLA Modules:
  0.0 109.8 jit_solution(6227450175624471977)
XLA Ops:
  0.0 11.1 %product.1 = (f32[1,392,128]{2,1,0:T(8,128)}, f32[3,392,128]{2,1,0:T(8,128)}, f32[3,392,128]{2,1,0:T(8,128)}, f32[1,392,128]{2,1,0:T(8,128)}, f32[3,392,128]{2,1...) custom-call(s32[16]{0:T(128)} %pairing.1, f32[2,12]{1,0:T(2,128)} %ratio.1, ...), custom_call_target="tpu_custom_call" | custom-call | flops 3221225472 | bytes 15794176 | tf_op jit(solution)/shard_map/product/pallas_call | solution.py:162
  11.1 0.0 copy-start
  11.1 3.3 %collective-permute-start = (f32[1,392,128]{2,1,0:T(8,128)}, f32[1,392,128]{2,1,0:T(8,128)S(1)}, u32[]{:S(2)}, u32[]{:S(2)}) collective-permute-start(f32[1,392,128]{2,1,0:T(8,128)} %get-tuple-element.24), channel_id=1, source_target_pairs={{0,16},{16,0},{1,17},{17,1},{2,18},{18,2},{3,19},{19,3},{4,20},{20... | collective-permute-start | bytes 602120 | tf_op jit(solution)/shard_map/ppermute | solution.py:467
  14.5 0.9 copy-done.3
  15.4 0.2 lift.1.keep
  15.6 0.0 copy-start.7
  15.6 0.0 copy-start.6
  15.7 0.1 collective-permute-done.got
  15.8 0.5 collective-permute-start.1
  16.2 3.9 %collective-permute-start.3 = (f32[2,392,128]{2,1,0:T(8,128)S(1)}, f32[2,392,128]{2,1,0:T(8,128)S(1)}, u32[]{:S(2)}, u32[]{:S(2)}) collective-permute-start(f32[2,392,128]{2,1,0:T(8,128)S(1)} %collect.7.refs_0_), channel_id=1, source_target_pairs={{0,1},{1,2},{2,3},{3,4},{4,5},{5,6},{6,7},{7,0},{16,23},{17,16},{1... | collective-permute-start | bytes 1204232 | tf_op jit(solution)/shard_map/ppermute | solution.py:470
  20.1 0.0 collective-permute-done.1.got
  20.1 0.0 copy-start.1
  20.1 1.1 copy-done.1
  21.2 0.0 copy-start.2
  21.2 1.9 %collective-permute-start.5 = (f32[2,392,128]{2,1,0:T(8,128)S(1)}, f32[2,392,128]{2,1,0:T(8,128)S(1)}, u32[]{:S(2)}, u32[]{:S(2)}) collective-permute-start(f32[2,392,128]{2,1,0:T(8,128)S(1)} %collect.8.refs_1_), channel_id=1, source_target_pairs={{0,1},{1,2},{2,3},{3,4},{4,5},{5,6},{6,7},{7,0},{16,23},{17,16},{1... | collective-permute-start | bytes 1204232 | tf_op jit(solution)/shard_map/ppermute | solution.py:478
  23.1 0.0 collective-permute-start.2
  23.1 1.8 %collective-permute-done.3.refs_0_ = f32[2,392,128]{2,1,0:T(8,128)S(1)} collective-permute-done((f32[2,392,128]{2,1,0:T(8,128)S(1)}, f32[2,392,128]{2,1,0:T(8,128)S(1)}, u32[]{:S(2)}, u32[]{:S(2)}) %collective-permute-start.3) | collective-permute-done | bytes 401440 | tf_op jit(solution)/shard_map/ppermute | solution.py:470
  24.9 0.1 collect.9.refs_1_
  25.0 3.2 %collective-permute-start.4 = (f32[2,392,128]{2,1,0:T(8,128)S(1)}, f32[2,392,128]{2,1,0:T(8,128)S(1)}, u32[]{:S(2)}, u32[]{:S(2)}) collective-permute-start(f32[2,392,128]{2,1,0:T(8,128)S(1)} %collect.9.refs_1_), channel_id=1, source_target_pairs={{0,1},{1,2},{2,3},{3,4},{4,5},{5,6},{6,7},{7,0},{16,23},{17,16},{1... | collective-permute-start | bytes 1204232 | tf_op jit(solution)/shard_map/ppermute | solution.py:478
  28.1 1.1 collective-permute-done.5.refs_0_
  29.2 3.2 %collective-permute-start.7 = (f32[2,392,128]{2,1,0:T(8,128)S(1)}, f32[2,392,128]{2,1,0:T(8,128)S(1)}, u32[]{:S(2)}, u32[]{:S(2)}) collective-permute-start(f32[2,392,128]{2,1,0:T(8,128)S(1)} %collect.10.refs_1_), channel_id=1, source_target_pairs={{0,1},{1,2},{2,3},{3,4},{4,5},{5,6},{6,7},{7,0},{16,23},{17,16},{1... | collective-permute-start | bytes 1204232 | tf_op jit(solution)/shard_map/ppermute | solution.py:478
  32.4 1.1 collective-permute-done.4.refs_0_
  33.5 0.0 collective-permute-done.2.got
  33.5 0.0 copy-done
  33.5 0.1 collect.11.refs_1_
  33.6 3.2 %collective-permute-start.6 = (f32[2,392,128]{2,1,0:T(8,128)S(1)}, f32[2,392,128]{2,1,0:T(8,128)S(1)}, u32[]{:S(2)}, u32[]{:S(2)}) collective-permute-start(f32[2,392,128]{2,1,0:T(8,128)S(1)} %collect.11.refs_1_), channel_id=1, source_target_pairs={{0,1},{1,2},{2,3},{3,4},{4,5},{5,6},{6,7},{7,0},{16,23},{17,16},{1... | collective-permute-start | bytes 1204232 | tf_op jit(solution)/shard_map/ppermute | solution.py:478
  36.8 1.0 collective-permute-done.7.refs_0_
  37.8 3.2 %collective-permute-start.9 = (f32[2,392,128]{2,1,0:T(8,128)S(1)}, f32[2,392,128]{2,1,0:T(8,128)S(1)}, u32[]{:S(2)}, u32[]{:S(2)}) collective-permute-start(f32[2,392,128]{2,1,0:T(8,128)S(1)} %collect.12.refs_1_), channel_id=1, source_target_pairs={{0,1},{1,2},{2,3},{3,4},{4,5},{5,6},{6,7},{7,0},{16,23},{17,16},{1... | collective-permute-start | bytes 1204232 | tf_op jit(solution)/shard_map/ppermute | solution.py:478
  41.0 0.0 copy-done.7
  41.0 0.1 copy.11
  41.2 0.1 reduce
  41.3 0.0 copy-done.6
  41.3 0.1 select_reduce_fusion.2
  41.4 0.7 collective-permute-done.6.refs_0_
  42.1 0.1 collect.13
  42.2 3.2 %collective-permute-start.10 = (f32[1,392,128]{2,1,0:T(8,128)S(1)}, f32[1,392,128]{2,1,0:T(8,128)S(1)}, u32[]{:S(2)}, u32[]{:S(2)}) collective-permute-start(f32[1,392,128]{2,1,0:T(8,128)S(1)} %get-tuple-element.32.before), channel_id=1, source_target_pairs={{0,17},{1,18},{2,19},{3,20},{4,21},{5,22},{6,23},{7,16},{16,7},{17... | collective-permute-start | bytes 602120 | tf_op jit(solution)/shard_map/ppermute | solution.py:480
  45.3 0.7 collective-permute-start.8
  46.1 0.3 collective-permute-done.9.arrived.refs_2_
  46.4 2.8 %collective-permute-start.11 = (f32[392,128]{1,0:T(8,128)S(1)}, f32[392,128]{1,0:T(8,128)S(1)}, u32[]{:S(2)}, u32[]{:S(2)}) collective-permute-start(f32[392,128]{1,0:T(8,128)S(1)} %other_half.1), channel_id=1, source_target_pairs={{0,16},{16,0},{1,17},{17,1},{2,18},{18,2},{3,19},{19,3},{4,20},{20... | collective-permute-start | bytes 602120 | tf_op jit(solution)/shard_map/ppermute | solution.py:480
  49.2 0.1 select_reduce_fusion.1
  49.3 1.3 %collective-permute-done.10 = f32[1,392,128]{2,1,0:T(8,128)S(1)} collective-permute-done((f32[1,392,128]{2,1,0:T(8,128)S(1)}, f32[1,392,128]{2,1,0:T(8,128)S(1)}, u32[]{:S(2)}, u32[]{:S(2)}) %collective-permute-start.10) | collective-permute-done | bytes 200736 | tf_op jit(solution)/shard_map/ppermute | solution.py:480
  50.5 1.3 %collective-permute-done.8.refs_1_ = f32[1,392,128]{2,1,0:T(8,128)S(1)} collective-permute-done((f32[1,392,128]{2,1,0:T(8,128)S(1)}, f32[1,392,128]{2,1,0:T(8,128)S(1)}, u32[]{:S(2)}, u32[]{:S(2)}) %collective-permute-start.8) | collective-permute-done | bytes 200736 | tf_op jit(solution)/shard_map/ppermute | solution.py:480
  51.8 0.0 collective-permute-done.11.refs_4_
  51.8 0.0 copy-done.2
  51.8 1.3 %mail.1.refs_5_ = f32[16,3,16,128]{3,2,1,0:T(8,128)} custom-call(f32[2,392,128]{2,1,0:T(8,128)S(1)} %copy-done.2, f32[1,392,128]{2,1,0:T(8,128)S(1)} %collective-permute-done.8.refs_1_, f32[2,392,128]{2,1,0:T(8,128)S(1)} %collective-permute-done.9.arrived.refs_2_, f32[392,128]{1,0:T(8,128)S(1)} %bitcast.5, f32[392,128]{1,0:T(8,128)S(1)} %collective-permute-done.11.refs_4_), custom_call_target="tpu_custom_call" | custom-call | tf_op jit(solution)/shard_map/mail/pallas_call | solution.py:285
  53.1 6.9 %all-to-all-start = ((f32[16,3,16,128]{3,2,1,0:T(8,128)}), f32[16,3,16,128]{3,2,1,0:T(8,128)S(1)}, u32[]{:S(2)}, u32[]{:S(2)}) async-start(f32[16,3,16,128]{3,2,1,0:T(8,128)} %mail.1.refs_5_), calls=%async_computation | async-start | bytes 786432 | tf_op jit(solution)/shard_map/all_to_all | solution.py:516
  60.0 0.1 direct.1
  60.1 1.5 %collective-permute-start.12 = (f32[24,16,128]{2,1,0:T(8,128)S(1)}, f32[24,16,128]{2,1,0:T(8,128)S(1)}, u32[]{:S(2)}, u32[]{:S(2)}) collective-permute-start(f32[24,16,128]{2,1,0:T(8,128)S(1)} %get-tuple-element.34), channel_id=1, source_target_pairs={{0,8},{8,0},{1,9},{9,1},{2,10},{10,2},{3,11},{11,3},{4,12},{12,4},... | collective-permute-start | bytes 589832 | tf_op jit(solution)/shard_map/ppermute | solution.py:515
  61.5 3.8 %reduce-precision_convert_fusion = (bf16[1,512,384]{2,1,0:T(8,128)(2,1)S(1)}, bf16[1,512,384]{2,1,0:T(8,128)(2,1)S(1)}) fusion(f32[512]{0:T(512)S(1)} %compare_select_fusion.2, s32[384]{0:T(512)S(1)} %add_select_fusion.1, s32[512]{0:T(512)S(1)} %fusion.25, pred[384]{0:T(512)(128)(4,1)S(1)} %fusion.11), kind=kLoop, calls=%fused_computation.2 | loop fusion | flops 3145728 | bytes 792448 | tf_op jit(solution)/shard_map/convert
  65.4 0.9 collective-permute-done.12.got
  66.3 4.4 %all-to-all-done.mail = f32[16,3,16,128]{3,2,1,0:T(8,128)S(1)} async-done(((f32[16,3,16,128]{3,2,1,0:T(8,128)}), f32[16,3,16,128]{3,2,1,0:T(8,128)S(1)}, u32[]{:S(2)}, u32[]{:S(2)}) %all-to-all-start) | async-done | bytes 393248 | tf_op jit(solution)/shard_map/all_to_all | solution.py:516
  70.7 1.0 join.1
  71.7 9.5 %all-to-all-start.1 = ((f32[16,24,256]{2,1,0:T(8,128)}), f32[16,24,256]{2,1,0:T(8,128)S(1)}, u32[]{:S(2)}, u32[]{:S(2)}) async-start(f32[16,24,256]{2,1,0:T(8,128)} %join.1), calls=%async_computation.1 | async-start | bytes 786432 | tf_op jit(solution)/shard_map/all_to_all | solution.py:518
  81.2 0.1 pad_maximum_fusion.basis
  81.3 0.1 fusion.6.relabel
  81.4 9.9 %all-to-all-done.1 = f32[16,24,256]{2,1,0:T(8,128)S(1)} async-done(((f32[16,24,256]{2,1,0:T(8,128)}), f32[16,24,256]{2,1,0:T(8,128)S(1)}, u32[]{:S(2)}, u32[]{:S(2)}) %all-to-all-start.1) | async-done | bytes 393248 | tf_op jit(solution)/shard_map/all_to_all | solution.py:518
  91.3 1.6 %transform.1 = f32[512,256]{1,0:T(8,128)} custom-call(bf16[2,512,384]{2,1,0:T(8,128)(2,1)S(1)} %pad_maximum_fusion.basis, f32[384,256]{1,0:T(8,128)S(1)} %bitcast.4, bf16[256,256]{1,0:T(8,128)(2,1)S(1)} %fusion.6.relabel), custom_call_target="tpu_custom_call" | custom-call | tf_op jit(solution)/shard_map/transform/pallas_call | solution.py:353
  92.9 4.1 %all-to-all-start.2 = ((f32[16,32,256]{2,1,0:T(8,128)}), f32[16,32,256]{2,1,0:T(8,128)S(1)}, u32[]{:S(2)}, u32[]{:S(2)}) async-start(f32[16,32,256]{2,1,0:T(8,128)} %bitcast.3), calls=%async_computation.2 | async-start | bytes 1048576 | tf_op jit(solution)/shard_map/all_to_all | solution.py:521
  97.0 0.0 copy-done.8
  97.0 0.1 select_reduce_fusion.3
  97.1 11.0 %all-to-all-done.2.traces = f32[16,32,256]{2,1,0:T(8,128)S(1)} async-done(((f32[16,32,256]{2,1,0:T(8,128)}), f32[16,32,256]{2,1,0:T(8,128)S(1)}, u32[]{:S(2)}, u32[]{:S(2)}) %all-to-all-start.2) | async-done | bytes 524320 | tf_op jit(solution)/shard_map/all_to_all | solution.py:521
  108.1 0.0 copy-done.4
  108.2 0.0 copy-done.5
  108.2 1.7 %update.1 = bf16[32,16,256]{2,1,0:T(8,128)(2,1)} custom-call(f32[32]{0:T(128)S(1)} %convert_element_type.24.events, s32[32]{0:T(128)S(1)} %compare_convert_fusion.inside, f32[16,32,256]{2,1,0:T(8,128)S(1)} %all-to-all-done.2.traces, bf16[32,16,256]{2,1,0:T(8,128)(2,1)S(1)} %copy-done.4, bf16[32,16,256]{2,1,0:T(8,128)(2,1)S(1)} %copy-done.5), custom_call_target="tpu_custom_call" | custom-call | tf_op jit(solution)/shard_map/update/pallas_call | solution.py:378
  (21 shorter events, 0.3 us)
Async XLA Ops:
  11.1 22.4 %copy-start = (f32[3,392,128]{2,1,0:T(8,128)S(1)}, f32[3,392,128]{2,1,0:T(8,128)}, u32[]{:S(2)}) copy-start(f32[3,392,128]{2,1,0:T(8,128)} %get-tuple-element.21.keep) | copy-start | bytes 1806340
  11.1 4.6 %collective-permute-start = (f32[1,392,128]{2,1,0:T(8,128)}, f32[1,392,128]{2,1,0:T(8,128)S(1)}, u32[]{:S(2)}, u32[]{:S(2)}) collective-permute-start(f32[1,392,128]{2,1,0:T(8,128)} %get-tuple-element.24), channel_id=1, source_target_pairs={{0,16},{16,0},{1,17},{17,1},{2,18},{18,2},{3,19},{19,3},{4,20},{20... | collective-permute-start | bytes 602120 | tf_op jit(solution)/shard_map/ppermute | solution.py:467
  14.5 0.9 copy-start.3
  15.6 25.4 %copy-start.7 = (s32[16]{0:T(128)S(1)}, s32[16]{0:T(128)}, u32[]{:S(2)}) copy-start(s32[16]{0:T(128)} %param.11) | copy-start | bytes 196
  15.6 25.7 %copy-start.6 = (s32[16]{0:T(128)S(1)}, s32[16]{0:T(128)}, u32[]{:S(2)}) copy-start(s32[16]{0:T(128)} %pairing.1) | copy-start | bytes 196
  15.8 4.3 %collective-permute-start.1 = (f32[3,392,128]{2,1,0:T(8,128)}, f32[3,392,128]{2,1,0:T(8,128)S(1)}, u32[]{:S(2)}, u32[]{:S(2)}) collective-permute-start(f32[3,392,128]{2,1,0:T(8,128)} %get-tuple-element.26), channel_id=1, source_target_pairs={{0,16},{16,0},{1,17},{17,1},{2,18},{18,2},{3,19},{19,3},{4,20},{20... | collective-permute-start | bytes 1806344 | tf_op jit(solution)/shard_map/ppermute | solution.py:469
  16.2 8.7 %collective-permute-start.3 = (f32[2,392,128]{2,1,0:T(8,128)S(1)}, f32[2,392,128]{2,1,0:T(8,128)S(1)}, u32[]{:S(2)}, u32[]{:S(2)}) collective-permute-start(f32[2,392,128]{2,1,0:T(8,128)S(1)} %collect.7.refs_0_), channel_id=1, source_target_pairs={{0,1},{1,2},{2,3},{3,4},{4,5},{5,6},{6,7},{7,0},{16,23},{17,16},{1... | collective-permute-start | bytes 1204232 | tf_op jit(solution)/shard_map/ppermute | solution.py:470
  20.1 1.1 copy-start.1
  21.2 30.6 %copy-start.2 = (f32[2,392,128]{2,1,0:T(8,128)S(1)}, f32[2,392,128]{2,1,0:T(8,128)}, u32[]{:S(2)}) copy-start(f32[2,392,128]{2,1,0:T(8,128)} %get-tuple-element.20.refs_0_) | copy-start | bytes 1204228
  21.2 8.0 %collective-permute-start.5 = (f32[2,392,128]{2,1,0:T(8,128)S(1)}, f32[2,392,128]{2,1,0:T(8,128)S(1)}, u32[]{:S(2)}, u32[]{:S(2)}) collective-permute-start(f32[2,392,128]{2,1,0:T(8,128)S(1)} %collect.8.refs_1_), channel_id=1, source_target_pairs={{0,1},{1,2},{2,3},{3,4},{4,5},{5,6},{6,7},{7,0},{16,23},{17,16},{1... | collective-permute-start | bytes 1204232 | tf_op jit(solution)/shard_map/ppermute | solution.py:478
  23.1 10.4 %collective-permute-start.2 = (f32[3,392,128]{2,1,0:T(8,128)}, f32[3,392,128]{2,1,0:T(8,128)S(1)}, u32[]{:S(2)}, u32[]{:S(2)}) collective-permute-start(f32[3,392,128]{2,1,0:T(8,128)} %get-tuple-element.29), channel_id=1, source_target_pairs={{0,16},{16,0},{1,17},{17,1},{2,18},{18,2},{3,19},{19,3},{4,20},{20... | collective-permute-start | bytes 1806344 | tf_op jit(solution)/shard_map/ppermute | solution.py:474
  25.0 8.5 %collective-permute-start.4 = (f32[2,392,128]{2,1,0:T(8,128)S(1)}, f32[2,392,128]{2,1,0:T(8,128)S(1)}, u32[]{:S(2)}, u32[]{:S(2)}) collective-permute-start(f32[2,392,128]{2,1,0:T(8,128)S(1)} %collect.9.refs_1_), channel_id=1, source_target_pairs={{0,1},{1,2},{2,3},{3,4},{4,5},{5,6},{6,7},{7,0},{16,23},{17,16},{1... | collective-permute-start | bytes 1204232 | tf_op jit(solution)/shard_map/ppermute | solution.py:478
  29.2 8.6 %collective-permute-start.7 = (f32[2,392,128]{2,1,0:T(8,128)S(1)}, f32[2,392,128]{2,1,0:T(8,128)S(1)}, u32[]{:S(2)}, u32[]{:S(2)}) collective-permute-start(f32[2,392,128]{2,1,0:T(8,128)S(1)} %collect.10.refs_1_), channel_id=1, source_target_pairs={{0,1},{1,2},{2,3},{3,4},{4,5},{5,6},{6,7},{7,0},{16,23},{17,16},{1... | collective-permute-start | bytes 1204232 | tf_op jit(solution)/shard_map/ppermute | solution.py:478
  33.6 8.5 %collective-permute-start.6 = (f32[2,392,128]{2,1,0:T(8,128)S(1)}, f32[2,392,128]{2,1,0:T(8,128)S(1)}, u32[]{:S(2)}, u32[]{:S(2)}) collective-permute-start(f32[2,392,128]{2,1,0:T(8,128)S(1)} %collect.11.refs_1_), channel_id=1, source_target_pairs={{0,1},{1,2},{2,3},{3,4},{4,5},{5,6},{6,7},{7,0},{16,23},{17,16},{1... | collective-permute-start | bytes 1204232 | tf_op jit(solution)/shard_map/ppermute | solution.py:478
  37.8 8.6 %collective-permute-start.9 = (f32[2,392,128]{2,1,0:T(8,128)S(1)}, f32[2,392,128]{2,1,0:T(8,128)S(1)}, u32[]{:S(2)}, u32[]{:S(2)}) collective-permute-start(f32[2,392,128]{2,1,0:T(8,128)S(1)} %collect.12.refs_1_), channel_id=1, source_target_pairs={{0,1},{1,2},{2,3},{3,4},{4,5},{5,6},{6,7},{7,0},{16,23},{17,16},{1... | collective-permute-start | bytes 1204232 | tf_op jit(solution)/shard_map/ppermute | solution.py:478
  42.2 8.4 %collective-permute-start.10 = (f32[1,392,128]{2,1,0:T(8,128)S(1)}, f32[1,392,128]{2,1,0:T(8,128)S(1)}, u32[]{:S(2)}, u32[]{:S(2)}) collective-permute-start(f32[1,392,128]{2,1,0:T(8,128)S(1)} %get-tuple-element.32.before), channel_id=1, source_target_pairs={{0,17},{1,18},{2,19},{3,20},{4,21},{5,22},{6,23},{7,16},{16,7},{17... | collective-permute-start | bytes 602120 | tf_op jit(solution)/shard_map/ppermute | solution.py:480
  45.3 51.6 %copy-start.8 = (s32[32]{0:T(128)S(1)}, s32[32]{0:T(128)}, u32[]{:S(2)}) copy-start(s32[32]{0:T(128)} %param.12) | copy-start | bytes 388
  45.3 62.8 %copy-start.4 = (bf16[32,16,256]{2,1,0:T(8,128)(2,1)S(1)}, bf16[32,16,256]{2,1,0:T(8,128)(2,1)}, u32[]{:S(2)}) copy-start(bf16[32,16,256]{2,1,0:T(8,128)(2,1)} %older.1) | copy-start | bytes 786436
  45.3 62.8 %copy-start.5 = (bf16[32,16,256]{2,1,0:T(8,128)(2,1)S(1)}, bf16[32,16,256]{2,1,0:T(8,128)(2,1)}, u32[]{:S(2)}) copy-start(bf16[32,16,256]{2,1,0:T(8,128)(2,1)} %data.1) | copy-start | bytes 786436
  45.3 6.5 %collective-permute-start.8 = (f32[1,392,128]{2,1,0:T(8,128)S(1)}, f32[1,392,128]{2,1,0:T(8,128)S(1)}, u32[]{:S(2)}, u32[]{:S(2)}) collective-permute-start(f32[1,392,128]{2,1,0:T(8,128)S(1)} %get-tuple-element.31), channel_id=1, source_target_pairs={{0,1},{1,2},{2,3},{3,4},{4,5},{5,6},{6,7},{7,0},{16,23},{17,16},{1... | collective-permute-start | bytes 602120 | tf_op jit(solution)/shard_map/ppermute | solution.py:480
  46.4 5.4 %collective-permute-start.11 = (f32[392,128]{1,0:T(8,128)S(1)}, f32[392,128]{1,0:T(8,128)S(1)}, u32[]{:S(2)}, u32[]{:S(2)}) collective-permute-start(f32[392,128]{1,0:T(8,128)S(1)} %other_half.1), channel_id=1, source_target_pairs={{0,16},{16,0},{1,17},{17,1},{2,18},{18,2},{3,19},{19,3},{4,20},{20... | collective-permute-start | bytes 602120 | tf_op jit(solution)/shard_map/ppermute | solution.py:480
  53.1 17.6 %all-to-all-start = ((f32[16,3,16,128]{3,2,1,0:T(8,128)}), f32[16,3,16,128]{3,2,1,0:T(8,128)S(1)}, u32[]{:S(2)}, u32[]{:S(2)}) async-start(f32[16,3,16,128]{3,2,1,0:T(8,128)} %mail.1.refs_5_), calls=%async_computation | async-start | bytes 786432 | tf_op jit(solution)/shard_map/all_to_all | solution.py:516
  60.1 6.2 %collective-permute-start.12 = (f32[24,16,128]{2,1,0:T(8,128)S(1)}, f32[24,16,128]{2,1,0:T(8,128)S(1)}, u32[]{:S(2)}, u32[]{:S(2)}) collective-permute-start(f32[24,16,128]{2,1,0:T(8,128)S(1)} %get-tuple-element.34), channel_id=1, source_target_pairs={{0,8},{8,0},{1,9},{9,1},{2,10},{10,2},{3,11},{11,3},{4,12},{12,4},... | collective-permute-start | bytes 589832 | tf_op jit(solution)/shard_map/ppermute | solution.py:515
  71.7 19.6 %all-to-all-start.1 = ((f32[16,24,256]{2,1,0:T(8,128)}), f32[16,24,256]{2,1,0:T(8,128)S(1)}, u32[]{:S(2)}, u32[]{:S(2)}) async-start(f32[16,24,256]{2,1,0:T(8,128)} %join.1), calls=%async_computation.1 | async-start | bytes 786432 | tf_op jit(solution)/shard_map/all_to_all | solution.py:518
  92.9 15.3 %all-to-all-start.2 = ((f32[16,32,256]{2,1,0:T(8,128)}), f32[16,32,256]{2,1,0:T(8,128)S(1)}, u32[]{:S(2)}, u32[]{:S(2)}) async-start(f32[16,32,256]{2,1,0:T(8,128)} %bitcast.3), calls=%async_computation.2 | async-start | bytes 1048576 | tf_op jit(solution)/shard_map/all_to_all | solution.py:521

commit v6 on v5

--- a/solution.py
+++ b/solution.py
@@ -362,10 +362,11 @@
 
 def update_kernel(events, inside, traces, older, data, out):
     count = older.shape[0]
+    turned = jnp.swapaxes(traces[...], 0, 1)
     for t in range(count):
         old = older[t].astype(jnp.float32)
         moved = old + step_weight * events[t] * (
-            data[t].astype(jnp.float32) - old - traces[:, t, :]
+            data[t].astype(jnp.float32) - old - turned[t]
         )
         size = jnp.maximum(jnp.abs(moved) - shrink_level, 0.0)
         shrunk = jnp.where(moved < 0.0, -size, size)
@@ -467,6 +468,7 @@
     payload = collect(0, lift(keep_first), swap(give_first), keep_first)
     payload, give = lax.optimization_barrier((payload, give))
     got = swap(give)
+    keep = lift(keep)
     flying = [step(payload)]
     for n in range(5):
         if n == 1:

time: 110 us -> 110 us (level)
  starting transfers between devices: 50.9 us -> 49.8 us
    ppermute x5, starting transfers between devices: 14.7 us -> 13.6 us  [ring_sums(): flying = flying[-1:] + [step(payload)]]
where the time goes in v6:
time: 110 us
  starting transfers between devices  49.8 us (45%)
  waiting for transfers between devices  35.8 us (33%)
  Pallas kernels  17.4 us (16%)
  other arithmetic  4.53 us (4%)
  local copies, waits for them, and re-layouts  2.11 us (2%)
    ppermute x5, starting transfers between devices, ring_sums(): flying = flying[-1:] + [step(payload)]  13.6 us
    pallas_call x1, Pallas kernels, product(): pl.pallas_call(product_kernel, in_specs=[smem, smem, anywhere, anywhere],...  11.1 us
    all_to_all x1, waiting for transfers between devices, on_device(): lax.all_to_all(slotted, freq, split_axis=0, concat_axis=0, tiled=True)  11 us
    all_to_all x1, waiting for transfers between devices, on_device(): lax.all_to_all(whole, freq, split_axis=0, concat_axis=0, tiled=True)  9.87 us
    all_to_all x1, starting transfers between devices, on_device(): lax.all_to_all(whole, freq, split_axis=0, concat_axis=0, tiled=True)  9.52 us
    all_to_all x1, starting transfers between devices, on_device(): mail = lax.all_to_all(mail, src, split_axis=0, concat_axis=0, tiled=True)  6.86 us
    all_to_all x1, waiting for transfers between devices, on_device(): mail = lax.all_to_all(mail, src, split_axis=0, concat_axis=0, tiled=True)  4.4 us
    ppermute x5, waiting for transfers between devices, ring_sums(): flying = flying[-1:] + [step(payload)]  4.18 us
  transfers between devices with their start and end apart: 16, of which 13 were waited for; matrix products, arithmetic and copies ran while one was open for 4% of the time, Pallas kernels for 1%

profile of v6, /device:TPU:1, one launch (start us, length us, event | category | flops | bytes accessed | tf_op | source)
XLA Modules:
  0.0 109.8 jit_solution(1579310743716129375)
XLA Ops:
  0.0 11.1 %product.1 = (f32[1,392,128]{2,1,0:T(8,128)}, f32[3,392,128]{2,1,0:T(8,128)}, f32[3,392,128]{2,1,0:T(8,128)}, f32[1,392,128]{2,1,0:T(8,128)}, f32[3,392,128]{2,1...) custom-call(s32[16]{0:T(128)} %pairing.1, f32[2,12]{1,0:T(2,128)} %ratio.1, ...), custom_call_target="tpu_custom_call" | custom-call | flops 3221225472 | bytes 15794176 | tf_op jit(solution)/shard_map/product/pallas_call | solution.py:162
  11.1 0.0 copy-start
  11.1 3.3 %collective-permute-start = (f32[1,392,128]{2,1,0:T(8,128)}, f32[1,392,128]{2,1,0:T(8,128)S(1)}, u32[]{:S(2)}, u32[]{:S(2)}) collective-permute-start(f32[1,392,128]{2,1,0:T(8,128)} %get-tuple-element.24), channel_id=1, source_target_pairs={{0,16},{16,0},{1,17},{17,1},{2,18},{18,2},{3,19},{19,3},{4,20},{20... | collective-permute-start | bytes 602120 | tf_op jit(solution)/shard_map/ppermute | solution.py:468
  14.5 0.0 copy-start.2
  14.5 0.9 copy-done.2
  15.4 0.2 lift.3.keep
  15.6 0.1 collective-permute-done.got
  15.8 0.5 collective-permute-start.1
  16.2 3.9 %collective-permute-start.3 = (f32[2,392,128]{2,1,0:T(8,128)S(1)}, f32[2,392,128]{2,1,0:T(8,128)S(1)}, u32[]{:S(2)}, u32[]{:S(2)}) collective-permute-start(f32[2,392,128]{2,1,0:T(8,128)S(1)} %collect.7.refs_0_), channel_id=1, source_target_pairs={{0,1},{1,2},{2,3},{3,4},{4,5},{5,6},{6,7},{7,0},{16,23},{17,16},{1... | collective-permute-start | bytes 1204232 | tf_op jit(solution)/shard_map/ppermute | solution.py:472
  20.1 1.1 copy-done.3
  21.2 0.1 lift.2.keep
  21.3 0.0 collective-permute-done.1.got
  21.4 0.0 copy-start.1
  21.4 0.8 collective-permute-start.5
  22.2 0.0 collective-permute-start.2
  22.2 2.7 %collective-permute-done.3.refs_0_ = f32[2,392,128]{2,1,0:T(8,128)S(1)} collective-permute-done((f32[2,392,128]{2,1,0:T(8,128)S(1)}, f32[2,392,128]{2,1,0:T(8,128)S(1)}, u32[]{:S(2)}, u32[]{:S(2)}) %collective-permute-start.3) | collective-permute-done | bytes 401440 | tf_op jit(solution)/shard_map/ppermute | solution.py:472
  24.9 0.1 collect.9.refs_1_
  25.0 3.2 %collective-permute-start.4 = (f32[2,392,128]{2,1,0:T(8,128)S(1)}, f32[2,392,128]{2,1,0:T(8,128)S(1)}, u32[]{:S(2)}, u32[]{:S(2)}) collective-permute-start(f32[2,392,128]{2,1,0:T(8,128)S(1)} %collect.9.refs_1_), channel_id=1, source_target_pairs={{0,1},{1,2},{2,3},{3,4},{4,5},{5,6},{6,7},{7,0},{16,23},{17,16},{1... | collective-permute-start | bytes 1204232 | tf_op jit(solution)/shard_map/ppermute | solution.py:480
  28.1 1.1 collective-permute-done.5.refs_0_
  29.2 0.1 collect.10.refs_1_
  29.3 3.2 %collective-permute-start.7 = (f32[2,392,128]{2,1,0:T(8,128)S(1)}, f32[2,392,128]{2,1,0:T(8,128)S(1)}, u32[]{:S(2)}, u32[]{:S(2)}) collective-permute-start(f32[2,392,128]{2,1,0:T(8,128)S(1)} %collect.10.refs_1_), channel_id=1, source_target_pairs={{0,1},{1,2},{2,3},{3,4},{4,5},{5,6},{6,7},{7,0},{16,23},{17,16},{1... | collective-permute-start | bytes 1204232 | tf_op jit(solution)/shard_map/ppermute | solution.py:480
  32.4 1.1 collective-permute-done.4.refs_0_
  33.5 0.0 collective-permute-done.2.got
  33.5 0.0 copy-done
  33.5 0.1 collect.11.refs_1_
  33.6 3.2 %collective-permute-start.6 = (f32[2,392,128]{2,1,0:T(8,128)S(1)}, f32[2,392,128]{2,1,0:T(8,128)S(1)}, u32[]{:S(2)}, u32[]{:S(2)}) collective-permute-start(f32[2,392,128]{2,1,0:T(8,128)S(1)} %collect.11.refs_1_), channel_id=1, source_target_pairs={{0,1},{1,2},{2,3},{3,4},{4,5},{5,6},{6,7},{7,0},{16,23},{17,16},{1... | collective-permute-start | bytes 1204232 | tf_op jit(solution)/shard_map/ppermute | solution.py:480
  36.8 1.0 collective-permute-done.7.refs_0_
  37.8 3.2 %collective-permute-start.9 = (f32[2,392,128]{2,1,0:T(8,128)S(1)}, f32[2,392,128]{2,1,0:T(8,128)S(1)}, u32[]{:S(2)}, u32[]{:S(2)}) collective-permute-start(f32[2,392,128]{2,1,0:T(8,128)S(1)} %collect.12.refs_1_), channel_id=1, source_target_pairs={{0,1},{1,2},{2,3},{3,4},{4,5},{5,6},{6,7},{7,0},{16,23},{17,16},{1... | collective-permute-start | bytes 1204232 | tf_op jit(solution)/shard_map/ppermute | solution.py:480
  41.0 0.0 copy-done.7
  41.0 0.1 copy.11
  41.2 0.1 reduce
  41.3 0.0 copy-done.6
  41.3 0.1 select_reduce_fusion.2
  41.4 0.7 collective-permute-done.6.refs_0_
  42.1 0.1 collect.13
  42.2 3.2 %collective-permute-start.10 = (f32[1,392,128]{2,1,0:T(8,128)S(1)}, f32[1,392,128]{2,1,0:T(8,128)S(1)}, u32[]{:S(2)}, u32[]{:S(2)}) collective-permute-start(f32[1,392,128]{2,1,0:T(8,128)S(1)} %get-tuple-element.32.before), channel_id=1, source_target_pairs={{0,17},{1,18},{2,19},{3,20},{4,21},{5,22},{6,23},{7,16},{16,7},{17... | collective-permute-start | bytes 602120 | tf_op jit(solution)/shard_map/ppermute | solution.py:482
  45.3 0.7 collective-permute-start.8
  46.1 0.3 collective-permute-done.9.arrived.refs_2_
  46.4 2.8 %collective-permute-start.11 = (f32[392,128]{1,0:T(8,128)S(1)}, f32[392,128]{1,0:T(8,128)S(1)}, u32[]{:S(2)}, u32[]{:S(2)}) collective-permute-start(f32[392,128]{1,0:T(8,128)S(1)} %other_half.1), channel_id=1, source_target_pairs={{0,16},{16,0},{1,17},{17,1},{2,18},{18,2},{3,19},{19,3},{4,20},{20... | collective-permute-start | bytes 602120 | tf_op jit(solution)/shard_map/ppermute | solution.py:482
  49.2 0.1 select_reduce_fusion.1
  49.3 1.3 %collective-permute-done.10 = f32[1,392,128]{2,1,0:T(8,128)S(1)} collective-permute-done((f32[1,392,128]{2,1,0:T(8,128)S(1)}, f32[1,392,128]{2,1,0:T(8,128)S(1)}, u32[]{:S(2)}, u32[]{:S(2)}) %collective-permute-start.10) | collective-permute-done | bytes 200736 | tf_op jit(solution)/shard_map/ppermute | solution.py:482
  50.5 1.3 %collective-permute-done.8.refs_1_ = f32[1,392,128]{2,1,0:T(8,128)S(1)} collective-permute-done((f32[1,392,128]{2,1,0:T(8,128)S(1)}, f32[1,392,128]{2,1,0:T(8,128)S(1)}, u32[]{:S(2)}, u32[]{:S(2)}) %collective-permute-start.8) | collective-permute-done | bytes 200736 | tf_op jit(solution)/shard_map/ppermute | solution.py:482
  51.8 0.0 collective-permute-done.11.refs_4_
  51.8 0.0 copy-done.1
  51.8 1.3 %mail.1.refs_5_ = f32[16,3,16,128]{3,2,1,0:T(8,128)} custom-call(f32[2,392,128]{2,1,0:T(8,128)S(1)} %copy-done.1, f32[1,392,128]{2,1,0:T(8,128)S(1)} %collective-permute-done.8.refs_1_, f32[2,392,128]{2,1,0:T(8,128)S(1)} %collective-permute-done.9.arrived.refs_2_, f32[392,128]{1,0:T(8,128)S(1)} %bitcast.5, f32[392,128]{1,0:T(8,128)S(1)} %collective-permute-done.11.refs_4_), custom_call_target="tpu_custom_call" | custom-call | tf_op jit(solution)/shard_map/mail/pallas_call | solution.py:285
  53.1 6.9 %all-to-all-start = ((f32[16,3,16,128]{3,2,1,0:T(8,128)}), f32[16,3,16,128]{3,2,1,0:T(8,128)S(1)}, u32[]{:S(2)}, u32[]{:S(2)}) async-start(f32[16,3,16,128]{3,2,1,0:T(8,128)} %mail.1.refs_5_), calls=%async_computation | async-start | bytes 786432 | tf_op jit(solution)/shard_map/all_to_all | solution.py:518
  60.0 0.1 direct.1
  60.1 1.5 %collective-permute-start.12 = (f32[24,16,128]{2,1,0:T(8,128)S(1)}, f32[24,16,128]{2,1,0:T(8,128)S(1)}, u32[]{:S(2)}, u32[]{:S(2)}) collective-permute-start(f32[24,16,128]{2,1,0:T(8,128)S(1)} %get-tuple-element.34), channel_id=1, source_target_pairs={{0,8},{8,0},{1,9},{9,1},{2,10},{10,2},{3,11},{11,3},{4,12},{12,4},... | collective-permute-start | bytes 589832 | tf_op jit(solution)/shard_map/ppermute | solution.py:517
  61.6 3.8 %reduce-precision_convert_fusion = (bf16[1,512,384]{2,1,0:T(8,128)(2,1)S(1)}, bf16[1,512,384]{2,1,0:T(8,128)(2,1)S(1)}) fusion(f32[512]{0:T(512)S(1)} %compare_select_fusion.2, s32[384]{0:T(512)S(1)} %add_select_fusion.1, s32[512]{0:T(512)S(1)} %fusion.25, pred[384]{0:T(512)(128)(4,1)S(1)} %fusion.11), kind=kLoop, calls=%fused_computation.2 | loop fusion | flops 3145728 | bytes 792448 | tf_op jit(solution)/shard_map/convert
  65.4 0.9 collective-permute-done.12.got
  66.3 4.4 %all-to-all-done.mail = f32[16,3,16,128]{3,2,1,0:T(8,128)S(1)} async-done(((f32[16,3,16,128]{3,2,1,0:T(8,128)}), f32[16,3,16,128]{3,2,1,0:T(8,128)S(1)}, u32[]{:S(2)}, u32[]{:S(2)}) %all-to-all-start) | async-done | bytes 393248 | tf_op jit(solution)/shard_map/all_to_all | solution.py:518
  70.7 1.0 join.1
  71.7 9.5 %all-to-all-start.1 = ((f32[16,24,256]{2,1,0:T(8,128)}), f32[16,24,256]{2,1,0:T(8,128)S(1)}, u32[]{:S(2)}, u32[]{:S(2)}) async-start(f32[16,24,256]{2,1,0:T(8,128)} %join.1), calls=%async_computation.1 | async-start | bytes 786432 | tf_op jit(solution)/shard_map/all_to_all | solution.py:520
  81.2 0.1 pad_maximum_fusion.basis
  81.3 0.1 fusion.6.relabel
  81.4 9.9 %all-to-all-done.1 = f32[16,24,256]{2,1,0:T(8,128)S(1)} async-done(((f32[16,24,256]{2,1,0:T(8,128)}), f32[16,24,256]{2,1,0:T(8,128)S(1)}, u32[]{:S(2)}, u32[]{:S(2)}) %all-to-all-start.1) | async-done | bytes 393248 | tf_op jit(solution)/shard_map/all_to_all | solution.py:520
  91.3 1.6 %transform.1 = f32[512,256]{1,0:T(8,128)} custom-call(bf16[2,512,384]{2,1,0:T(8,128)(2,1)S(1)} %pad_maximum_fusion.basis, f32[384,256]{1,0:T(8,128)S(1)} %bitcast.4, bf16[256,256]{1,0:T(8,128)(2,1)S(1)} %fusion.6.relabel), custom_call_target="tpu_custom_call" | custom-call | tf_op jit(solution)/shard_map/transform/pallas_call | solution.py:353
  92.9 4.1 %all-to-all-start.2 = ((f32[16,32,256]{2,1,0:T(8,128)}), f32[16,32,256]{2,1,0:T(8,128)S(1)}, u32[]{:S(2)}, u32[]{:S(2)}) async-start(f32[16,32,256]{2,1,0:T(8,128)} %bitcast.3), calls=%async_computation.2 | async-start | bytes 1048576 | tf_op jit(solution)/shard_map/all_to_all | solution.py:523
  97.0 0.0 copy-done.8
  97.0 0.1 select_reduce_fusion.3
  97.1 11.0 %all-to-all-done.2.traces = f32[16,32,256]{2,1,0:T(8,128)S(1)} async-done(((f32[16,32,256]{2,1,0:T(8,128)}), f32[16,32,256]{2,1,0:T(8,128)S(1)}, u32[]{:S(2)}, u32[]{:S(2)}) %all-to-all-start.2) | async-done | bytes 524320 | tf_op jit(solution)/shard_map/all_to_all | solution.py:523
  108.2 0.0 copy-done.4
  108.2 0.0 copy-done.5
  108.2 1.6 %update.1 = bf16[32,16,256]{2,1,0:T(8,128)(2,1)} custom-call(f32[32]{0:T(128)S(1)} %convert_element_type.24.events, s32[32]{0:T(128)S(1)} %compare_convert_fusion.inside, f32[16,32,256]{2,1,0:T(8,128)S(1)} %all-to-all-done.2.traces, bf16[32,16,256]{2,1,0:T(8,128)(2,1)S(1)} %copy-done.4, bf16[32,16,256]{2,1,0:T(8,128)(2,1)S(1)} %copy-done.5), custom_call_target="tpu_custom_call" | custom-call | tf_op jit(solution)/shard_map/update/pallas_call | solution.py:379
  (22 shorter events, 0.2 us)
Async XLA Ops:
  11.1 22.4 %copy-start = (f32[3,392,128]{2,1,0:T(8,128)S(1)}, f32[3,392,128]{2,1,0:T(8,128)}, u32[]{:S(2)}) copy-start(f32[3,392,128]{2,1,0:T(8,128)} %get-tuple-element.21.keep) | copy-start | bytes 1806340
  11.1 4.6 %collective-permute-start = (f32[1,392,128]{2,1,0:T(8,128)}, f32[1,392,128]{2,1,0:T(8,128)S(1)}, u32[]{:S(2)}, u32[]{:S(2)}) collective-permute-start(f32[1,392,128]{2,1,0:T(8,128)} %get-tuple-element.24), channel_id=1, source_target_pairs={{0,16},{16,0},{1,17},{17,1},{2,18},{18,2},{3,19},{19,3},{4,20},{20... | collective-permute-start | bytes 602120 | tf_op jit(solution)/shard_map/ppermute | solution.py:468
  14.5 0.9 copy-start.2
  15.8 5.5 %collective-permute-start.1 = (f32[3,392,128]{2,1,0:T(8,128)}, f32[3,392,128]{2,1,0:T(8,128)S(1)}, u32[]{:S(2)}, u32[]{:S(2)}) collective-permute-start(f32[3,392,128]{2,1,0:T(8,128)} %get-tuple-element.26), channel_id=1, source_target_pairs={{0,16},{16,0},{1,17},{17,1},{2,18},{18,2},{3,19},{19,3},{4,20},{20... | collective-permute-start | bytes 1806344 | tf_op jit(solution)/shard_map/ppermute | solution.py:470
  16.2 8.7 %collective-permute-start.3 = (f32[2,392,128]{2,1,0:T(8,128)S(1)}, f32[2,392,128]{2,1,0:T(8,128)S(1)}, u32[]{:S(2)}, u32[]{:S(2)}) collective-permute-start(f32[2,392,128]{2,1,0:T(8,128)S(1)} %collect.7.refs_0_), channel_id=1, source_target_pairs={{0,1},{1,2},{2,3},{3,4},{4,5},{5,6},{6,7},{7,0},{16,23},{17,16},{1... | collective-permute-start | bytes 1204232 | tf_op jit(solution)/shard_map/ppermute | solution.py:472
  20.1 1.1 copy-start.3
  21.2 19.9 %copy-start.7 = (s32[16]{0:T(128)S(1)}, s32[16]{0:T(128)}, u32[]{:S(2)}) copy-start(s32[16]{0:T(128)} %param.11) | copy-start | bytes 196
  21.2 20.2 %copy-start.6 = (s32[16]{0:T(128)S(1)}, s32[16]{0:T(128)}, u32[]{:S(2)}) copy-start(s32[16]{0:T(128)} %pairing.1) | copy-start | bytes 196
  21.4 30.5 %copy-start.1 = (f32[2,392,128]{2,1,0:T(8,128)S(1)}, f32[2,392,128]{2,1,0:T(8,128)}, u32[]{:S(2)}) copy-start(f32[2,392,128]{2,1,0:T(8,128)} %get-tuple-element.20.refs_0_) | copy-start | bytes 1204228
  21.4 7.8 %collective-permute-start.5 = (f32[2,392,128]{2,1,0:T(8,128)S(1)}, f32[2,392,128]{2,1,0:T(8,128)S(1)}, u32[]{:S(2)}, u32[]{:S(2)}) collective-permute-start(f32[2,392,128]{2,1,0:T(8,128)S(1)} %collect.8.refs_1_), channel_id=1, source_target_pairs={{0,1},{1,2},{2,3},{3,4},{4,5},{5,6},{6,7},{7,0},{16,23},{17,16},{1... | collective-permute-start | bytes 1204232 | tf_op jit(solution)/shard_map/ppermute | solution.py:480
  22.2 11.3 %collective-permute-start.2 = (f32[3,392,128]{2,1,0:T(8,128)}, f32[3,392,128]{2,1,0:T(8,128)S(1)}, u32[]{:S(2)}, u32[]{:S(2)}) collective-permute-start(f32[3,392,128]{2,1,0:T(8,128)} %get-tuple-element.29), channel_id=1, source_target_pairs={{0,16},{16,0},{1,17},{17,1},{2,18},{18,2},{3,19},{19,3},{4,20},{20... | collective-permute-start | bytes 1806344 | tf_op jit(solution)/shard_map/ppermute | solution.py:476
  25.0 8.5 %collective-permute-start.4 = (f32[2,392,128]{2,1,0:T(8,128)S(1)}, f32[2,392,128]{2,1,0:T(8,128)S(1)}, u32[]{:S(2)}, u32[]{:S(2)}) collective-permute-start(f32[2,392,128]{2,1,0:T(8,128)S(1)} %collect.9.refs_1_), channel_id=1, source_target_pairs={{0,1},{1,2},{2,3},{3,4},{4,5},{5,6},{6,7},{7,0},{16,23},{17,16},{1... | collective-permute-start | bytes 1204232 | tf_op jit(solution)/shard_map/ppermute | solution.py:480
  29.3 8.6 %collective-permute-start.7 = (f32[2,392,128]{2,1,0:T(8,128)S(1)}, f32[2,392,128]{2,1,0:T(8,128)S(1)}, u32[]{:S(2)}, u32[]{:S(2)}) collective-permute-start(f32[2,392,128]{2,1,0:T(8,128)S(1)} %collect.10.refs_1_), channel_id=1, source_target_pairs={{0,1},{1,2},{2,3},{3,4},{4,5},{5,6},{6,7},{7,0},{16,23},{17,16},{1... | collective-permute-start | bytes 1204232 | tf_op jit(solution)/shard_map/ppermute | solution.py:480
  33.6 8.5 %collective-permute-start.6 = (f32[2,392,128]{2,1,0:T(8,128)S(1)}, f32[2,392,128]{2,1,0:T(8,128)S(1)}, u32[]{:S(2)}, u32[]{:S(2)}) collective-permute-start(f32[2,392,128]{2,1,0:T(8,128)S(1)} %collect.11.refs_1_), channel_id=1, source_target_pairs={{0,1},{1,2},{2,3},{3,4},{4,5},{5,6},{6,7},{7,0},{16,23},{17,16},{1... | collective-permute-start | bytes 1204232 | tf_op jit(solution)/shard_map/ppermute | solution.py:480
  37.8 8.6 %collective-permute-start.9 = (f32[2,392,128]{2,1,0:T(8,128)S(1)}, f32[2,392,128]{2,1,0:T(8,128)S(1)}, u32[]{:S(2)}, u32[]{:S(2)}) collective-permute-start(f32[2,392,128]{2,1,0:T(8,128)S(1)} %collect.12.refs_1_), channel_id=1, source_target_pairs={{0,1},{1,2},{2,3},{3,4},{4,5},{5,6},{6,7},{7,0},{16,23},{17,16},{1... | collective-permute-start | bytes 1204232 | tf_op jit(solution)/shard_map/ppermute | solution.py:480
  42.2 8.4 %collective-permute-start.10 = (f32[1,392,128]{2,1,0:T(8,128)S(1)}, f32[1,392,128]{2,1,0:T(8,128)S(1)}, u32[]{:S(2)}, u32[]{:S(2)}) collective-permute-start(f32[1,392,128]{2,1,0:T(8,128)S(1)} %get-tuple-element.32.before), channel_id=1, source_target_pairs={{0,17},{1,18},{2,19},{3,20},{4,21},{5,22},{6,23},{7,16},{16,7},{17... | collective-permute-start | bytes 602120 | tf_op jit(solution)/shard_map/ppermute | solution.py:482
  45.3 51.6 %copy-start.8 = (s32[32]{0:T(128)S(1)}, s32[32]{0:T(128)}, u32[]{:S(2)}) copy-start(s32[32]{0:T(128)} %param.12) | copy-start | bytes 388
  45.3 62.8 %copy-start.4 = (bf16[32,16,256]{2,1,0:T(8,128)(2,1)S(1)}, bf16[32,16,256]{2,1,0:T(8,128)(2,1)}, u32[]{:S(2)}) copy-start(bf16[32,16,256]{2,1,0:T(8,128)(2,1)} %older.1) | copy-start | bytes 786436
  45.3 62.8 %copy-start.5 = (bf16[32,16,256]{2,1,0:T(8,128)(2,1)S(1)}, bf16[32,16,256]{2,1,0:T(8,128)(2,1)}, u32[]{:S(2)}) copy-start(bf16[32,16,256]{2,1,0:T(8,128)(2,1)} %data.1) | copy-start | bytes 786436
  45.3 6.5 %collective-permute-start.8 = (f32[1,392,128]{2,1,0:T(8,128)S(1)}, f32[1,392,128]{2,1,0:T(8,128)S(1)}, u32[]{:S(2)}, u32[]{:S(2)}) collective-permute-start(f32[1,392,128]{2,1,0:T(8,128)S(1)} %get-tuple-element.31), channel_id=1, source_target_pairs={{0,1},{1,2},{2,3},{3,4},{4,5},{5,6},{6,7},{7,0},{16,23},{17,16},{1... | collective-permute-start | bytes 602120 | tf_op jit(solution)/shard_map/ppermute | solution.py:482
  46.4 5.4 %collective-permute-start.11 = (f32[392,128]{1,0:T(8,128)S(1)}, f32[392,128]{1,0:T(8,128)S(1)}, u32[]{:S(2)}, u32[]{:S(2)}) collective-permute-start(f32[392,128]{1,0:T(8,128)S(1)} %other_half.1), channel_id=1, source_target_pairs={{0,16},{16,0},{1,17},{17,1},{2,18},{18,2},{3,19},{19,3},{4,20},{20... | collective-permute-start | bytes 602120 | tf_op jit(solution)/shard_map/ppermute | solution.py:482
  53.1 17.6 %all-to-all-start = ((f32[16,3,16,128]{3,2,1,0:T(8,128)}), f32[16,3,16,128]{3,2,1,0:T(8,128)S(1)}, u32[]{:S(2)}, u32[]{:S(2)}) async-start(f32[16,3,16,128]{3,2,1,0:T(8,128)} %mail.1.refs_5_), calls=%async_computation | async-start | bytes 786432 | tf_op jit(solution)/shard_map/all_to_all | solution.py:518
  60.1 6.2 %collective-permute-start.12 = (f32[24,16,128]{2,1,0:T(8,128)S(1)}, f32[24,16,128]{2,1,0:T(8,128)S(1)}, u32[]{:S(2)}, u32[]{:S(2)}) collective-permute-start(f32[24,16,128]{2,1,0:T(8,128)S(1)} %get-tuple-element.34), channel_id=1, source_target_pairs={{0,8},{8,0},{1,9},{9,1},{2,10},{10,2},{3,11},{11,3},{4,12},{12,4},... | collective-permute-start | bytes 589832 | tf_op jit(solution)/shard_map/ppermute | solution.py:517
  71.7 19.6 %all-to-all-start.1 = ((f32[16,24,256]{2,1,0:T(8,128)}), f32[16,24,256]{2,1,0:T(8,128)S(1)}, u32[]{:S(2)}, u32[]{:S(2)}) async-start(f32[16,24,256]{2,1,0:T(8,128)} %join.1), calls=%async_computation.1 | async-start | bytes 786432 | tf_op jit(solution)/shard_map/all_to_all | solution.py:520
  92.9 15.3 %all-to-all-start.2 = ((f32[16,32,256]{2,1,0:T(8,128)}), f32[16,32,256]{2,1,0:T(8,128)S(1)}, u32[]{:S(2)}, u32[]{:S(2)}) async-start(f32[16,32,256]{2,1,0:T(8,128)} %bitcast.3), calls=%async_computation.2 | async-start | bytes 1048576 | tf_op jit(solution)/shard_map/all_to_all | solution.py:523
